TPU v7x, 32 devices: a whole 2x2x4 slice. The times are simulated.
32 devices in a mesh: groups: 2 (over y), dp: 8 (over z, x), tensor: 2 (over core).
Axes of the slice: x: 2, y: 2, z: 4, core: 2. Of those that a mesh axis runs over, the one named last changes fastest.
Arguments:
- tokens: bfloat16 [4096, 5120], P(('groups', 'dp'), 'tensor'), parts along dimension 0, may hold values from -60 to 60
- base_key_matrix: bfloat16 [5120, 1024], P('tensor'), may hold values from -0.078125 to 0.078125
- adapter_down_weight: bfloat16 [256, 64, 5120], P(('groups', 'dp'), None, 'tensor'), parts along dimension 0, may hold values from -0.078125 to 0.078125
- adapter_up_weight: bfloat16 [256, 64, 1024], P(('groups', 'dp'), None, 'tensor'), parts along dimension 0, may hold values from -0.75 to 0.75
- key_norm_scale: float32 [128], replicated, may hold values from 0.25 to 1.75
- request_adapter: int32 [4096], P(('groups', 'dp')), parts along dimension 0, may hold values from 0 to 127, as said below
- adapter_slot_table: int32 [256], P('groups'), parts along dimension 0, may hold values from 0 to 127, as said below
- cached_token_length: int32 [4096], P(('groups', 'dp')), parts along dimension 0, may hold values from 1 to 4096
Outputs:
- new_keys: bfloat16 [4096, 1024], P(('groups', 'dp'), 'tensor'), parts along dimension 0
There are 2 independent parts, one for each index of `groups`. A program takes and returns all parts, laid end to end along the dimension named above; an argument that names none is the same for every part. Nothing has to cross between parts.
Inputs may be any that keep to these rules, and one draw needn't show every extreme that they name: `request_adapter`: in the 256 requests of each index of dp, exactly 96 use adapters stored on one owner (slot // 16), the same owner for every index and every request block of the part, and every other owner gets 23 or 22 of them. A permutation: adapter a is row adapter_slot_table[a] of adapter_down_weight and adapter_up_weight.
All inputs are finite; a program needn't handle non-finite values.
Results may differ from a plain program's by a relative error of at most 0.0051.
Values may be sent and summed in bfloat16 or wider, within the bound.
No kernel may reach another device: no remote copies, remote signals or barrier semaphores. Data moves between devices by JAX's collectives and lax.ppermute only.
A program may use at most 128 MiB of HBM per device.

v0:
```python
import jax
import jax.numpy as jnp
from jax import lax
from jax.sharding import PartitionSpec as P

rope_theta = 1000000.0


def rotate(normed, cached_token_length):
    head_size = normed.shape[-1]
    half_head = head_size // 2
    inv_freq = rope_theta ** (-(jnp.arange(half_head, dtype=jnp.float32) * 2.0) / head_size)
    angles = cached_token_length.astype(jnp.float32)[:, None] * inv_freq[None, :]
    cosine = jnp.cos(angles)[:, None, :]
    sine = jnp.sin(angles)[:, None, :]
    lead_half = normed[..., :half_head]
    tail_half = normed[..., half_head:]
    return jnp.concatenate(
        [lead_half * cosine - tail_half * sine, tail_half * cosine + lead_half * sine], axis=-1
    )


def block_mask(adapter_idx, stored_weight, rank_size):
    return (jnp.arange(stored_weight * rank_size) // rank_size)[None, :] == adapter_idx[:, None]


def reduce_portion(flattened_rows, adapter_idx, down_store):
    stored_weight, rank_size, width = down_store.shape
    down_table = down_store.reshape(stored_weight * rank_size, width)
    scores = lax.dot_general(
        flattened_rows, down_table, (((1,), (1,)), ((), ())), preferred_element_type=jnp.float32
    )
    picked = jnp.where(block_mask(adapter_idx, stored_weight, rank_size), scores, 0.0)
    return picked.reshape(flattened_rows.shape[0], stored_weight, rank_size).sum(axis=1)


def expand_portion(reduced_input, adapter_idx, up_store):
    stored_weight, rank_size, width = up_store.shape
    spread_in = jnp.where(
        block_mask(adapter_idx, stored_weight, rank_size),
        jnp.tile(reduced_input, (1, stored_weight)),
        jnp.zeros((), jnp.bfloat16),
    )
    product = jnp.dot(
        spread_in,
        up_store.reshape(stored_weight * rank_size, width),
        preferred_element_type=jnp.float32,
    )
    return product.astype(jnp.bfloat16)


def finish(base_part, delta_rows, key_norm_scale, cached_token_length):
    head_size = key_norm_scale.shape[0]
    key_vals = base_part + delta_rows.astype(jnp.float32)
    head_view = key_vals.reshape(key_vals.shape[0], -1, head_size)
    normed = (
        head_view
        * lax.rsqrt(jnp.mean(head_view * head_view, axis=-1, keepdims=True) + 1e-06)
        * key_norm_scale
    )
    rotated = rotate(normed, cached_token_length)
    return rotated.reshape(key_vals.shape).astype(jnp.bfloat16)


def on_device(
    tokens,
    base_key_matrix,
    adapter_down_weight,
    adapter_up_weight,
    key_norm_scale,
    request_adapter,
    adapter_slot_table,
    cached_token_length,
):
    row_count, half_width = tokens.shape
    stored_weight = adapter_down_weight.shape[0]
    owners_count = lax.axis_size("dp")
    per_share = (row_count + owners_count + 2) // (owners_count + 3)
    capacity = 4 * per_share
    partial_value = jnp.dot(tokens, base_key_matrix, preferred_element_type=jnp.float32)
    base_part = lax.psum_scatter(partial_value, "tensor", scatter_dimension=1, tiled=True)
    slot_idx = jnp.take(adapter_slot_table, request_adapter)
    owner_of = slot_idx // stored_weight
    local_idx = slot_idx % stored_weight
    one_hot = (owner_of[:, None] == jnp.arange(owners_count)[None, :]).astype(jnp.int32)
    before = jnp.cumsum(one_hot, axis=0) - one_hot
    rank_in = jnp.sum(before * one_hot, axis=1)
    position = owner_of * capacity + rank_in
    send_rows = (
        jnp.zeros((owners_count * capacity, half_width), jnp.bfloat16).at[position].set(tokens)
    )
    send_local = jnp.zeros((owners_count * capacity,), jnp.int32).at[position].set(local_idx)
    send_rows = send_rows.reshape(owners_count, capacity, half_width)
    send_local = send_local.reshape(owners_count, capacity)
    got_rows = lax.all_to_all(send_rows, "dp", split_axis=0, concat_axis=0, tiled=True)
    got_local = lax.all_to_all(send_local, "dp", split_axis=0, concat_axis=0, tiled=True)
    sources, items = got_local.shape
    flattened_rows = got_rows.reshape(sources * items, half_width)
    flattened_local = got_local.reshape(sources * items)
    partial_reduced = reduce_portion(flattened_rows, flattened_local, adapter_down_weight)
    reduced_input = lax.psum(partial_reduced, "tensor").astype(jnp.bfloat16)
    expanded_delta = expand_portion(reduced_input, flattened_local, adapter_up_weight)
    returned = expanded_delta.reshape(sources, items, expanded_delta.shape[-1])
    back_rows = lax.all_to_all(returned, "dp", split_axis=0, concat_axis=0, tiled=True)
    delta_rows = back_rows.reshape(owners_count * capacity, -1)[position]
    return finish(base_part, delta_rows, key_norm_scale, cached_token_length)


def solution(mesh):
    placed = (
        P(("groups", "dp"), "tensor"),
        P("tensor", None),
        P(("groups", "dp"), None, "tensor"),
        P(("groups", "dp"), None, "tensor"),
        P(),
        P(("groups", "dp")),
        P("groups"),
        P(("groups", "dp")),
    )
    return jax.shard_map(
        on_device,
        mesh=mesh,
        in_specs=placed,
        out_specs=P(("groups", "dp"), "tensor"),
        check_vma=False,
    )
```

profile of v0, /device:TPU:0, one launch (start us, length us, event | category | flops | bytes accessed | tf_op | source)
XLA Modules:
  0.0 176.5 jit_solution(15498368192318065195)
XLA Ops:
  6.5 0.8 compare_select_fusion.6
  7.3 1.9 %gather_fusion = s32[256]{0:T(256)S(1)} fusion(s32[128]{0:T(128)} %param.14, s32[1024]{0:T(1024)S(1)} %pad_clamp_fusion.1), kind=kCustom, calls=%fused_computation | custom fusion | bytes 3072 | tf_op jit(solution)/shard_map/jit(_take)/gather | solution.py:82
  9.2 0.7 and_select_fusion
  9.9 0.6 reduce-window.6
  10.9 1.4 scatter_custom_fusion
  12.3 0.7 all_to_all.12
  13.0 7.3 %all-to-all-start = ((s32[8,1,96]{2,1,0:T(1,128)}), s32[8,1,96]{2,1,0:T(1,128)S(1)}, u32[]{:S(2)}, u32[]{:S(2)}) async-start(s32[8,1,96]{2,1,0:T(1,128)} %all_to_all.12), calls=%async_computation.1 | async-start | bytes 8192 | tf_op jit(solution)/shard_map/all_to_all | solution.py:96
  20.2 5.8 %scatter_custom_fusion.1 = bf16[768,2560]{1,0:T(8,128)(2,1)} fusion(s32[256]{0:T(256)S(1)} %compare_select_fusion.5, bf16[256,2560]{1,0:T(8,128)(2,1)} %param.8, bf16[]{:T(256)} %constant.85.clone.1), kind=kCustom, calls=%fused_computation.6 | custom fusion | bytes 3932672 | tf_op jit(solution)/shard_map/scatter | solution.py:90
  26.0 0.6 all-to-all-done
  26.6 5.5 %all-to-all-start.1 = ((bf16[8,96,2560]{2,1,0:T(8,128)(2,1)}), bf16[8,96,2560]{2,1,0:T(8,128)(2,1)}, u32[]{:S(2)}, u32[]{:S(2)}) async-start(bf16[8,96,2560]{2,1,0:T(8,128)(2,1)} %bitcast.26), calls=%async_computation.2 | async-start | bytes 7864320 | tf_op jit(solution)/shard_map/all_to_all | solution.py:95
  32.2 5.1 %fusion.17 = f32[256,1024]{1,0:T(8,128)} fusion(bf16[256,2560]{1,0:T(8,128)(2,1)S(1)} %copy-done.3, bf16[2560,1024]{1,0:T(8,128)(2,1)} %param.9), kind=kOutput, calls=%fused_computation.59 | convolution fusion | flops 1342177280 | bytes 7602176 | tf_op jit(solution)/shard_map/dot_general | solution.py:80
  37.8 0.7 reduce.5
  38.6 80.7 %all-to-all-done.1 = bf16[8,96,2560]{2,1,0:T(8,128)(2,1)} async-done(((bf16[8,96,2560]{2,1,0:T(8,128)(2,1)}), bf16[8,96,2560]{2,1,0:T(8,128)(2,1)}, u32[]{:S(2)}, u32[]{:S(2)}) %all-to-all-start.1) | async-done | bytes 3932192 | tf_op jit(solution)/shard_map/all_to_all | solution.py:95
  119.2 9.6 %compare_select_fusion = f32[768,1024]{1,0:T(8,128)} fusion(bf16[768,2560]{1,0:T(8,128)(2,1)} %bitcast.4, bf16[1024,2560]{1,0:T(8,128)(2,1)} %bitcast.31, s32[1024]{0:T(1024)S(1)} %add_select_fusion.1, s32[768]{0:T(1024)S(1)} %eq.66), kind=kOutput, calls=%fused_computation.4 | convolution fusion | flops 4028104704 | bytes 12327936 | tf_op jit(solution)/shard_map/dot_general | solution.py:30
  128.8 3.5 %copy.12 = f32[768,1024]{0,1:T(8,128)} copy(f32[768,1024]{1,0:T(8,128)} %compare_select_fusion) | data formatting | bytes 6291456 | tf_op jit(solution)/shard_map/jit(_where)/select_n | solution.py:33
  132.4 2.1 %reduce_sum.28 = f32[768,64]{0,1:T(8,128)S(1)} reduce(f32[768,16,64]{0,2,1:T(8,128)} %bitcast.27, f32[]{:T(128)} %constant.86.clone.1), dimensions={1}, to_apply=%region_6.7 | reduce | flops 737280 | bytes 3342340 | tf_op jit(solution)/shard_map/reduce_sum | solution.py:34
  134.4 4.0 %all-reduce.1 = bf16[768,64]{0,1:T(8,128)(2,1)S(1)} all-reduce(f32[768,64]{0,1:T(8,128)S(1)} %reduce_sum.28), channel_id=1, replica_groups=mesh['groups'=2,'dp'=8,'tensor'=2] {'tensor'}, use_global_device_ids=true, to_apply=%region_7.8 | all-reduce | flops 49152 | bytes 294912 | tf_op jit(solution)/shard_map/psum | solution.py:101
  138.4 2.0 %bitcast_convert_fusion = bf16[768,512]{1,0:T(8,128)(2,1)} fusion(bf16[16,64,512]{2,1,0:T(8,128)(2,1)S(1)} %copy-done, s32[768]{0:T(1024)S(1)} %eq.66, s32[16,64]{1,0:T(8,128)S(1)} %add_select_fusion, bf16[768,64]{0,1:T(8,128)(2,1)S(1)} %all-reduce.1), kind=kOutput, calls=%fused_computation.9 | convolution fusion | flops 807272448 | bytes 1940480 | tf_op jit(solution)/shard_map/dot_general | solution.py:44
  140.4 3.7 %all-to-all-start.2 = ((bf16[8,96,512]{2,1,0:T(8,128)(2,1)}), bf16[8,96,512]{2,1,0:T(8,128)(2,1)S(1)}, u32[]{:S(2)}, u32[]{:S(2)}) async-start(bf16[8,96,512]{2,1,0:T(8,128)(2,1)} %bitcast.8), calls=%async_computation.3 | async-start | bytes 1572864 | tf_op jit(solution)/shard_map/all_to_all | solution.py:104
  144.2 0.5 multiply_cosine_fusion
  144.8 20.1 %all-to-all-done.2 = bf16[8,96,512]{2,1,0:T(8,128)(2,1)S(1)} async-done(((bf16[8,96,512]{2,1,0:T(8,128)(2,1)}), bf16[8,96,512]{2,1,0:T(8,128)(2,1)S(1)}, u32[]{:S(2)}, u32[]{:S(2)}) %all-to-all-start.2) | async-done | bytes 786464 | tf_op jit(solution)/shard_map/all_to_all | solution.py:104
  164.8 1.2 gather_fusion.1
  166.0 1.1 convert_add_fusion
  169.0 0.7 copy.18
  (31 shorter events, 2.8 us)
Async XLA Ops:
  6.5 131.9 %copy-start = (bf16[16,64,512]{2,1,0:T(8,128)(2,1)S(1)}, bf16[16,64,512]{2,1,0:T(8,128)(2,1)}, u32[]{:S(2)}) copy-start(bf16[16,64,512]{2,1,0:T(8,128)(2,1)} %param.11) | copy-start | bytes 3145732
  13.0 13.6 %all-to-all-start = ((s32[8,1,96]{2,1,0:T(1,128)}), s32[8,1,96]{2,1,0:T(1,128)S(1)}, u32[]{:S(2)}, u32[]{:S(2)}) async-start(s32[8,1,96]{2,1,0:T(1,128)} %all_to_all.12), calls=%async_computation.1 | async-start | bytes 8192 | tf_op jit(solution)/shard_map/all_to_all | solution.py:96
  26.6 5.6 %copy-start.3 = (bf16[256,2560]{1,0:T(8,128)(2,1)S(1)}, bf16[256,2560]{1,0:T(8,128)(2,1)}, u32[]{:S(2)}) copy-start(bf16[256,2560]{1,0:T(8,128)(2,1)} %param.8) | copy-start | bytes 3932164
  26.6 92.6 %all-to-all-start.1 = ((bf16[8,96,2560]{2,1,0:T(8,128)(2,1)}), bf16[8,96,2560]{2,1,0:T(8,128)(2,1)}, u32[]{:S(2)}, u32[]{:S(2)}) async-start(bf16[8,96,2560]{2,1,0:T(8,128)(2,1)} %bitcast.26), calls=%async_computation.2 | async-start | bytes 7864320 | tf_op jit(solution)/shard_map/all_to_all | solution.py:95
  32.1 133.9 %reduce-scatter.2.cloned.1.call-start = ((), (), s32[]{:S(2)}) async-start(), calls=%async_computation.4 | async-start | bytes 1572864 | tf_op jit(solution)/shard_map/reduce_scatter | solution.py:81
  138.4 5.7 %copy-start.1 = (s32[256]{0:T(256)S(1)}, s32[256]{0:T(256)}, u32[]{:S(2)}) copy-start(s32[256]{0:T(256)} %param.15) | copy-start | bytes 3076
  140.4 24.4 %all-to-all-start.2 = ((bf16[8,96,512]{2,1,0:T(8,128)(2,1)}), bf16[8,96,512]{2,1,0:T(8,128)(2,1)S(1)}, u32[]{:S(2)}, u32[]{:S(2)}) async-start(bf16[8,96,512]{2,1,0:T(8,128)(2,1)} %bitcast.8), calls=%async_computation.3 | async-start | bytes 1572864 | tf_op jit(solution)/shard_map/all_to_all | solution.py:104
  144.2 23.5 %copy-start.2 = (f32[128]{0:T(128)S(1)}, f32[128]{0:T(128)}, u32[]{:S(2)}) copy-start(f32[128]{0:T(128)} %param.12) | copy-start | bytes 1540
Sparse Core Ops, SparseCore 0:
  37.4 9.9 reduce-scatter.1
where the time goes:
time: 177 us
  waiting for transfers between devices  101 us (57%)
  matrix products  16.7 us (9%)
  starting transfers between devices  16.5 us (9%)
  local copies, waits for them, and re-layouts  16.2 us (9%)
  between operations  13.6 us (8%)
  other arithmetic  8.17 us (5%)
  blocking collectives  3.97 us (2%)
    all_to_all x1, waiting for transfers between devices, on_device(): lax.all_to_all(send_rows, 'dp', split_axis=0, concat_axis=0, tiled=True)  80.7 us
    all_to_all x1, waiting for transfers between devices, on_device(): lax.all_to_all(returned, 'dp', split_axis=0, concat_axis=0, tiled=True)  20.1 us
    dot_general x1, matrix products, reduce_portion(): lax.dot_general(flattened_rows, down_table, (((1,), (1,)), ((), ())), pre...  9.61 us
    all_to_all x1, starting transfers between devices, on_device(): lax.all_to_all(send_local, 'dp', split_axis=0, concat_axis=0, tiled=True)  7.25 us
    scatter x1, local copies, waits for them, and re-layouts, on_device(): jnp.zeros((owners_count * capacity, half_width), jnp.bfloat16).at[position]  5.78 us
    all_to_all x1, starting transfers between devices, on_device(): lax.all_to_all(send_rows, 'dp', split_axis=0, concat_axis=0, tiled=True)  5.52 us
    dot_general x1, matrix products, on_device(): jnp.dot(tokens, base_key_matrix, preferred_element_type=jnp.float32)  5.08 us
    psum x1, blocking collectives, on_device(): reduced_input = lax.psum(partial_reduced, 'tensor').astype(jnp.bfloat16)  3.97 us
  transfers between devices with their start and end apart: 4, of which 3 were waited for; matrix products, arithmetic and copies ran while one was open for 18% of the time, Pallas kernels for 0%

commit v1 on v0

v1 whole, which is shorter than its diff:
```python
import functools

import jax
import jax.numpy as jnp
from jax import lax
from jax.experimental import pallas as pl
from jax.experimental.pallas import tpu as pltpu
from jax.sharding import PartitionSpec as P

rope_theta = 1000000.0
LANES = 128
EXTRA = 128
HOT_PARTS = 3
VMEM_BYTES = 48 * 1024 * 1024


def whole():
    return pl.BlockSpec(memory_space=pltpu.VMEM)


def params():
    return pltpu.CompilerParams(vmem_limit_bytes=VMEM_BYTES)


def ring_order(owners):
    return [i for i in range(0, owners, 2)] + [i for i in range(owners - 1, 0, -2)]


def to_column(row):
    count = row.shape[1]
    square = lax.broadcasted_iota(jnp.int32, (count, count), 0) == lax.broadcasted_iota(
        jnp.int32, (count, count), 1
    )
    return jnp.sum(jnp.where(square, row, 0), axis=1, keepdims=True)


def pack_kernel(
    stored, owners, share, request_ref, table_ref, tokens_ref, cold_ref, hot_ref, place_ref
):
    count = request_ref.shape[1]
    width = tokens_ref.shape[1]
    request_col = to_column(request_ref[...])
    adapters = table_ref.shape[1]
    match = request_col == lax.broadcasted_iota(jnp.int32, (count, adapters), 1)
    slot_col = jnp.sum(jnp.where(match, table_ref[...], 0), axis=1, keepdims=True)
    row_id = lax.broadcasted_iota(jnp.int32, (count, count), 0)
    col_id = lax.broadcasted_iota(jnp.int32, (count, count), 1)
    slot_row = jnp.sum(jnp.where(row_id == col_id, slot_col, 0), axis=0, keepdims=True)
    owner_col = slot_col // stored
    owner_row = slot_row // stored
    same = owner_col == owner_row
    rank_col = jnp.sum(jnp.where(same & (col_id < row_id), 1, 0), axis=1, keepdims=True)
    rank_row = jnp.sum(jnp.where(same & (row_id < col_id), 1, 0), axis=0, keepdims=True)
    cold_total = owners * share
    hot_total = HOT_PARTS * share

    def place(owner, rank):
        return jnp.where(rank < share, owner * share + rank, cold_total + rank - share)

    place_ref[...] = place(owner_col, rank_col)
    place_row = place(owner_row, rank_row)
    local_row = slot_row - owner_row * stored
    cold_pick = place_row == lax.broadcasted_iota(jnp.int32, (cold_total, count), 0)
    hot_pick = place_row - cold_total == lax.broadcasted_iota(jnp.int32, (hot_total, count), 0)
    tokens = tokens_ref[...]
    cold_ref[:, :width] = jnp.dot(
        cold_pick.astype(jnp.float32).astype(jnp.bfloat16), tokens, preferred_element_type=jnp.float32
    ).astype(jnp.bfloat16)
    hot_ref[...] = jnp.dot(
        hot_pick.astype(jnp.float32).astype(jnp.bfloat16), tokens, preferred_element_type=jnp.float32
    ).astype(jnp.bfloat16)
    lane = lax.broadcasted_iota(jnp.int32, (cold_total, EXTRA), 1)
    part_row = lax.broadcasted_iota(jnp.int32, (cold_total, count), 0) % share
    extra = jnp.sum(jnp.where(cold_pick, local_row + 1, 0), axis=1, keepdims=True) - 1
    extra = jnp.where(lane == 0, extra, 0)
    for part in range(HOT_PARTS):
        chosen = place_row == cold_total + part * share + part_row
        hot_local = jnp.sum(jnp.where(chosen, local_row, 0), axis=1, keepdims=True)
        hot_owner = jnp.sum(jnp.where(chosen, owner_row + 1, 0), axis=1, keepdims=True) - 1
        extra = jnp.where(lane == 1 + part, hot_local, extra)
        extra = jnp.where(lane == 1 + HOT_PARTS + part, hot_owner, extra)
    cold_ref[:, width:] = extra.astype(jnp.float32).astype(jnp.bfloat16)


def pack(request, table, tokens, stored, owners, share):
    count, width = tokens.shape
    return pl.pallas_call(
        functools.partial(pack_kernel, stored, owners, share),
        out_shape=(
            jax.ShapeDtypeStruct((owners * share, width + EXTRA), jnp.bfloat16),
            jax.ShapeDtypeStruct((HOT_PARTS * share, width), jnp.bfloat16),
            jax.ShapeDtypeStruct((count, 1), jnp.int32),
        ),
        in_specs=[whole()] * 3,
        out_specs=(whole(),) * 3,
        compiler_params=params(),
    )(request.reshape(1, -1), table.reshape(1, -1), tokens)


def down_kernel(rank, parts, *refs):
    rows_refs = refs[:parts]
    local_refs = refs[parts : 2 * parts]
    weight_ref = refs[2 * parts]
    out_refs = refs[2 * parts + 1 : 3 * parts + 1]
    totals = refs[3 * parts + 1 :]
    step = pl.program_id(0)
    for rows_ref, total in zip(rows_refs, totals):
        product = lax.dot_general(
            rows_ref[...],
            weight_ref[...],
            (((1,), (1,)), ((), ())),
            preferred_element_type=jnp.float32,
        )

        @pl.when(step == 0)
        def _():
            total[...] = product

        @pl.when(step > 0)
        def _():
            total[...] += product

    @pl.when(step == pl.num_programs(0) - 1)
    def _():
        for local_ref, out_ref, total in zip(local_refs, out_refs, totals):
            local = local_ref[...]
            count = local.shape[0]
            pair = LANES // rank
            lane_block = lax.broadcasted_iota(jnp.int32, (count, LANES), 1) // rank
            summed = jnp.zeros((count, LANES), jnp.float32)
            for j in range(total.shape[1] // LANES):
                hit = lane_block + j * pair == local
                summed = summed + jnp.where(hit, total[:, j * LANES : (j + 1) * LANES], 0.0)
            out = summed[:, :rank]
            for k in range(1, pair):
                out = out + summed[:, k * rank : (k + 1) * rank]
            out_ref[...] = out


def down(row_arrays, locals_, table, rank):
    stored_rank, width = table.shape
    parts = len(row_arrays)
    chunk = 512
    while width % chunk:
        chunk -= LANES
    steps = width // chunk
    return pl.pallas_call(
        functools.partial(down_kernel, rank, parts),
        grid=(steps,),
        out_shape=tuple(jax.ShapeDtypeStruct((r.shape[0], rank), jnp.float32) for r in row_arrays),
        in_specs=[pl.BlockSpec((r.shape[0], chunk), lambda k: (0, k)) for r in row_arrays]
        + [pl.BlockSpec((r.shape[0], 1), lambda k: (0, 0)) for r in row_arrays]
        + [pl.BlockSpec((stored_rank, chunk), lambda k: (0, k))],
        out_specs=tuple(pl.BlockSpec((r.shape[0], rank), lambda k: (0, 0)) for r in row_arrays),
        scratch_shapes=[pltpu.VMEM((r.shape[0], stored_rank), jnp.float32) for r in row_arrays],
        compiler_params=params(),
        cost_estimate=pl.CostEstimate(
            flops=2 * sum(r.shape[0] for r in row_arrays) * stored_rank * width,
            bytes_accessed=2 * stored_rank * width,
            transcendentals=0,
        ),
    )(*row_arrays, *locals_, table)


def up_kernel(rank, own_ref, other_ref, local_ref, weight_ref, out_ref):
    shrunk = (own_ref[...] + other_ref[...]).astype(jnp.bfloat16).astype(jnp.float32)
    count = shrunk.shape[0]
    stored_rank = weight_ref.shape[0]
    pair = LANES // rank
    doubled = jnp.concatenate([shrunk] * pair, axis=1)
    lane_block = lax.broadcasted_iota(jnp.int32, (count, LANES), 1) // rank
    local = local_ref[...]
    spread = jnp.concatenate(
        [
            jnp.where(lane_block + j * pair == local, doubled, 0.0).astype(jnp.bfloat16)
            for j in range(stored_rank // LANES)
        ],
        axis=1,
    )
    out_ref[...] = jnp.dot(spread, weight_ref[...], preferred_element_type=jnp.float32).astype(
        jnp.bfloat16
    )


def up(own, other, local, table):
    count, rank = own.shape
    return pl.pallas_call(
        functools.partial(up_kernel, rank),
        out_shape=jax.ShapeDtypeStruct((count, table.shape[1]), jnp.bfloat16),
        in_specs=[whole()] * 4,
        out_specs=whole(),
        compiler_params=params(),
        cost_estimate=pl.CostEstimate(
            flops=2 * count * table.shape[0] * table.shape[1],
            bytes_accessed=2 * table.shape[0] * table.shape[1],
            transcendentals=0,
        ),
    )(own, other, local, table)


def finish_kernel(
    head, own_ref, other_ref, cold_ref, hot_ref, place_ref, scale_ref, cos_ref, sin_ref, out_ref
):
    count, width = own_ref.shape
    cold_total = cold_ref.shape[0]
    hot_total = hot_ref.shape[0]
    place = place_ref[...]
    from_cold = place == lax.broadcasted_iota(jnp.int32, (count, cold_total), 1)
    from_hot = place - cold_total == lax.broadcasted_iota(jnp.int32, (count, hot_total), 1)
    delta = jnp.dot(
        from_cold.astype(jnp.float32).astype(jnp.bfloat16), cold_ref[...], preferred_element_type=jnp.float32
    ) + jnp.dot(
        from_hot.astype(jnp.float32).astype(jnp.bfloat16), hot_ref[...], preferred_element_type=jnp.float32
    )
    keys = own_ref[...] + other_ref[...] + delta
    cosine = cos_ref[...]
    sine = sin_ref[...]
    for h in range(width // head):
        one = keys[:, h * head : (h + 1) * head]
        normed = (
            one
            * lax.rsqrt(jnp.mean(one * one, axis=-1, keepdims=True) + 1e-06)
            * scale_ref[...]
        )
        turned = pltpu.roll(normed, head // 2, 1)
        out_ref[:, h * head : (h + 1) * head] = (normed * cosine + turned * sine).astype(jnp.bfloat16)


def finish(own, other, cold, hot, place, scale, cosine, sine):
    return pl.pallas_call(
        functools.partial(finish_kernel, scale.shape[0]),
        out_shape=jax.ShapeDtypeStruct(own.shape, jnp.bfloat16),
        in_specs=[whole()] * 8,
        out_specs=whole(),
        compiler_params=params(),
    )(own, other, cold, hot, place, scale.reshape(1, -1), cosine, sine)


def rope_tables(head, cached_token_length):
    half = head // 2
    inv_freq = rope_theta ** (-(jnp.arange(half, dtype=jnp.float32) * 2.0) / head)
    angles = cached_token_length.astype(jnp.float32)[:, None] * inv_freq[None, :]
    cosine = jnp.cos(angles)
    sine = jnp.sin(angles)
    return jnp.concatenate([cosine, cosine], axis=1), jnp.concatenate([-sine, sine], axis=1)


def swap(x):
    return lax.ppermute(x, "tensor", [(0, 1), (1, 0)])


def on_device(
    tokens,
    base_key_matrix,
    adapter_down_weight,
    adapter_up_weight,
    key_norm_scale,
    request_adapter,
    adapter_slot_table,
    cached_token_length,
):
    row_count, half_width = tokens.shape
    stored, rank, _ = adapter_down_weight.shape
    owners = lax.axis_size("dp")
    me = lax.axis_index("dp")
    side = lax.axis_index("tensor")
    share = (row_count + owners + 2) // (owners + 3)
    hot_count = HOT_PARTS * share
    down_table = adapter_down_weight.reshape(stored * rank, half_width)
    up_table = adapter_up_weight.reshape(stored * rank, -1)
    features = up_table.shape[1]

    cold_send, hot_send, place = pack(
        request_adapter, adapter_slot_table, tokens, stored, owners, share
    )

    ring = ring_order(owners)
    to_next = [(ring[i], ring[(i + 1) % owners]) for i in range(owners)]
    to_last = [(b, a) for a, b in to_next]
    spots = [0] * owners
    for spot, index in enumerate(ring):
        spots[index] = spot
    my_spot = jnp.take(jnp.array(spots, jnp.int32), me)
    ring_array = jnp.array(ring, jnp.int32)

    def source(distance):
        return jnp.take(ring_array, (my_spot + distance) % owners)

    cut = hot_count // 2 // 8 * 8 if hot_count >= 16 else hot_count // 2
    forward = backward = hot_send
    arrivals = [(0, hot_send)]
    for step in range(1, owners // 2):
        forward = lax.ppermute(forward, "dp", to_next)
        backward = lax.ppermute(backward, "dp", to_last)
        arrivals += [(-step, forward), (step, backward)]
    last_front = lax.ppermute(forward[:cut], "dp", to_next)
    last_rear = lax.ppermute(backward[cut:], "dp", to_last)

    got = lax.all_to_all(
        cold_send.reshape(owners, share, half_width + EXTRA), "dp", split_axis=0, concat_axis=0, tiled=True
    )
    routing = got[:, :, half_width : half_width + 1 + 2 * HOT_PARTS].astype(jnp.int32)
    cold_local = routing[:, :, 0].reshape(owners * share, 1)
    hot_local = jnp.where(
        routing[:, :, 1 + HOT_PARTS : 1 + 2 * HOT_PARTS] == me, routing[:, :, 1 : 1 + HOT_PARTS], -1
    )
    hot_local = jnp.transpose(hot_local, (0, 2, 1)).reshape(owners, hot_count)
    order = jnp.stack([source(d) for d, _ in arrivals] + [source(owners // 2)])
    hot_local = jnp.take(hot_local, order, axis=0)

    base = jnp.dot(tokens, base_key_matrix, preferred_element_type=jnp.float32)
    base_own = lax.dynamic_slice_in_dim(base, side * features, features, 1)
    base_other = swap(lax.dynamic_slice_in_dim(base, (1 - side) * features, features, 1))

    got_rows = got.reshape(owners * share, half_width + EXTRA)[:, :half_width]
    (cold_part,) = down([got_rows], [cold_local], down_table, rank)
    cold_delta = up(cold_part, swap(cold_part), cold_local, up_table)
    cold_back = lax.all_to_all(
        cold_delta.reshape(owners, share, features), "dp", split_axis=0, concat_axis=0, tiled=True
    ).reshape(owners * share, features)

    groups = [[0]] + [[2 * s - 1, 2 * s] for s in range(1, owners // 2)]
    columns = [hot_local[i].reshape(hot_count, 1) for i in range(owners)]
    parts = []
    for group in groups:
        parts += down([arrivals[i][1] for i in group], [columns[i] for i in group], down_table, rank)
    parts += down(
        [last_front, last_rear], [columns[-1][:cut], columns[-1][cut:]], down_table, rank
    )
    hot_part = jnp.concatenate(parts, axis=0)
    hot_delta = up(hot_part, swap(hot_part), hot_local.reshape(-1, 1), up_table)
    by_source = jnp.zeros((owners,), jnp.int32).at[order].set(jnp.arange(owners, dtype=jnp.int32))
    hot_return = jnp.take(hot_delta.reshape(owners, hot_count, features), by_source, axis=0)
    hot_got = lax.all_to_all(hot_return, "dp", split_axis=0, concat_axis=0, tiled=True)
    hot_back = jnp.sum(hot_got.astype(jnp.float32), axis=0).astype(jnp.bfloat16)

    cosine, sine = rope_tables(key_norm_scale.shape[0], cached_token_length)
    return finish(base_own, base_other, cold_back, hot_back, place, key_norm_scale, cosine, sine)


def solution(mesh):
    placed = (
        P(("groups", "dp"), "tensor"),
        P("tensor", None),
        P(("groups", "dp"), None, "tensor"),
        P(("groups", "dp"), None, "tensor"),
        P(),
        P(("groups", "dp")),
        P("groups"),
        P(("groups", "dp")),
    )
    return jax.shard_map(
        on_device,
        mesh=mesh,
        in_specs=placed,
        out_specs=P(("groups", "dp"), "tensor"),
        check_vma=False,
    )
```

time: 177 us -> 151 us (0.85)
  waiting for transfers between devices: 101 us -> 41 us
  Pallas kernels: 0 us -> 35.8 us
  starting transfers between devices: 16.5 us -> 30.5 us
  matrix products: 16.7 us -> 4 us
  local copies, waits for them, and re-layouts: 16.2 us -> 28.2 us
  between operations: 13.6 us -> 6.01 us
  blocking collectives: 3.97 us -> 0 us
  other arithmetic: 8.17 us -> 4.86 us
    all_to_all x3, waiting for transfers between devices: 101 us -> 9.09 us  [the longest x1 6.33 us: on_device(): lax.all_to_all(cold_delta.reshape(owners, share, features), 'dp', split_a...]
    pallas_call x0 -> x10, Pallas kernels: none -> 35.8 us  [the longest x6 29.5 us: down(): pl.pallas_call(functools.partial(down_kernel, rank, parts), grid=(steps,)...]
    ppermute x0 -> x11, waiting for transfers between devices: none -> 31.9 us  [the longest x3 29.4 us: on_device(): forward = lax.ppermute(forward, 'dp', to_next)]
    unnamed x9 -> x40, local copies, waits for them, and re-layouts: 0.76 us -> 16.7 us
    ppermute x0 -> x11, starting transfers between devices: none -> 15.5 us  [the longest x3 11.5 us: on_device(): forward = lax.ppermute(forward, 'dp', to_next)]
    dot_general x3 -> x1, matrix products: 16.7 us -> 4 us  [on_device(): base = jnp.dot(tokens, base_key_matrix, preferred_element_type=jnp.float32)]
    scatter x2 -> x1, local copies, waits for them, and re-layouts: 7.18 us -> 0.6 us  [on_device(): jnp.zeros((owners,), jnp.int32).at[order]]
    psum x1 -> x0, blocking collectives: 3.97 us -> none  [on_device(): reduced_input = lax.psum(partial_reduced, 'tensor').astype(jnp.bfloat16)]
  transfers between devices with their start and end apart: 4 -> 14, of which waited for: 3 -> 6; matrix products, arithmetic and copies ran while one was open for 18% -> 14% of each run, Pallas kernels for 0% -> 17%
where the time goes in v1:
time: 151 us; the launch traced here: 150 us
  waiting for transfers between devices  41 us (27%)
  Pallas kernels  35.8 us (24%)
  starting transfers between devices  30.5 us (20%)
  local copies, waits for them, and re-layouts  28.2 us (19%)
  between operations  6.01 us (4%)
  other arithmetic  4.86 us (3%)
  matrix products  4 us (3%)
    pallas_call x6, Pallas kernels, down(): pl.pallas_call(functools.partial(down_kernel, rank, parts), grid=(steps,)...  29.5 us
    ppermute x3, waiting for transfers between devices, on_device(): forward = lax.ppermute(forward, 'dp', to_next)  29.4 us
    unnamed x40, local copies, waits for them, and re-layouts  16.7 us
    ppermute x3, starting transfers between devices, on_device(): forward = lax.ppermute(forward, 'dp', to_next)  11.5 us
    all_to_all x1, starting transfers between devices, on_device(): lax.all_to_all(cold_send.reshape(owners, share, half_width + EXTRA), 'dp'...  7.25 us
    all_to_all x1, waiting for transfers between devices, on_device(): lax.all_to_all(cold_delta.reshape(owners, share, features), 'dp', split_a...  6.33 us
    all_to_all x1, starting transfers between devices, on_device(): lax.all_to_all(hot_return, 'dp', split_axis=0, concat_axis=0, tiled=True)  4.19 us
    dot_general x1, matrix products, on_device(): base = jnp.dot(tokens, base_key_matrix, preferred_element_type=jnp.float32)  4 us
  transfers between devices with their start and end apart: 14, of which 6 were waited for; matrix products, arithmetic and copies ran while one was open for 14% of the time, Pallas kernels for 17%

profile of v1, /device:TPU:0, one launch (start us, length us, event | category | flops | bytes accessed | tf_op | source)
XLA Modules:
  0.0 150.3 jit_solution(13618695733223526850)
XLA Ops:
  2.7 2.0 %shard_map.100 = (bf16[192,2688]{1,0:T(8,128)(2,1)}, bf16[72,2560]{1,0:T(8,128)(2,1)S(1)}, s32[256,1]{1,0:T(8,128)S(1)}) custom-call(s32[1,256]{1,0:T(1,128)S(1)} %bitcast.67, s32[1,128]{1,0:T(1,128)S(1)} %bitcast.68, bf16[256,2560]{1,0:T(8,128)(2,1)S(1)} %copy-done.4), custom_call_target="tpu_custom_call" | custom-call | tf_op jit(solution)/shard_map/pallas_call | solution.py:87
  4.7 7.3 %all-to-all-start = ((bf16[8,24,2688]{2,1,0:T(8,128)(2,1)}), bf16[8,24,2688]{2,1,0:T(8,128)(2,1)}, u32[]{:S(2)}, u32[]{:S(2)}) async-start(bf16[8,24,2688]{2,1,0:T(8,128)(2,1)} %bitcast.2), calls=%async_computation | async-start | bytes 2064384 | tf_op jit(solution)/shard_map/all_to_all | solution.py:299
  11.9 2.0 %collective-permute-start.2 = (bf16[72,2560]{1,0:T(8,128)(2,1)S(1)}, bf16[72,2560]{1,0:T(8,128)(2,1)S(1)}, u32[]{:S(2)}, u32[]{:S(2)}) collective-permute-start(bf16[72,2560]{1,0:T(8,128)(2,1)S(1)} %get-tuple-element.17.refs_0_), channel_id=1, source_target_pairs={{0,4},{4,8},{8,12},{12,14},{14,10},{10,6},{6,2},{2,0},{1,5},{5,9},... | collective-permute-start | bytes 1105928 | tf_op jit(solution)/shard_map/ppermute | solution.py:293
  14.0 22.6 %collective-permute-done.2.refs_0_ = bf16[72,2560]{1,0:T(8,128)(2,1)S(1)} collective-permute-done((bf16[72,2560]{1,0:T(8,128)(2,1)S(1)}, bf16[72,2560]{1,0:T(8,128)(2,1)S(1)}, u32[]{:S(2)}, u32[]{:S(2)}) %collective-permute-start.2) | collective-permute-done | bytes 368672 | tf_op jit(solution)/shard_map/ppermute | solution.py:293
  36.6 7.0 %collective-permute-start.4 = (bf16[72,2560]{1,0:T(8,128)(2,1)S(1)}, bf16[72,2560]{1,0:T(8,128)(2,1)S(1)}, u32[]{:S(2)}, u32[]{:S(2)}) collective-permute-start(bf16[72,2560]{1,0:T(8,128)(2,1)S(1)} %collective-permute-done.2.refs_0_), channel_id=1, source_target_pairs={{0,4},{4,8},{8,12},{12,14},{14,10},{10,6},{6,2},{2,0},{1,5},{5,9},... | collective-permute-start | bytes 1105928 | tf_op jit(solution)/shard_map/ppermute | solution.py:293
  45.8 1.7 %fusion.5 = (s32[1]{0:T(128)}, s32[1]{0:T(128)}, s32[1]{0:T(128)}, s32[1]{0:T(128)}, s32[1]{0:T(128)}, /*index=5*/s32[1]{0:T(128)}, s32[1]{0:T(128)}, s32[1]{0:T(128)}) fusion(s32[8]{0:T(128)} %constant.173.clone..sunk.16, s32[]{:T(128)S(6)} %select_n.166, s32[]{:T(128)S(6)} %select_n.163, s32[]{:T(128)S(6)} %select_n.160, s32[]{:T(128)S(6)} %select_n.157, ...), kind=kLoop, calls=%fused_computation.45 | loop fusion | bytes 96 | solution.py:287
  52.4 2.5 %collective-permute-start.6 = (bf16[72,2560]{1,0:T(8,128)(2,1)S(1)}, bf16[72,2560]{1,0:T(8,128)(2,1)S(1)}, u32[]{:S(2)}, u32[]{:S(2)}) collective-permute-start(bf16[72,2560]{1,0:T(8,128)(2,1)S(1)} %collective-permute-done.4.refs_0_), channel_id=1, source_target_pairs={{0,4},{4,8},{8,12},{12,14},{14,10},{10,6},{6,2},{2,0},{1,5},{5,9},... | collective-permute-start | bytes 1105928 | tf_op jit(solution)/shard_map/ppermute | solution.py:293
  56.9 6.7 %collective-permute-done.6.refs_0_ = bf16[72,2560]{1,0:T(8,128)(2,1)S(1)} collective-permute-done((bf16[72,2560]{1,0:T(8,128)(2,1)S(1)}, bf16[72,2560]{1,0:T(8,128)(2,1)S(1)}, u32[]{:S(2)}, u32[]{:S(2)}) %collective-permute-start.6) | collective-permute-done | bytes 368672 | tf_op jit(solution)/shard_map/ppermute | solution.py:293
  70.1 2.5 %copy-done = bf16[16,64,2560]{2,1,0:T(8,128)(2,1)S(1)} copy-done((bf16[16,64,2560]{2,1,0:T(8,128)(2,1)S(1)}, bf16[16,64,2560]{2,1,0:T(8,128)(2,1)}, u32[]{:S(2)}) %copy-start) | copy-done | bytes 5242904
  72.6 2.9 %shard_map.103 = f32[72,64]{1,0:T(8,128)S(1)} custom-call(bf16[72,2560]{1,0:T(8,128)(2,1)S(1)} %get-tuple-element.17.refs_0_, s32[72,1]{1,0:T(8,128)S(1)} %copy.40.refs_1_, bf16[1024,2560]{1,0:T(8,128)(2,1)S(1)} %bitcast.56), custom_call_target="tpu_custom_call" | custom-call | flops 377487360 | bytes 5242880 | tf_op jit(solution)/shard_map/pallas_call | solution.py:147
  76.8 2.5 %copy-done.1 = bf16[16,64,2560]{2,1,0:T(8,128)(2,1)S(1)} copy-done((bf16[16,64,2560]{2,1,0:T(8,128)(2,1)S(1)}, bf16[16,64,2560]{2,1,0:T(8,128)(2,1)}, u32[]{:S(2)}) %copy-start.1) | copy-done | bytes 5242904
  79.2 5.3 %shard_map.104 = (f32[72,64]{1,0:T(8,128)S(1)}, f32[72,64]{1,0:T(8,128)S(1)}) custom-call(bf16[72,2560]{1,0:T(8,128)(2,1)S(1)} %collective-permute-done.2.refs_0_, bf16[72,2560]{1,0:T(8,128)(2,1)S(1)} %collective-permute-done.3.refs_1_, s32[72,1]{1,0:T(8,128)S(1)} %copy.41.refs_2_, s32[72,1]{1,0:T(8,128)S(1)} %copy.42.refs_3_, bf16[1024,2560]{1,0:T(8,128)(2,1)S(1)} %bitcast.57), custom_call_target="tpu_custom_call" | custom-call | flops 754974720 | bytes 5242880 | tf_op jit(solution)/shard_map/pallas_call | solution.py:147
  85.8 5.3 %shard_map.105 = (f32[72,64]{1,0:T(8,128)S(1)}, f32[72,64]{1,0:T(8,128)S(1)}) custom-call(bf16[72,2560]{1,0:T(8,128)(2,1)S(1)} %collective-permute-done.4.refs_0_, bf16[72,2560]{1,0:T(8,128)(2,1)S(1)} %collective-permute-done.5.refs_1_, s32[72,1]{1,0:T(8,128)S(1)} %copy.43.refs_2_, s32[72,1]{1,0:T(8,128)S(1)} %copy.44.refs_3_, bf16[1024,2560]{1,0:T(8,128)(2,1)S(1)} %bitcast.58), custom_call_target="tpu_custom_call" | custom-call | flops 754974720 | bytes 5242880 | tf_op jit(solution)/shard_map/pallas_call | solution.py:147
  92.4 5.3 %shard_map.106 = (f32[72,64]{1,0:T(8,128)S(1)}, f32[72,64]{1,0:T(8,128)S(1)}) custom-call(bf16[72,2560]{1,0:T(8,128)(2,1)S(1)} %collective-permute-done.6.refs_0_, bf16[72,2560]{1,0:T(8,128)(2,1)S(1)} %collective-permute-done.7.refs_1_, s32[72,1]{1,0:T(8,128)S(1)} %copy.45.refs_2_, s32[72,1]{1,0:T(8,128)S(1)} %copy.46.refs_3_, bf16[1024,2560]{1,0:T(8,128)(2,1)S(1)} %bitcast.59), custom_call_target="tpu_custom_call" | custom-call | flops 754974720 | bytes 5242880 | tf_op jit(solution)/shard_map/pallas_call | solution.py:147
  99.2 2.5 %copy-done.2 = bf16[16,64,2560]{2,1,0:T(8,128)(2,1)S(1)} copy-done((bf16[16,64,2560]{2,1,0:T(8,128)(2,1)S(1)}, bf16[16,64,2560]{2,1,0:T(8,128)(2,1)}, u32[]{:S(2)}) %copy-start.2) | copy-done | bytes 5242904
  101.7 4.9 %shard_map.107 = (f32[32,64]{1,0:T(8,128)S(1)}, f32[40,64]{1,0:T(8,128)S(1)}) custom-call(bf16[32,2560]{1,0:T(8,128)(2,1)S(1)} %collective-permute-done.8.refs_0_, bf16[40,2560]{1,0:T(8,128)(2,1)S(1)} %collective-permute-done.9.refs_1_, s32[32,1]{1,0:T(8,128)S(1)} %copy.47.refs_2_, s32[40,1]{1,0:T(8,128)S(1)} %copy.48.refs_3_, bf16[1024,2560]{1,0:T(8,128)(2,1)S(1)} %bitcast.60), custom_call_target="tpu_custom_call" | custom-call | flops 377487360 | bytes 5242880 | tf_op jit(solution)/shard_map/pallas_call | solution.py:147
  111.3 1.8 %shard_map.108 = bf16[576,512]{1,0:T(8,128)(2,1)S(1)} custom-call(f32[576,64]{1,0:T(8,128)} %constant_dynamic-update-slice_fusion.own_ref, f32[576,64]{1,0:T(8,128)S(1)} %copy-done.7, s32[576,1]{1,0:T(8,128)S(1)} %select_n.184.local_ref, bf16[1024,512]{1,0:T(8,128)(2,1)S(1)} %bitcast.61), custom_call_target="tpu_custom_call" | custom-call | flops 603979776 | bytes 1048576 | tf_op jit(solution)/shard_map/pallas_call | solution.py:187
  114.5 2.0 %broadcast_select_fusion = bf16[8,72,512]{2,1,0:T(8,128)(2,1)} fusion(bf16[8,72,512]{2,1,0:T(8,128)(2,1)} %gather_fusion.1, pred[8]{0:T(512)(128)(4,1)S(1)} %get-tuple-element.228), kind=kLoop, calls=%fused_computation.3 | loop fusion | flops 294912 | bytes 1179656 | tf_op jit(solution)/shard_map/jit(_take)/select_n | solution.py:333
  116.5 4.2 %all-to-all-start.2 = ((bf16[8,72,512]{2,1,0:T(8,128)(2,1)}), bf16[8,72,512]{2,1,0:T(8,128)(2,1)}, u32[]{:S(2)}, u32[]{:S(2)}) async-start(bf16[8,72,512]{2,1,0:T(8,128)(2,1)} %broadcast_select_fusion), calls=%async_computation.2 | async-start | bytes 1179648 | tf_op jit(solution)/shard_map/all_to_all | solution.py:334
  120.7 4.0 %fusion.6 = f32[256,1024]{1,0:T(8,128)S(1)} fusion(bf16[256,2560]{1,0:T(8,128)(2,1)S(1)} %copy-done.5, bf16[2560,1024]{1,0:T(8,128)(2,1)} %param.11), kind=kOutput, calls=%fused_computation.46 | convolution fusion | flops 1342177280 | bytes 7602176 | tf_op jit(solution)/shard_map/dot_general | solution.py:311
  126.3 5.7 %shard_map.101.own_ref = f32[192,64]{1,0:T(8,128)S(1)} custom-call(bf16[192,2560]{1,0:T(8,128)(2,1)S(1)} %slice.124.refs_0_, s32[192,1]{1,0:T(8,128)S(1)} %bitcast.63, bf16[1024,2560]{1,0:T(8,128)(2,1)} %bitcast.55), custom_call_target="tpu_custom_call" | custom-call | flops 1006632960 | bytes 5242880 | tf_op jit(solution)/shard_map/pallas_call | solution.py:147
  134.5 2.8 %all-to-all-done.2 = bf16[8,72,512]{2,1,0:T(8,128)(2,1)} async-done(((bf16[8,72,512]{2,1,0:T(8,128)(2,1)}), bf16[8,72,512]{2,1,0:T(8,128)(2,1)}, u32[]{:S(2)}, u32[]{:S(2)}) %all-to-all-start.2) | async-done | bytes 589856 | tf_op jit(solution)/shard_map/all_to_all | solution.py:334
  137.2 3.6 %all-to-all-start.1 = ((bf16[8,24,512]{2,1,0:T(8,128)(2,1)}), bf16[8,24,512]{2,1,0:T(8,128)(2,1)S(1)}, u32[]{:S(2)}, u32[]{:S(2)}) async-start(bf16[8,24,512]{2,1,0:T(8,128)(2,1)} %bitcast.8), calls=%async_computation.1 | async-start | bytes 393216 | tf_op jit(solution)/shard_map/all_to_all | solution.py:318
  142.6 6.3 %all-to-all-done.1 = bf16[8,24,512]{2,1,0:T(8,128)(2,1)S(1)} async-done(((bf16[8,24,512]{2,1,0:T(8,128)(2,1)}), bf16[8,24,512]{2,1,0:T(8,128)(2,1)S(1)}, u32[]{:S(2)}, u32[]{:S(2)}) %all-to-all-start.1) | async-done | bytes 196640 | tf_op jit(solution)/shard_map/all_to_all | solution.py:318
  (97 shorter events, 30.9 us)
Async XLA Ops:
  4.7 62.4 %all-to-all-start = ((bf16[8,24,2688]{2,1,0:T(8,128)(2,1)}), bf16[8,24,2688]{2,1,0:T(8,128)(2,1)}, u32[]{:S(2)}, u32[]{:S(2)}) async-start(bf16[8,24,2688]{2,1,0:T(8,128)(2,1)} %bitcast.2), calls=%async_computation | async-start | bytes 2064384 | tf_op jit(solution)/shard_map/all_to_all | solution.py:299
  11.9 24.7 %collective-permute-start.2 = (bf16[72,2560]{1,0:T(8,128)(2,1)S(1)}, bf16[72,2560]{1,0:T(8,128)(2,1)S(1)}, u32[]{:S(2)}, u32[]{:S(2)}) collective-permute-start(bf16[72,2560]{1,0:T(8,128)(2,1)S(1)} %get-tuple-element.17.refs_0_), channel_id=1, source_target_pairs={{0,4},{4,8},{8,12},{12,14},{14,10},{10,6},{6,2},{2,0},{1,5},{5,9},... | collective-permute-start | bytes 1105928 | tf_op jit(solution)/shard_map/ppermute | solution.py:293
  14.0 29.7 %collective-permute-start.3 = (bf16[72,2560]{1,0:T(8,128)(2,1)S(1)}, bf16[72,2560]{1,0:T(8,128)(2,1)S(1)}, u32[]{:S(2)}, u32[]{:S(2)}) collective-permute-start(bf16[72,2560]{1,0:T(8,128)(2,1)S(1)} %get-tuple-element.17.refs_0_), channel_id=1, source_target_pairs={{4,0},{8,4},{12,8},{14,12},{10,14},{6,10},{2,6},{0,2},{5,1},{9,5},... | collective-permute-start | bytes 1105928 | tf_op jit(solution)/shard_map/ppermute | solution.py:294
  36.6 15.8 %collective-permute-start.4 = (bf16[72,2560]{1,0:T(8,128)(2,1)S(1)}, bf16[72,2560]{1,0:T(8,128)(2,1)S(1)}, u32[]{:S(2)}, u32[]{:S(2)}) collective-permute-start(bf16[72,2560]{1,0:T(8,128)(2,1)S(1)} %collective-permute-done.2.refs_0_), channel_id=1, source_target_pairs={{0,4},{4,8},{8,12},{12,14},{14,10},{10,6},{6,2},{2,0},{1,5},{5,9},... | collective-permute-start | bytes 1105928 | tf_op jit(solution)/shard_map/ppermute | solution.py:293
  43.6 11.3 %collective-permute-start.5 = (bf16[72,2560]{1,0:T(8,128)(2,1)S(1)}, bf16[72,2560]{1,0:T(8,128)(2,1)S(1)}, u32[]{:S(2)}, u32[]{:S(2)}) collective-permute-start(bf16[72,2560]{1,0:T(8,128)(2,1)S(1)} %collective-permute-done.3.refs_1_), channel_id=1, source_target_pairs={{4,0},{8,4},{12,8},{14,12},{10,14},{6,10},{2,6},{0,2},{5,1},{9,5},... | collective-permute-start | bytes 1105928 | tf_op jit(solution)/shard_map/ppermute | solution.py:294
  52.4 11.2 %collective-permute-start.6 = (bf16[72,2560]{1,0:T(8,128)(2,1)S(1)}, bf16[72,2560]{1,0:T(8,128)(2,1)S(1)}, u32[]{:S(2)}, u32[]{:S(2)}) collective-permute-start(bf16[72,2560]{1,0:T(8,128)(2,1)S(1)} %collective-permute-done.4.refs_0_), channel_id=1, source_target_pairs={{0,4},{4,8},{8,12},{12,14},{14,10},{10,6},{6,2},{2,0},{1,5},{5,9},... | collective-permute-start | bytes 1105928 | tf_op jit(solution)/shard_map/ppermute | solution.py:293
  55.0 10.9 %collective-permute-start.7 = (bf16[72,2560]{1,0:T(8,128)(2,1)S(1)}, bf16[72,2560]{1,0:T(8,128)(2,1)S(1)}, u32[]{:S(2)}, u32[]{:S(2)}) collective-permute-start(bf16[72,2560]{1,0:T(8,128)(2,1)S(1)} %collective-permute-done.5.refs_1_), channel_id=1, source_target_pairs={{4,0},{8,4},{12,8},{14,12},{10,14},{6,10},{2,6},{0,2},{5,1},{9,5},... | collective-permute-start | bytes 1105928 | tf_op jit(solution)/shard_map/ppermute | solution.py:294
  56.9 11.0 %copy-start.13 = (s32[8]{0:T(128)}, s32[8]{0:T(128)S(1)}, u32[]{:S(2)}) copy-start(s32[8]{0:T(128)S(1)} %scatter_custom_fusion) | copy-start | bytes 100
  64.3 34.9 %collective-permute-start.8 = (bf16[32,2560]{1,0:T(8,128)(2,1)}, bf16[32,2560]{1,0:T(8,128)(2,1)S(1)}, u32[]{:S(2)}, u32[]{:S(2)}) collective-permute-start(bf16[32,2560]{1,0:T(8,128)(2,1)} %slice.129), channel_id=1, source_target_pairs={{0,4},{4,8},{8,12},{12,14},{14,10},{10,6},{6,2},{2,0},{1,5},{5,9},... | collective-permute-start | bytes 491528 | tf_op jit(solution)/shard_map/ppermute | solution.py:296
  66.6 32.6 %collective-permute-start.9 = (bf16[40,2560]{1,0:T(8,128)(2,1)}, bf16[40,2560]{1,0:T(8,128)(2,1)S(1)}, u32[]{:S(2)}, u32[]{:S(2)}) collective-permute-start(bf16[40,2560]{1,0:T(8,128)(2,1)} %slice.130), channel_id=1, source_target_pairs={{4,0},{8,4},{12,8},{14,12},{10,14},{6,10},{2,6},{0,2},{5,1},{9,5},... | collective-permute-start | bytes 614408 | tf_op jit(solution)/shard_map/ppermute | solution.py:297
  70.1 2.5 %copy-start = (bf16[16,64,2560]{2,1,0:T(8,128)(2,1)S(1)}, bf16[16,64,2560]{2,1,0:T(8,128)(2,1)}, u32[]{:S(2)}) copy-start(bf16[16,64,2560]{2,1,0:T(8,128)(2,1)} %param.12) | copy-start | bytes 15728644
  85.8 12.5 %copy-start.12 = (s32[32,1]{0,1:T(1,128)S(1)}, s32[32,1]{0,1:T(1,128)}, u32[]{:S(2)}) copy-start(s32[32,1]{0,1:T(1,128)} %slice_bitcast_fusion.1) | copy-start | bytes 388
  85.8 12.6 %copy-start.15 = (s32[40,1]{0,1:T(1,128)S(1)}, s32[40,1]{0,1:T(1,128)}, u32[]{:S(2)}) copy-start(s32[40,1]{0,1:T(1,128)} %slice_bitcast_fusion) | copy-start | bytes 484
  92.4 17.9 %copy-start.3 = (bf16[16,64,512]{2,1,0:T(8,128)(2,1)S(1)}, bf16[16,64,512]{2,1,0:T(8,128)(2,1)}, u32[]{:S(2)}) copy-start(bf16[16,64,512]{2,1,0:T(8,128)(2,1)} %param.13) | copy-start | bytes 3145732
  97.7 10.0 %copy-start.14 = (s32[8]{0:T(128)S(1)}, s32[8]{0:T(128)}, u32[]{:S(2)}) copy-start(s32[8]{0:T(128)} %copy-done.13) | copy-start | bytes 100
  99.2 2.5 %copy-start.2 = (bf16[16,64,2560]{2,1,0:T(8,128)(2,1)S(1)}, bf16[16,64,2560]{2,1,0:T(8,128)(2,1)}, u32[]{:S(2)}) copy-start(bf16[16,64,2560]{2,1,0:T(8,128)(2,1)} %param.12) | copy-start | bytes 15728644
  101.7 19.0 %copy-start.5 = (bf16[256,2560]{1,0:T(8,128)(2,1)S(1)}, bf16[256,2560]{1,0:T(8,128)(2,1)}, u32[]{:S(2)}) copy-start(bf16[256,2560]{1,0:T(8,128)(2,1)} %tokens_ref.1) | copy-start | bytes 3932164
  107.8 1.8 %collective-permute-start.10 = (f32[576,64]{1,0:T(8,128)}, f32[576,64]{1,0:T(8,128)S(1)}, u32[]{:S(2)}, u32[]{:S(2)}) collective-permute-start(f32[576,64]{1,0:T(8,128)} %constant_dynamic-update-slice_fusion.own_ref), channel_id=1, source_target_pairs={{0,1},{1,0},{2,3},{3,2},{4,5},{5,4},{6,7},{7,6},{8,9},{9,8},{10,11... | collective-permute-start | bytes 442376 | tf_op jit(solution)/shard_map/ppermute | solution.py:249
  116.5 20.8 %all-to-all-start.2 = ((bf16[8,72,512]{2,1,0:T(8,128)(2,1)}), bf16[8,72,512]{2,1,0:T(8,128)(2,1)}, u32[]{:S(2)}, u32[]{:S(2)}) async-start(bf16[8,72,512]{2,1,0:T(8,128)(2,1)} %broadcast_select_fusion), calls=%async_computation.2 | async-start | bytes 1179648 | tf_op jit(solution)/shard_map/all_to_all | solution.py:334
  124.7 7.7 %copy-start.11 = (s32[256]{0:T(256)S(1)}, s32[256]{0:T(256)}, u32[]{:S(2)}) copy-start(s32[256]{0:T(256)} %param.17) | copy-start | bytes 3076
  124.8 17.8 %collective-permute-start = (f32[256,512]{1,0:T(8,128)S(1)}, f32[256,512]{1,0:T(8,128)S(1)}, u32[]{:S(2)}, u32[]{:S(2)}) collective-permute-start(f32[256,512]{1,0:T(8,128)S(1)} %get-tuple-element.207), channel_id=1, source_target_pairs={{0,1},{1,0},{2,3},{3,2},{4,5},{5,4},{6,7},{7,6},{8,9},{9,8},{10,11... | collective-permute-start | bytes 1572872 | tf_op jit(solution)/shard_map/ppermute | solution.py:249
  126.2 22.7 %copy-start.10 = (f32[128]{0:T(128)S(1)}, f32[128]{0:T(128)}, u32[]{:S(2)}) copy-start(f32[128]{0:T(128)} %param.14) | copy-start | bytes 1540
  131.9 1.4 collective-permute-start.1
  137.2 11.7 %all-to-all-start.1 = ((bf16[8,24,512]{2,1,0:T(8,128)(2,1)}), bf16[8,24,512]{2,1,0:T(8,128)(2,1)S(1)}, u32[]{:S(2)}, u32[]{:S(2)}) async-start(bf16[8,24,512]{2,1,0:T(8,128)(2,1)} %bitcast.8), calls=%async_computation.1 | async-start | bytes 393216 | tf_op jit(solution)/shard_map/all_to_all | solution.py:318
  (6 other events, 6.8 us)

commit v2 on v1

v2 whole, which is shorter than its diff:
```python
import functools

import jax
import jax.numpy as jnp
from jax import lax
from jax.experimental import pallas as pl
from jax.experimental.pallas import tpu as pltpu
from jax.sharding import PartitionSpec as P

rope_theta = 1000000.0
LANES = 128
EXTRA = 128
HOT_PARTS = 3
VMEM_BYTES = 60 * 1024 * 1024


def whole():
    return pl.BlockSpec(memory_space=pltpu.VMEM)


def params():
    return pltpu.CompilerParams(vmem_limit_bytes=VMEM_BYTES)


def ring_order(owners):
    return [i for i in range(0, owners, 2)] + [i for i in range(owners - 1, 0, -2)]


def to_column(row):
    count = row.shape[1]
    square = lax.broadcasted_iota(jnp.int32, (count, count), 0) == lax.broadcasted_iota(
        jnp.int32, (count, count), 1
    )
    return jnp.sum(jnp.where(square, row, 0), axis=1, keepdims=True)


def pack_kernel(
    stored, owners, share, request_ref, table_ref, tokens_ref, cold_ref, hot_ref, place_ref, busy_ref
):
    count = request_ref.shape[1]
    width = tokens_ref.shape[1]
    request_col = to_column(request_ref[...])
    adapters = table_ref.shape[1]
    match = request_col == lax.broadcasted_iota(jnp.int32, (count, adapters), 1)
    slot_col = jnp.sum(jnp.where(match, table_ref[...], 0), axis=1, keepdims=True)
    row_id = lax.broadcasted_iota(jnp.int32, (count, count), 0)
    col_id = lax.broadcasted_iota(jnp.int32, (count, count), 1)
    slot_row = jnp.sum(jnp.where(row_id == col_id, slot_col, 0), axis=0, keepdims=True)
    owner_col = slot_col // stored
    owner_row = slot_row // stored
    same = owner_col == owner_row
    rank_col = jnp.sum(jnp.where(same & (col_id < row_id), 1, 0), axis=1, keepdims=True)
    rank_row = jnp.sum(jnp.where(same & (row_id < col_id), 1, 0), axis=0, keepdims=True)
    cold_total = owners * share
    hot_total = HOT_PARTS * share

    def place(owner, rank):
        return jnp.where(rank < share, owner * share + rank, cold_total + rank - share)

    place_ref[...] = place(owner_col, rank_col)
    busy_ref[...] = jnp.max(jnp.where(rank_row >= share, owner_row, 0), axis=1, keepdims=True)
    place_row = place(owner_row, rank_row)
    local_row = slot_row - owner_row * stored
    tokens = tokens_ref[...]
    for first, total, out_ref in ((0, cold_total, cold_ref), (cold_total, hot_total, hot_ref)):
        pick = place_row - first == lax.broadcasted_iota(jnp.int32, (total, count), 0)
        out_ref[:, :width] = jnp.dot(
            pick.astype(jnp.float32).astype(jnp.bfloat16), tokens, preferred_element_type=jnp.float32
        ).astype(jnp.bfloat16)
        owner = jnp.sum(jnp.where(pick, owner_row + 1, 0), axis=1, keepdims=True) - 1
        local = jnp.sum(jnp.where(pick, local_row, 0), axis=1, keepdims=True)
        lane = lax.broadcasted_iota(jnp.int32, (total, EXTRA), 1)
        extra = jnp.where(lane == 0, owner, jnp.where(lane == 1, local, 0))
        out_ref[:, width:] = extra.astype(jnp.float32).astype(jnp.bfloat16)


def pack(request, table, tokens, stored, owners, share):
    count, width = tokens.shape
    return pl.pallas_call(
        functools.partial(pack_kernel, stored, owners, share),
        out_shape=(
            jax.ShapeDtypeStruct((owners * share, width + EXTRA), jnp.bfloat16),
            jax.ShapeDtypeStruct((HOT_PARTS * share, width + EXTRA), jnp.bfloat16),
            jax.ShapeDtypeStruct((count, 1), jnp.int32),
            jax.ShapeDtypeStruct((1, 1), jnp.int32),
        ),
        in_specs=[whole()] * 3,
        out_specs=(whole(),) * 4,
        compiler_params=params(),
    )(request.reshape(1, -1), table.reshape(1, -1), tokens)


def local_column(extra, me):
    extra = extra.astype(jnp.float32)
    return jnp.where(extra[:, 0:1] == me.astype(jnp.float32), extra[:, 1:2], -1.0).astype(jnp.int32)


def down_kernel(rank, parts, me_ref, *refs):
    rows_refs = refs[:parts]
    extra_refs = refs[parts : 2 * parts]
    weight_ref, out_ref, total = refs[2 * parts :]
    step = pl.program_id(0)
    rows = rows_refs[0][...] if parts == 1 else jnp.concatenate([r[...] for r in rows_refs], axis=0)
    product = lax.dot_general(
        rows, weight_ref[...], (((1,), (1,)), ((), ())), preferred_element_type=jnp.float32
    )

    @pl.when(step == 0)
    def _():
        total[...] = product

    @pl.when(step > 0)
    def _():
        total[...] += product

    @pl.when(step == pl.num_programs(0) - 1)
    def _():
        local = jnp.concatenate([local_column(r[...], me_ref[0]) for r in extra_refs], axis=0)
        count = local.shape[0]
        pair = LANES // rank
        lane_block = lax.broadcasted_iota(jnp.int32, (count, LANES), 1) // rank
        summed = jnp.zeros((count, LANES), jnp.float32)
        for j in range(total.shape[1] // LANES):
            hit = lane_block + j * pair == local
            summed = summed + jnp.where(hit, total[:, j * LANES : (j + 1) * LANES], 0.0)
        out = summed[:, :rank]
        for k in range(1, pair):
            out = out + summed[:, k * rank : (k + 1) * rank]
        out_ref[...] = out


def down(me, row_arrays, table, rank):
    stored_rank, width = table.shape
    parts = len(row_arrays)
    count = sum(r.shape[0] for r in row_arrays)
    chunk = 512
    while width % chunk:
        chunk -= LANES
    last = width // EXTRA
    return pl.pallas_call(
        functools.partial(down_kernel, rank, parts),
        grid_spec=pltpu.PrefetchScalarGridSpec(
            num_scalar_prefetch=1,
            grid=(width // chunk,),
            in_specs=[pl.BlockSpec((r.shape[0], chunk), lambda k, m: (0, k)) for r in row_arrays]
            + [pl.BlockSpec((r.shape[0], EXTRA), lambda k, m: (0, last)) for r in row_arrays]
            + [pl.BlockSpec((stored_rank, chunk), lambda k, m: (0, k))],
            out_specs=pl.BlockSpec((count, rank), lambda k, m: (0, 0)),
            scratch_shapes=[pltpu.VMEM((count, stored_rank), jnp.float32)],
        ),
        out_shape=jax.ShapeDtypeStruct((count, rank), jnp.float32),
        compiler_params=params(),
        cost_estimate=pl.CostEstimate(
            flops=2 * count * stored_rank * width,
            bytes_accessed=2 * stored_rank * width,
            transcendentals=0,
        ),
    )(me, *row_arrays, *row_arrays, table)


def spread_product(shrunk, local, weight, rank):
    count = shrunk.shape[0]
    pair = LANES // rank
    doubled = jnp.concatenate([shrunk] * pair, axis=1)
    lane_block = lax.broadcasted_iota(jnp.int32, (count, LANES), 1) // rank
    spread = jnp.concatenate(
        [
            jnp.where(lane_block + j * pair == local, doubled, 0.0).astype(jnp.bfloat16)
            for j in range(weight.shape[0] // LANES)
        ],
        axis=1,
    )
    return jnp.dot(spread, weight, preferred_element_type=jnp.float32).astype(jnp.bfloat16)


def up_kernel(rank, blocks, me_ref, to_ref, *refs):
    own_refs = refs[:blocks]
    other_refs = refs[blocks : 2 * blocks]
    count_extra = len(refs) - 2 * blocks - 2
    extra_refs = refs[2 * blocks : 2 * blocks + count_extra]
    weight_ref = refs[-2]
    out_ref = refs[-1]
    own = jnp.concatenate([r[...] for r in own_refs], axis=0)
    other = jnp.concatenate([r[...] for r in other_refs], axis=0)
    local = jnp.concatenate([local_column(r[...], me_ref[0]) for r in extra_refs], axis=0)
    shrunk = (own + other).astype(jnp.bfloat16).astype(jnp.float32)
    out_ref[...] = spread_product(shrunk, local, weight_ref[...], rank)


def up_cold(me, own, other, rows, table):
    count, rank = own.shape
    last = (rows.shape[1] - EXTRA) // EXTRA
    return pl.pallas_call(
        functools.partial(up_kernel, rank, 1),
        grid_spec=pltpu.PrefetchScalarGridSpec(
            num_scalar_prefetch=2,
            grid=(1,),
            in_specs=[
                pl.BlockSpec((count, rank), lambda i, m, t: (0, 0)),
                pl.BlockSpec((count, rank), lambda i, m, t: (0, 0)),
                pl.BlockSpec((count, EXTRA), lambda i, m, t: (0, last)),
                pl.BlockSpec(table.shape, lambda i, m, t: (0, 0)),
            ],
            out_specs=pl.BlockSpec((count, table.shape[1]), lambda i, m, t: (0, 0)),
        ),
        out_shape=jax.ShapeDtypeStruct((count, table.shape[1]), jnp.bfloat16),
        compiler_params=params(),
        cost_estimate=pl.CostEstimate(
            flops=2 * count * table.shape[0] * table.shape[1],
            bytes_accessed=2 * table.shape[0] * table.shape[1],
            transcendentals=0,
        ),
    )(me, me, own, other, rows, table)


def up_hot_kernel(rank, sizes, extra_counts, keeps, me_ref, to_ref, *refs):
    groups = len(sizes)
    own_refs = refs[:groups]
    other_refs = refs[groups : 2 * groups]
    extra_refs = refs[2 * groups : 2 * groups + sum(extra_counts)]
    weight_ref, out_ref, buffer, sems = refs[-4:]
    local, at = [], 0
    for n in extra_counts:
        local += [local_column(r[...], me_ref[0]) for r in extra_refs[at : at + n]]
        at += n
    local = jnp.concatenate(local, axis=0)
    own = jnp.concatenate([r[...] for r in own_refs], axis=0)
    other = jnp.concatenate([r[...] for r in other_refs], axis=0)
    shrunk = (own + other).astype(jnp.bfloat16).astype(jnp.float32)
    product = spread_product(shrunk, local, weight_ref[...], rank).astype(jnp.float32)
    blocks, count = buffer.shape[:2]
    copies = []
    for b in range(blocks):
        buffer[b] = product[b * count : (b + 1) * count].astype(jnp.bfloat16)
        copies.append(pltpu.make_async_copy(buffer.at[b], out_ref.at[to_ref[b]], sems.at[b]))
        copies[-1].start()
    for copy in copies:
        copy.wait()


def up_hot(me, targets, owns, others, row_groups, table, count, owners, earlier=None):
    rank = owns[0].shape[1]
    blocks = targets.shape[0]
    arrays = [r for group in row_groups for r in group]
    last = (arrays[0].shape[1] - EXTRA) // EXTRA
    full = [pl.BlockSpec(x.shape, lambda i, m, t: (0, 0)) for x in owns]
    kept = [] if earlier is None else [earlier]
    return pl.pallas_call(
        functools.partial(
            up_hot_kernel, rank, [x.shape[0] for x in owns], [len(g) for g in row_groups], len(kept)
        ),
        grid_spec=pltpu.PrefetchScalarGridSpec(
            num_scalar_prefetch=2,
            grid=(1,),
            in_specs=full
            + full
            + [pl.BlockSpec((r.shape[0], EXTRA), lambda i, m, t: (0, last)) for r in arrays]
            + [pl.BlockSpec(memory_space=pl.ANY) for _ in kept]
            + [pl.BlockSpec(table.shape, lambda i, m, t: (0, 0))],
            out_specs=pl.BlockSpec(memory_space=pl.ANY),
            scratch_shapes=[
                pltpu.VMEM((blocks, count, table.shape[1]), jnp.bfloat16),
                pltpu.SemaphoreType.DMA((blocks,)),
            ],
        ),
        out_shape=jax.ShapeDtypeStruct((owners, count, table.shape[1]), jnp.bfloat16),
        input_output_aliases={2 + 2 * len(owns) + len(arrays): 0} if kept else {},
        compiler_params=params(),
        cost_estimate=pl.CostEstimate(
            flops=2 * blocks * count * table.shape[0] * table.shape[1],
            bytes_accessed=2 * table.shape[0] * table.shape[1],
            transcendentals=0,
        ),
    )(me, targets, *owns, *others, *arrays, *kept, table)


def finish_kernel(
    head, busy_ref, own_ref, other_ref, cold_ref, hot_ref, place_ref, scale_ref, cos_ref, sin_ref, out_ref
):
    count, width = own_ref.shape
    cold_total = cold_ref.shape[0]
    hot_total = hot_ref.shape[1]
    place = place_ref[...]
    from_cold = place == lax.broadcasted_iota(jnp.int32, (count, cold_total), 1)
    from_hot = place - cold_total == lax.broadcasted_iota(jnp.int32, (count, hot_total), 1)
    delta = jnp.dot(
        from_cold.astype(jnp.float32).astype(jnp.bfloat16), cold_ref[...], preferred_element_type=jnp.float32
    ) + jnp.dot(
        from_hot.astype(jnp.float32).astype(jnp.bfloat16), hot_ref[0], preferred_element_type=jnp.float32
    )
    keys = own_ref[...] + other_ref[...] + delta
    cosine = cos_ref[...]
    sine = sin_ref[...]
    for h in range(width // head):
        one = keys[:, h * head : (h + 1) * head]
        normed = (
            one
            * lax.rsqrt(jnp.mean(one * one, axis=-1, keepdims=True) + 1e-06)
            * scale_ref[...]
        )
        turned = pltpu.roll(normed, head // 2, 1)
        out_ref[:, h * head : (h + 1) * head] = (normed * cosine + turned * sine).astype(jnp.bfloat16)


def finish(busy, own, other, cold, hot, place, scale, cosine, sine):
    def full(x):
        return pl.BlockSpec(x.shape, lambda i, b: (0, 0))

    scale = scale.reshape(1, -1)
    return pl.pallas_call(
        functools.partial(finish_kernel, scale.shape[1]),
        grid_spec=pltpu.PrefetchScalarGridSpec(
            num_scalar_prefetch=1,
            grid=(1,),
            in_specs=[
                full(own),
                full(other),
                full(cold),
                pl.BlockSpec((1,) + hot.shape[1:], lambda i, b: (b[0], 0, 0)),
                full(place),
                full(scale),
                full(cosine),
                full(sine),
            ],
            out_specs=full(own),
        ),
        out_shape=jax.ShapeDtypeStruct(own.shape, jnp.bfloat16),
        compiler_params=params(),
    )(busy, own, other, cold, hot, place, scale, cosine, sine)


def after(value, *earlier):
    return lax.optimization_barrier((value,) + earlier)[0]


def rope_tables(head, cached_token_length):
    half = head // 2
    inv_freq = rope_theta ** (-(jnp.arange(half, dtype=jnp.float32) * 2.0) / head)
    angles = cached_token_length.astype(jnp.float32)[:, None] * inv_freq[None, :]
    cosine = jnp.cos(angles)
    sine = jnp.sin(angles)
    return jnp.concatenate([cosine, cosine], axis=1), jnp.concatenate([-sine, sine], axis=1)


def swap(x):
    return lax.ppermute(x, "tensor", [(0, 1), (1, 0)])


def on_device(
    tokens,
    base_key_matrix,
    adapter_down_weight,
    adapter_up_weight,
    key_norm_scale,
    request_adapter,
    adapter_slot_table,
    cached_token_length,
):
    row_count, half_width = tokens.shape
    stored, rank, _ = adapter_down_weight.shape
    owners = lax.axis_size("dp")
    me = lax.axis_index("dp")
    side = lax.axis_index("tensor")
    share = (row_count + owners + 2) // (owners + 3)
    hot_count = HOT_PARTS * share
    down_table = adapter_down_weight.reshape(stored * rank, half_width)
    up_table = adapter_up_weight.reshape(stored * rank, -1)
    features = up_table.shape[1]

    cold_send, hot_send, place, busy = pack(
        request_adapter, adapter_slot_table, tokens, stored, owners, share
    )
    here = me.reshape(1).astype(jnp.int32)

    ring = ring_order(owners)
    to_next = [(ring[i], ring[(i + 1) % owners]) for i in range(owners)]
    to_last = [(b, a) for a, b in to_next]
    distances = [0] + [d for s in range(1, owners // 2) for d in (-s, s)] + [owners // 2]
    sources = [[0] * owners for _ in ring]
    for spot, index in enumerate(ring):
        sources[index] = [ring[(spot + d) % owners] for d in distances]
    order = lax.dynamic_index_in_dim(jnp.array(sources, jnp.int32), me, 0, keepdims=False)

    cut = hot_count // 2 // 8 * 8 if hot_count >= 16 else hot_count // 2
    half_way = owners // 2
    forward = lax.ppermute(hot_send, "dp", to_next)
    backward = lax.ppermute(hot_send, "dp", to_last)
    got = lax.all_to_all(
        cold_send.reshape(owners, share, half_width + EXTRA), "dp", split_axis=0, concat_axis=0, tiled=True
    ).reshape(owners * share, half_width + EXTRA)

    base = jnp.dot(tokens, base_key_matrix, preferred_element_type=jnp.float32)
    base_own = lax.dynamic_slice_in_dim(base, side * features, features, 1)
    base_other = swap(lax.dynamic_slice_in_dim(base, (1 - side) * features, features, 1))
    cosine, sine = rope_tables(key_norm_scale.shape[0], cached_token_length)

    row_groups = [[hot_send]]
    part = down(here, [hot_send], down_table, rank)
    parts, others = [part], [swap(part)]
    todo = [part, base]
    for step in range(1, half_way):
        forward, backward, *_ = lax.optimization_barrier((forward, backward, *todo))
        group = [forward, backward]
        if step < half_way - 1:
            forward = lax.ppermute(forward, "dp", to_next)
            backward = lax.ppermute(backward, "dp", to_last)
        else:
            last_front = lax.ppermute(forward[:cut], "dp", to_next)
            last_rear = lax.ppermute(backward[cut:], "dp", to_last)
        row_groups.append(group)
        part = down(here, group, down_table, rank)
        parts.append(part)
        others.append(swap(part))
        todo = [part]
        if step == max(half_way - 2, 1):
            cold_part = down(here, [got], down_table, rank)
            cold_delta = up_cold(here, cold_part, swap(cold_part), got, up_table)
            cold_back = lax.all_to_all(
                cold_delta.reshape(owners, share, features), "dp", split_axis=0, concat_axis=0, tiled=True
            ).reshape(owners * share, features)
            todo += [cold_delta]

    hot_delta = up_hot(
        here, order[: owners - 1], parts, others, row_groups, up_table, hot_count, owners
    )
    last_front, last_rear, hot_delta, cold_back = lax.optimization_barrier(
        (last_front, last_rear, hot_delta, cold_back)
    )
    group = [last_front, last_rear]
    part = down(here, group, down_table, rank)
    hot_delta = up_hot(
        here,
        order[owners - 1 :],
        [part],
        [swap(part)],
        [group],
        up_table,
        hot_count,
        owners,
        hot_delta,
    )
    hot_back = lax.all_to_all(hot_delta, "dp", split_axis=0, concat_axis=0, tiled=True)
    return finish(
        busy.reshape(1), base_own, base_other, cold_back, hot_back, place, key_norm_scale, cosine, sine
    )


def solution(mesh):
    placed = (
        P(("groups", "dp"), "tensor"),
        P("tensor", None),
        P(("groups", "dp"), None, "tensor"),
        P(("groups", "dp"), None, "tensor"),
        P(),
        P(("groups", "dp")),
        P("groups"),
        P(("groups", "dp")),
    )
    return jax.shard_map(
        on_device,
        mesh=mesh,
        in_specs=placed,
        out_specs=P(("groups", "dp"), "tensor"),
        check_vma=False,
    )
```

time: 151 us -> 137 us (0.907)
  Pallas kernels: 35.8 us -> 54.5 us
  local copies, waits for them, and re-layouts: 28.2 us -> 10.6 us
  waiting for transfers between devices: 41 us -> 32.5 us
  between operations: 6.01 us -> 0.18 us
  other arithmetic: 4.86 us -> 1.41 us
    ppermute x3 -> x2, waiting for transfers between devices: 29.4 us -> 0.58 us  [on_device(): forward = lax.ppermute(forward, 'dp', to_next)]
    pallas_call x9 -> x10, Pallas kernels: 33.8 us -> 51.2 us  [the longest x6 38.3 us: down(): pl.pallas_call(functools.partial(down_kernel, rank, parts), grid_spec=plt...]
    ppermute x0 -> x2, waiting for transfers between devices: none -> 13.7 us  [the longest x1 13.7 us: on_device(): backward = lax.ppermute(hot_send, 'dp', to_last)]
    unnamed x40 -> x42, local copies, waits for them, and re-layouts: 16.7 us -> 5.95 us
    all_to_all x1, waiting for transfers between devices: 2.76 us -> 13.4 us  [on_device(): lax.all_to_all(hot_delta, 'dp', split_axis=0, concat_axis=0, tiled=True)]
    all_to_all x1, waiting for transfers between devices: 6.33 us -> 0.01 us  [on_device(): lax.all_to_all(cold_delta.reshape(owners, share, features), 'dp', split_a...]
    another operation x12 -> x0, local copies, waits for them, and re-layouts: 3.83 us -> none  [the longest x1 1.65 us: source(): return jnp.take(ring_array, (my_spot + distance) % owners)]
    ppermute x3 -> x2, starting transfers between devices: 11.5 us -> 8.6 us  [on_device(): forward = lax.ppermute(forward, 'dp', to_next)]
  transfers between devices with their start and end apart: 14 -> 18, of which waited for: 6 -> 7; matrix products, arithmetic and copies ran while one was open for 14% -> 8% of each run, Pallas kernels for 17% -> 28%
where the time goes in v2:
time: 137 us; the launch traced here: 136 us
  Pallas kernels  54.5 us (40%)
  waiting for transfers between devices  32.5 us (24%)
  starting transfers between devices  31.3 us (23%)
  local copies, waits for them, and re-layouts  10.6 us (8%)
  matrix products  5.41 us (4%)
  other arithmetic  1.41 us (1%)
    pallas_call x6, Pallas kernels, down(): pl.pallas_call(functools.partial(down_kernel, rank, parts), grid_spec=plt...  38.3 us
    ppermute x1, waiting for transfers between devices, on_device(): backward = lax.ppermute(hot_send, 'dp', to_last)  13.7 us
    all_to_all x1, waiting for transfers between devices, on_device(): lax.all_to_all(hot_delta, 'dp', split_axis=0, concat_axis=0, tiled=True)  13.4 us
    ppermute x2, starting transfers between devices, on_device(): forward = lax.ppermute(forward, 'dp', to_next)  8.6 us
    all_to_all x1, starting transfers between devices, on_device(): lax.all_to_all(cold_send.reshape(owners, share, half_width + EXTRA), 'dp'...  7.26 us
    pallas_call x2, Pallas kernels, up_hot(): pl.pallas_call(functools.partial(up_hot_kernel, rank, [x.shape[0] for x i...  6.99 us
    unnamed x42, local copies, waits for them, and re-layouts  5.95 us
    dot_general x1, matrix products, on_device(): base = jnp.dot(tokens, base_key_matrix, preferred_element_type=jnp.float32)  5.41 us
  transfers between devices with their start and end apart: 18, of which 7 were waited for; matrix products, arithmetic and copies ran while one was open for 8% of the time, Pallas kernels for 28%

profile of v2, /device:TPU:0, one launch (start us, length us, event | category | flops | bytes accessed | tf_op | source)
XLA Modules:
  0.0 135.9 jit_solution(5816750256282532948)
XLA Ops:
  0.0 3.3 %shard_map.91 = (bf16[192,2688]{1,0:T(8,128)(2,1)}, bf16[72,2688]{1,0:T(8,128)(2,1)}, s32[256,1]{1,0:T(8,128)}, s32[1,1]{1,0:T(1,128)}) custom-call(s32[1,256]{1,0:T(1,128)} %bitcast.31, s32[1,128]{1,0:T(1,128)} %bitcast.32, bf16[256,2560]{1,0:T(8,128)(2,1)} %tokens_ref.1), custom_call_target="tpu_custom_call" | custom-call | tf_op jit(solution)/shard_map/pallas_call | solution.py:79
  3.3 7.3 %all-to-all-start = ((bf16[8,24,2688]{2,1,0:T(8,128)(2,1)}), bf16[8,24,2688]{2,1,0:T(8,128)(2,1)S(1)}, u32[]{:S(2)}, u32[]{:S(2)}) async-start(bf16[8,24,2688]{2,1,0:T(8,128)(2,1)} %bitcast.28), calls=%async_computation | async-start | bytes 2064384 | tf_op jit(solution)/shard_map/all_to_all | solution.py:388
  10.6 2.0 %collective-permute-start.2 = (bf16[72,2688]{1,0:T(8,128)(2,1)}, bf16[72,2688]{1,0:T(8,128)(2,1)S(1)}, u32[]{:S(2)}, u32[]{:S(2)}) collective-permute-start(bf16[72,2688]{1,0:T(8,128)(2,1)} %get-tuple-element.20.refs_0_.refs_1_.refs_8_), channel_id=1, source_target_pairs={{4,0},{8,4},{12,8},{14,12},{10,14},{6,10},{2,6},{0,2},{5,1},{9,5},... | collective-permute-start | bytes 1161224 | tf_op jit(solution)/shard_map/ppermute | solution.py:387
  12.6 6.1 %shard_map.92.refs_0_ = f32[72,64]{1,0:T(8,128)} custom-call(s32[1]{0:T(128)} %bitcast.3.me_ref.to_ref, bf16[72,2688]{1,0:T(8,128)(2,1)} %get-tuple-element.20.refs_0_.refs_1_.refs_8_, bf16[72,2688]{1,0:T(8,128)(2,1)} %get-tuple-element.20.refs_0_.refs_1_.refs_8_, bf16[1024,2560]{1,0:T(8,128)(2,1)} %bitcast.16), custom_call_target="tpu_custom_call" | custom-call | flops 377487360 | bytes 5242880 | tf_op jit(solution)/shard_map/pallas_call | solution.py:140
  18.7 5.4 %fusion.1 = f32[256,1024]{1,0:T(8,128)} fusion(bf16[256,2560]{1,0:T(8,128)(2,1)} %tokens_ref.1, bf16[2560,1024]{1,0:T(8,128)(2,1)} %param.10), kind=kOutput, calls=%fused_computation.10 | convolution fusion | flops 1342177280 | bytes 7602176 | tf_op jit(solution)/shard_map/dot_general | solution.py:392
  24.1 13.7 %collective-permute-done.2.refs_1_.refs_3_.refs_10_ = bf16[72,2688]{1,0:T(8,128)(2,1)S(1)} collective-permute-done((bf16[72,2688]{1,0:T(8,128)(2,1)}, bf16[72,2688]{1,0:T(8,128)(2,1)S(1)}, u32[]{:S(2)}, u32[]{:S(2)}) %collective-permute-start.2) | collective-permute-done | bytes 387104 | tf_op jit(solution)/shard_map/ppermute | solution.py:387
  37.9 7.1 %collective-permute-start.3 = (bf16[72,2688]{1,0:T(8,128)(2,1)S(1)}, bf16[72,2688]{1,0:T(8,128)(2,1)S(1)}, u32[]{:S(2)}, u32[]{:S(2)}) collective-permute-start(bf16[72,2688]{1,0:T(8,128)(2,1)S(1)} %collective-permute-done.1.refs_0_.refs_2_.refs_9_), channel_id=1, source_target_pairs={{0,4},{4,8},{8,12},{12,14},{14,10},{10,6},{6,2},{2,0},{1,5},{5,9},... | collective-permute-start | bytes 1161224 | tf_op jit(solution)/shard_map/ppermute | solution.py:405
  45.0 6.5 %shard_map.93.refs_1_ = f32[144,64]{1,0:T(8,128)} custom-call(s32[1]{0:T(128)} %bitcast.3.me_ref.to_ref, bf16[72,2688]{1,0:T(8,128)(2,1)} %copy-done.4, bf16[72,2688]{1,0:T(8,128)(2,1)} %copy-done.3, bf16[72,2688]{1,0:T(8,128)(2,1)} %copy-done.4, bf16[72,2688]{1,0:T(8,128)(2,1)} %copy-done.3, bf16[1024,2560]{1,0:T(8,128)(2,1)} %bitcast.17), custom_call_target="tpu_custom_call" | custom-call | flops 754974720 | bytes 5242880 | tf_op jit(solution)/shard_map/pallas_call | solution.py:140
  52.0 2.2 %collective-permute-done.4.refs_1_.refs_3_.refs_12_ = bf16[72,2688]{1,0:T(8,128)(2,1)S(1)} collective-permute-done((bf16[72,2688]{1,0:T(8,128)(2,1)S(1)}, bf16[72,2688]{1,0:T(8,128)(2,1)S(1)}, u32[]{:S(2)}, u32[]{:S(2)}) %collective-permute-start.4) | collective-permute-done | bytes 387104 | tf_op jit(solution)/shard_map/ppermute | solution.py:406
  54.2 1.5 %collective-permute-start.5 = (bf16[72,2688]{1,0:T(8,128)(2,1)S(1)}, bf16[72,2688]{1,0:T(8,128)(2,1)S(1)}, u32[]{:S(2)}, u32[]{:S(2)}) collective-permute-start(bf16[72,2688]{1,0:T(8,128)(2,1)S(1)} %collective-permute-done.3.refs_0_.refs_2_.refs_11_), channel_id=1, source_target_pairs={{0,4},{4,8},{8,12},{12,14},{14,10},{10,6},{6,2},{2,0},{1,5},{5,9},... | collective-permute-start | bytes 1161224 | tf_op jit(solution)/shard_map/ppermute | solution.py:405
  57.5 1.0 copy-done
  58.5 6.6 %shard_map.95.refs_0_ = f32[192,64]{1,0:T(8,128)} custom-call(s32[1]{0:T(128)} %bitcast.3.me_ref.to_ref, bf16[192,2688]{1,0:T(8,128)(2,1)} %bitcast.22, bf16[192,2688]{1,0:T(8,128)(2,1)} %bitcast.23, bf16[1024,2560]{1,0:T(8,128)(2,1)} %bitcast.18), custom_call_target="tpu_custom_call" | custom-call | flops 1006632960 | bytes 5242880 | tf_op jit(solution)/shard_map/pallas_call | solution.py:140
  65.1 6.5 %shard_map.94.refs_2_ = f32[144,64]{1,0:T(8,128)} custom-call(s32[1]{0:T(128)} %bitcast.3.me_ref.to_ref, bf16[72,2688]{1,0:T(8,128)(2,1)} %copy-done.5, bf16[72,2688]{1,0:T(8,128)(2,1)} %copy-done.6, bf16[72,2688]{1,0:T(8,128)(2,1)} %copy-done.5, bf16[72,2688]{1,0:T(8,128)(2,1)} %copy-done.6, bf16[1024,2560]{1,0:T(8,128)(2,1)} %bitcast.19), custom_call_target="tpu_custom_call" | custom-call | flops 754974720 | bytes 5242880 | tf_op jit(solution)/shard_map/pallas_call | solution.py:140
  72.2 2.6 %shard_map.96 = bf16[192,512]{1,0:T(8,128)(2,1)} custom-call(s32[1]{0:T(128)} %bitcast.3.me_ref.to_ref, s32[1]{0:T(128)} %bitcast.3.me_ref.to_ref, f32[192,64]{1,0:T(8,128)} %shard_map.95.refs_0_, f32[192,64]{1,0:T(8,128)} %copy-done.14, bf16[192,2688]{1,0:T(8,128)(2,1)} %bitcast.24, bf16[1024,512]{1,0:T(8,128)(2,1)} %bitcast.25), custom_call_target="tpu_custom_call" | custom-call | flops 201326592 | bytes 1048576 | tf_op jit(solution)/shard_map/pallas_call | solution.py:193
  74.8 4.9 %all-to-all-start.1 = ((bf16[8,24,512]{2,1,0:T(8,128)(2,1)}), bf16[8,24,512]{2,1,0:T(8,128)(2,1)S(1)}, u32[]{:S(2)}, u32[]{:S(2)}) async-start(bf16[8,24,512]{2,1,0:T(8,128)(2,1)} %bitcast.30), calls=%async_computation.1 | async-start | bytes 393216 | tf_op jit(solution)/shard_map/all_to_all | solution.py:418
  81.2 6.5 %shard_map.97.refs_3_ = f32[144,64]{1,0:T(8,128)} custom-call(s32[1]{0:T(128)} %bitcast.3.me_ref.to_ref, bf16[72,2688]{1,0:T(8,128)(2,1)} %copy-done.2, bf16[72,2688]{1,0:T(8,128)(2,1)} %copy-done.1, bf16[72,2688]{1,0:T(8,128)(2,1)} %copy-done.2, bf16[72,2688]{1,0:T(8,128)(2,1)} %copy-done.1, bf16[1024,2560]{1,0:T(8,128)(2,1)} %bitcast.20), custom_call_target="tpu_custom_call" | custom-call | flops 754974720 | bytes 5242880 | tf_op jit(solution)/shard_map/pallas_call | solution.py:140
  89.9 1.9 %collective-permute-start.8 = (bf16[32,2688]{1,0:T(8,128)(2,1)S(1)}, bf16[32,2688]{1,0:T(8,128)(2,1)S(1)}, u32[]{:S(2)}, u32[]{:S(2)}) collective-permute-start(bf16[32,2688]{1,0:T(8,128)(2,1)S(1)} %slice.18), channel_id=1, source_target_pairs={{0,4},{4,8},{8,12},{12,14},{14,10},{10,6},{6,2},{2,0},{1,5},{5,9},... | collective-permute-start | bytes 516104 | tf_op jit(solution)/shard_map/ppermute | solution.py:408
  93.7 4.0 %shard_map.98.refs_4_ = bf16[8,72,512]{2,1,0:T(8,128)(2,1)} custom-call(s32[1]{0:T(128)} %bitcast.3.me_ref.to_ref, s32[7]{0:T(128)} %slice_bitcast_fusion.to_ref, f32[72,64]{1,0:T(8,128)} %shard_map.92.refs_0_, f32[144,64]{1,0:T(8,128)} %shard_map.93.refs_1_, f32[144,64]{1,0:T(8,128)} %shard_map.94.refs_2_, f32[144,64]{1,0:T(8,128)} %shard_map.97.refs_3_, ...), custom_call_target="tpu_custom_call" | custom-call | flops 528482304 | bytes 1048576 | tf_op jit(solution)/shard_map/pallas_call | solution.py:248
  97.7 1.4 %collective-permute-done.9.refs_1_.refs_3_ = bf16[40,2688]{1,0:T(8,128)(2,1)S(1)} collective-permute-done((bf16[40,2688]{1,0:T(8,128)(2,1)S(1)}, bf16[40,2688]{1,0:T(8,128)(2,1)S(1)}, u32[]{:S(2)}, u32[]{:S(2)}) %collective-permute-start.9) | collective-permute-done | bytes 215072 | tf_op jit(solution)/shard_map/ppermute | solution.py:409
  99.8 6.1 %shard_map.99.refs_0_ = f32[72,64]{1,0:T(8,128)} custom-call(s32[1]{0:T(128)} %bitcast.3.me_ref.to_ref, bf16[32,2688]{1,0:T(8,128)(2,1)} %copy-done.9, bf16[40,2688]{1,0:T(8,128)(2,1)} %copy-done.8, bf16[32,2688]{1,0:T(8,128)(2,1)} %copy-done.9, bf16[40,2688]{1,0:T(8,128)(2,1)} %copy-done.8, bf16[1024,2560]{1,0:T(8,128)(2,1)} %bitcast.21), custom_call_target="tpu_custom_call" | custom-call | flops 377487360 | bytes 5242880 | tf_op jit(solution)/shard_map/pallas_call | solution.py:140
  107.9 3.0 %shard_map.100 = bf16[8,72,512]{2,1,0:T(8,128)(2,1)} custom-call(s32[1]{0:T(128)} %bitcast.3.me_ref.to_ref, s32[1]{0:T(128)} %bitcast.11.to_ref, f32[72,64]{1,0:T(8,128)} %shard_map.99.refs_0_, f32[72,64]{1,0:T(8,128)} %copy-done.18, bf16[32,2688]{1,0:T(8,128)(2,1)} %copy-done.9, bf16[40,2688]{1,0:T(8,128)(2,1)} %copy-done.8, ...), custom_call_target="tpu_custom_call", output_to_operand_aliasing={{}: (6, {})} | custom-call | flops 75497472 | bytes 1048576 | tf_op jit(solution)/shard_map/pallas_call | solution.py:248
  111.0 4.6 %all-to-all-start.2 = ((bf16[8,72,512]{2,1,0:T(8,128)(2,1)}), bf16[8,72,512]{2,1,0:T(8,128)(2,1)S(1)}, u32[]{:S(2)}, u32[]{:S(2)}) async-start(bf16[8,72,512]{2,1,0:T(8,128)(2,1)} %shard_map.100), calls=%async_computation.2 | async-start | bytes 1179648 | tf_op jit(solution)/shard_map/all_to_all | solution.py:442
  118.4 13.4 %all-to-all-done.2.hot_ref = bf16[8,72,512]{2,1,0:T(8,128)(2,1)S(1)} async-done(((bf16[8,72,512]{2,1,0:T(8,128)(2,1)}), bf16[8,72,512]{2,1,0:T(8,128)(2,1)S(1)}, u32[]{:S(2)}, u32[]{:S(2)}) %all-to-all-start.2) | async-done | bytes 589856 | tf_op jit(solution)/shard_map/all_to_all | solution.py:442
  132.6 3.3 %shard_map.101 = bf16[256,512]{1,0:T(8,128)(2,1)} custom-call(s32[1]{0:T(128)} %bitcast.2.busy_ref, f32[256,512]{1,0:T(8,128)} %get-tuple-element.34.own_ref, f32[256,512]{1,0:T(8,128)} %copy-done.12, bf16[192,512]{1,0:T(8,128)(2,1)} %bitcast.29, bf16[8,72,512]{2,1,0:T(8,128)(2,1)} %copy-done.7, s32[256,1]{1,0:T(8,128)} %get-tuple-element.32.place_ref, ...), custom_call_target="tpu_custom_call" | custom-call | tf_op jit(solution)/shard_map/pallas_call | solution.py:310
  (76 shorter events, 15.0 us)
Async XLA Ops:
  3.3 54.2 %all-to-all-start = ((bf16[8,24,2688]{2,1,0:T(8,128)(2,1)}), bf16[8,24,2688]{2,1,0:T(8,128)(2,1)S(1)}, u32[]{:S(2)}, u32[]{:S(2)}) async-start(bf16[8,24,2688]{2,1,0:T(8,128)(2,1)} %bitcast.28), calls=%async_computation | async-start | bytes 2064384 | tf_op jit(solution)/shard_map/all_to_all | solution.py:388
  10.6 27.3 %collective-permute-start.2 = (bf16[72,2688]{1,0:T(8,128)(2,1)}, bf16[72,2688]{1,0:T(8,128)(2,1)S(1)}, u32[]{:S(2)}, u32[]{:S(2)}) collective-permute-start(bf16[72,2688]{1,0:T(8,128)(2,1)} %get-tuple-element.20.refs_0_.refs_1_.refs_8_), channel_id=1, source_target_pairs={{4,0},{8,4},{12,8},{14,12},{10,14},{6,10},{2,6},{0,2},{5,1},{9,5},... | collective-permute-start | bytes 1161224 | tf_op jit(solution)/shard_map/ppermute | solution.py:387
  12.6 25.3 %collective-permute-start.1 = (bf16[72,2688]{1,0:T(8,128)(2,1)}, bf16[72,2688]{1,0:T(8,128)(2,1)S(1)}, u32[]{:S(2)}, u32[]{:S(2)}) collective-permute-start(bf16[72,2688]{1,0:T(8,128)(2,1)} %get-tuple-element.20.refs_0_.refs_1_.refs_8_), channel_id=1, source_target_pairs={{0,4},{4,8},{8,12},{12,14},{14,10},{10,6},{6,2},{2,0},{1,5},{5,9},... | collective-permute-start | bytes 1161224 | tf_op jit(solution)/shard_map/ppermute | solution.py:386
  24.1 32.2 %copy-start.13 = (f32[72,64]{1,0:T(8,128)S(1)}, f32[72,64]{1,0:T(8,128)}, u32[]{:S(2)}) copy-start(f32[72,64]{1,0:T(8,128)} %shard_map.92.refs_0_) | copy-start | bytes 55300
  37.9 14.2 %collective-permute-start.3 = (bf16[72,2688]{1,0:T(8,128)(2,1)S(1)}, bf16[72,2688]{1,0:T(8,128)(2,1)S(1)}, u32[]{:S(2)}, u32[]{:S(2)}) collective-permute-start(bf16[72,2688]{1,0:T(8,128)(2,1)S(1)} %collective-permute-done.1.refs_0_.refs_2_.refs_9_), channel_id=1, source_target_pairs={{0,4},{4,8},{8,12},{12,14},{14,10},{10,6},{6,2},{2,0},{1,5},{5,9},... | collective-permute-start | bytes 1161224 | tf_op jit(solution)/shard_map/ppermute | solution.py:405
  44.9 9.3 %collective-permute-start.4 = (bf16[72,2688]{1,0:T(8,128)(2,1)S(1)}, bf16[72,2688]{1,0:T(8,128)(2,1)S(1)}, u32[]{:S(2)}, u32[]{:S(2)}) collective-permute-start(bf16[72,2688]{1,0:T(8,128)(2,1)S(1)} %collective-permute-done.2.refs_1_.refs_3_.refs_10_), channel_id=1, source_target_pairs={{4,0},{8,4},{12,8},{14,12},{10,14},{6,10},{2,6},{0,2},{5,1},{9,5},... | collective-permute-start | bytes 1161224 | tf_op jit(solution)/shard_map/ppermute | solution.py:406
  52.0 13.0 %copy-start.5 = (bf16[72,2688]{1,0:T(8,128)(2,1)}, bf16[72,2688]{1,0:T(8,128)(2,1)S(1)}, u32[]{:S(2)}) copy-start(bf16[72,2688]{1,0:T(8,128)(2,1)S(1)} %collective-permute-done.3.refs_0_.refs_2_.refs_11_) | copy-start | bytes 1161220
  54.2 25.5 %collective-permute-start.5 = (bf16[72,2688]{1,0:T(8,128)(2,1)S(1)}, bf16[72,2688]{1,0:T(8,128)(2,1)S(1)}, u32[]{:S(2)}, u32[]{:S(2)}) collective-permute-start(bf16[72,2688]{1,0:T(8,128)(2,1)S(1)} %collective-permute-done.3.refs_0_.refs_2_.refs_11_), channel_id=1, source_target_pairs={{0,4},{4,8},{8,12},{12,14},{14,10},{10,6},{6,2},{2,0},{1,5},{5,9},... | collective-permute-start | bytes 1161224 | tf_op jit(solution)/shard_map/ppermute | solution.py:405
  55.8 24.0 %collective-permute-start.6 = (bf16[72,2688]{1,0:T(8,128)(2,1)S(1)}, bf16[72,2688]{1,0:T(8,128)(2,1)S(1)}, u32[]{:S(2)}, u32[]{:S(2)}) collective-permute-start(bf16[72,2688]{1,0:T(8,128)(2,1)S(1)} %collective-permute-done.4.refs_1_.refs_3_.refs_12_), channel_id=1, source_target_pairs={{4,0},{8,4},{12,8},{14,12},{10,14},{6,10},{2,6},{0,2},{5,1},{9,5},... | collective-permute-start | bytes 1161224 | tf_op jit(solution)/shard_map/ppermute | solution.py:406
  56.3 35.5 %collective-permute-start.10 = (f32[72,64]{1,0:T(8,128)S(1)}, f32[72,64]{1,0:T(8,128)S(1)}, u32[]{:S(2)}, u32[]{:S(2)}) collective-permute-start(f32[72,64]{1,0:T(8,128)S(1)} %copy-done.13), channel_id=1, source_target_pairs={{0,1},{1,0},{2,3},{3,2},{4,5},{5,4},{6,7},{7,6},{8,9},{9,8},{10,11... | collective-permute-start | bytes 55304 | tf_op jit(solution)/shard_map/ppermute | solution.py:346
  57.0 35.5 %collective-permute-start.11 = (f32[144,64]{1,0:T(8,128)}, f32[144,64]{1,0:T(8,128)S(1)}, u32[]{:S(2)}, u32[]{:S(2)}) collective-permute-start(f32[144,64]{1,0:T(8,128)} %shard_map.93.refs_1_), channel_id=1, source_target_pairs={{0,1},{1,0},{2,3},{3,2},{4,5},{5,4},{6,7},{7,6},{8,9},{9,8},{10,11... | collective-permute-start | bytes 110600 | tf_op jit(solution)/shard_map/ppermute | solution.py:346
  65.1 6.5 %collective-permute-start.7 = (f32[192,64]{1,0:T(8,128)}, f32[192,64]{1,0:T(8,128)S(1)}, u32[]{:S(2)}, u32[]{:S(2)}) collective-permute-start(f32[192,64]{1,0:T(8,128)} %shard_map.95.refs_0_), channel_id=1, source_target_pairs={{0,1},{1,0},{2,3},{3,2},{4,5},{5,4},{6,7},{7,6},{8,9},{9,8},{10,11... | collective-permute-start | bytes 147464 | tf_op jit(solution)/shard_map/ppermute | solution.py:346
  71.6 20.9 %collective-permute-start.12 = (f32[144,64]{1,0:T(8,128)}, f32[144,64]{1,0:T(8,128)S(1)}, u32[]{:S(2)}, u32[]{:S(2)}) collective-permute-start(f32[144,64]{1,0:T(8,128)} %shard_map.94.refs_2_), channel_id=1, source_target_pairs={{0,1},{1,0},{2,3},{3,2},{4,5},{5,4},{6,7},{7,6},{8,9},{9,8},{10,11... | collective-permute-start | bytes 110600 | tf_op jit(solution)/shard_map/ppermute | solution.py:346
  74.8 24.3 %all-to-all-start.1 = ((bf16[8,24,512]{2,1,0:T(8,128)(2,1)}), bf16[8,24,512]{2,1,0:T(8,128)(2,1)S(1)}, u32[]{:S(2)}, u32[]{:S(2)}) async-start(bf16[8,24,512]{2,1,0:T(8,128)(2,1)} %bitcast.30), calls=%async_computation.1 | async-start | bytes 393216 | tf_op jit(solution)/shard_map/all_to_all | solution.py:418
  89.6 2.9 %collective-permute-start.13 = (f32[144,64]{1,0:T(8,128)}, f32[144,64]{1,0:T(8,128)S(1)}, u32[]{:S(2)}, u32[]{:S(2)}) collective-permute-start(f32[144,64]{1,0:T(8,128)} %shard_map.97.refs_3_), channel_id=1, source_target_pairs={{0,1},{1,0},{2,3},{3,2},{4,5},{5,4},{6,7},{7,6},{8,9},{9,8},{10,11... | collective-permute-start | bytes 110600 | tf_op jit(solution)/shard_map/ppermute | solution.py:346
  89.9 7.9 %collective-permute-start.8 = (bf16[32,2688]{1,0:T(8,128)(2,1)S(1)}, bf16[32,2688]{1,0:T(8,128)(2,1)S(1)}, u32[]{:S(2)}, u32[]{:S(2)}) collective-permute-start(bf16[32,2688]{1,0:T(8,128)(2,1)S(1)} %slice.18), channel_id=1, source_target_pairs={{0,4},{4,8},{8,12},{12,14},{14,10},{10,6},{6,2},{2,0},{1,5},{5,9},... | collective-permute-start | bytes 516104 | tf_op jit(solution)/shard_map/ppermute | solution.py:408
  91.7 7.4 %collective-permute-start.9 = (bf16[40,2688]{1,0:T(8,128)(2,1)S(1)}, bf16[40,2688]{1,0:T(8,128)(2,1)S(1)}, u32[]{:S(2)}, u32[]{:S(2)}) collective-permute-start(bf16[40,2688]{1,0:T(8,128)(2,1)S(1)} %slice.19), channel_id=1, source_target_pairs={{4,0},{8,4},{12,8},{14,12},{10,14},{6,10},{2,6},{0,2},{5,1},{9,5},... | collective-permute-start | bytes 645128 | tf_op jit(solution)/shard_map/ppermute | solution.py:409
  97.7 17.8 %copy-start.10 = (f32[256,1024]{1,0:T(8,128)S(1)}, f32[256,1024]{1,0:T(8,128)}, u32[]{:S(2)}) copy-start(f32[256,1024]{1,0:T(8,128)} %fusion.1) | copy-start | bytes 3145732
  99.1 17.3 %copy-start.11 = (bf16[8,24,512]{2,1,0:T(8,128)(2,1)}, bf16[8,24,512]{2,1,0:T(8,128)(2,1)S(1)}, u32[]{:S(2)}) copy-start(bf16[8,24,512]{2,1,0:T(8,128)(2,1)S(1)} %all-to-all-done.1) | copy-start | bytes 589828
  99.8 16.7 %copy-start.20 = (s32[256]{0:T(256)S(1)}, s32[256]{0:T(256)}, u32[]{:S(2)}) copy-start(s32[256]{0:T(256)} %param.16) | copy-start | bytes 3076
  105.9 1.4 %collective-permute-start.14 = (f32[72,64]{1,0:T(8,128)}, f32[72,64]{1,0:T(8,128)S(1)}, u32[]{:S(2)}, u32[]{:S(2)}) collective-permute-start(f32[72,64]{1,0:T(8,128)} %shard_map.99.refs_0_), channel_id=1, source_target_pairs={{0,1},{1,0},{2,3},{3,2},{4,5},{5,4},{6,7},{7,6},{8,9},{9,8},{10,11... | collective-permute-start | bytes 55304 | tf_op jit(solution)/shard_map/ppermute | solution.py:346
  111.0 20.8 %all-to-all-start.2 = ((bf16[8,72,512]{2,1,0:T(8,128)(2,1)}), bf16[8,72,512]{2,1,0:T(8,128)(2,1)S(1)}, u32[]{:S(2)}, u32[]{:S(2)}) async-start(bf16[8,72,512]{2,1,0:T(8,128)(2,1)} %shard_map.100), calls=%async_computation.2 | async-start | bytes 1179648 | tf_op jit(solution)/shard_map/all_to_all | solution.py:442
  116.5 1.9 %collective-permute-start = (f32[256,512]{1,0:T(8,128)S(1)}, f32[256,512]{1,0:T(8,128)S(1)}, u32[]{:S(2)}, u32[]{:S(2)}) collective-permute-start(f32[256,512]{1,0:T(8,128)S(1)} %get-tuple-element.33), channel_id=1, source_target_pairs={{0,1},{1,0},{2,3},{3,2},{4,5},{5,4},{6,7},{7,6},{8,9},{9,8},{10,11... | collective-permute-start | bytes 1572872 | tf_op jit(solution)/shard_map/ppermute | solution.py:346
  118.4 13.4 %copy-start.12 = (f32[256,512]{1,0:T(8,128)}, f32[256,512]{1,0:T(8,128)S(1)}, u32[]{:S(2)}) copy-start(f32[256,512]{1,0:T(8,128)S(1)} %collective-permute-done.other_ref) | copy-start | bytes 1572868
  (15 other events, 34.3 us)

commit v3 on v2

v3 whole, which is shorter than its diff:
```python
import functools

import jax
import jax.numpy as jnp
from jax import lax
from jax.experimental import pallas as pl
from jax.experimental.pallas import tpu as pltpu
from jax.sharding import PartitionSpec as P

rope_theta = 1000000.0
LANES = 128
EXTRA = 128
HOT_PARTS = 3
ALL_VMEM = 60 * 1024 * 1024
SOME_VMEM = 16 * 1024 * 1024


def whole():
    return pl.BlockSpec(memory_space=pltpu.VMEM)


def scalars():
    return pl.BlockSpec(memory_space=pltpu.SMEM)


def params(limit=SOME_VMEM):
    return pltpu.CompilerParams(vmem_limit_bytes=limit)


def ring_order(owners):
    return [i for i in range(0, owners, 2)] + [i for i in range(owners - 1, 0, -2)]


def to_column(row):
    count = row.shape[1]
    square = lax.broadcasted_iota(jnp.int32, (count, count), 0) == lax.broadcasted_iota(
        jnp.int32, (count, count), 1
    )
    return jnp.sum(jnp.where(square, row, 0), axis=1, keepdims=True)


def pack_kernel(
    stored, owners, share, pieces, request_ref, table_ref, tokens_ref, cold_ref, *refs
):
    hot_refs, (place_ref, busy_ref) = refs[: len(pieces)], refs[len(pieces) :]
    count = request_ref.shape[1]
    width = tokens_ref.shape[1]
    request_col = to_column(request_ref[...])
    adapters = table_ref.shape[1]
    match = request_col == lax.broadcasted_iota(jnp.int32, (count, adapters), 1)
    slot_col = jnp.sum(jnp.where(match, table_ref[...], 0), axis=1, keepdims=True)
    row_id = lax.broadcasted_iota(jnp.int32, (count, count), 0)
    col_id = lax.broadcasted_iota(jnp.int32, (count, count), 1)
    slot_row = jnp.sum(jnp.where(row_id == col_id, slot_col, 0), axis=0, keepdims=True)
    owner_col = slot_col // stored
    owner_row = slot_row // stored
    same = owner_col == owner_row
    rank_col = jnp.sum(jnp.where(same & (col_id < row_id), 1, 0), axis=1, keepdims=True)
    rank_row = jnp.sum(jnp.where(same & (row_id < col_id), 1, 0), axis=0, keepdims=True)
    cold_total = owners * share

    def place(owner, rank):
        return jnp.where(rank < share, owner * share + rank, cold_total + rank - share)

    place_ref[...] = place(owner_col, rank_col)
    busy_ref[...] = jnp.max(jnp.where(rank_row >= share, owner_row, 0), axis=1, keepdims=True)
    place_row = place(owner_row, rank_row)
    local_row = slot_row - owner_row * stored
    tokens = tokens_ref[...]
    outs, first = [(0, cold_total, cold_ref)], cold_total
    for total, out_ref in zip(pieces, hot_refs):
        outs.append((first, total, out_ref))
        first += total
    for first, total, out_ref in outs:
        pick = place_row - first == lax.broadcasted_iota(jnp.int32, (total, count), 0)
        out_ref[:, :width] = jnp.dot(
            pick.astype(jnp.float32).astype(jnp.bfloat16), tokens, preferred_element_type=jnp.float32
        ).astype(jnp.bfloat16)
        owner = jnp.sum(jnp.where(pick, owner_row + 1, 0), axis=1, keepdims=True) - 1
        local = jnp.sum(jnp.where(pick, local_row, 0), axis=1, keepdims=True)
        lane = lax.broadcasted_iota(jnp.int32, (total, EXTRA), 1)
        extra = jnp.where(lane == 0, owner, jnp.where(lane == 1, local, 0))
        out_ref[:, width:] = extra.astype(jnp.float32).astype(jnp.bfloat16)


def pack(request, table, tokens, stored, owners, share, pieces):
    count, width = tokens.shape
    return pl.pallas_call(
        functools.partial(pack_kernel, stored, owners, share, pieces),
        out_shape=(
            jax.ShapeDtypeStruct((owners * share, width + EXTRA), jnp.bfloat16),
            *(jax.ShapeDtypeStruct((n, width + EXTRA), jnp.bfloat16) for n in pieces),
            jax.ShapeDtypeStruct((count, 1), jnp.int32),
            jax.ShapeDtypeStruct((1, 1), jnp.int32),
        ),
        in_specs=[whole()] * 3,
        out_specs=(whole(),) * (3 + len(pieces)),
        compiler_params=params(ALL_VMEM),
    )(request.reshape(1, -1), table.reshape(1, -1), tokens)


def down_kernel(rank, parts, me_ref, *refs):
    rows_refs = refs[:parts]
    weight_ref, out_ref, local_ref = refs[parts:]
    width = weight_ref.shape[1]
    extra = jnp.concatenate([r[:, width:].astype(jnp.float32) for r in rows_refs], axis=0).T
    local = jnp.where(extra[0:1] == me_ref[0].astype(jnp.float32), extra[1:2], -1.0)
    rows = jnp.concatenate([r[:, :width] for r in rows_refs], axis=0)
    block = 4 * rank
    out = jnp.zeros(out_ref.shape, jnp.float32)
    for first in range(0, weight_ref.shape[0], block):
        product = lax.dot_general(
            weight_ref[first : first + block, :],
            rows,
            (((1,), (1,)), ((), ())),
            preferred_element_type=jnp.float32,
        )
        for j in range(block // rank):
            mine = local == float(first // rank + j)
            out = out + jnp.where(mine, product[j * rank : (j + 1) * rank, :], 0.0)
    out_ref[...] = out
    local_ref[...] = local


def down(me, row_arrays, table, rank):
    stored_rank, width = table.shape
    count = sum(r.shape[0] for r in row_arrays)
    return pl.pallas_call(
        functools.partial(down_kernel, rank, len(row_arrays)),
        in_specs=[scalars()] + [whole()] * (len(row_arrays) + 1),
        out_specs=(whole(), whole()),
        out_shape=(
            jax.ShapeDtypeStruct((rank, count), jnp.float32),
            jax.ShapeDtypeStruct((1, count), jnp.float32),
        ),
        compiler_params=params(),
        cost_estimate=pl.CostEstimate(
            flops=2 * count * stored_rank * width,
            bytes_accessed=2 * stored_rank * width,
            transcendentals=0,
        ),
    )(me, *row_arrays, table)


def update(own_ref, other_ref, local_ref, weight_ref):
    rank, count = own_ref.shape
    pair = LANES // rank
    shrunk = (own_ref[...] + other_ref[...]).astype(jnp.bfloat16).astype(jnp.float32)
    doubled = jnp.concatenate([shrunk] * pair, axis=0).T
    local = jnp.broadcast_to(local_ref[...], (LANES, count)).T.astype(jnp.int32)
    lane_block = lax.broadcasted_iota(jnp.int32, (count, LANES), 1) // rank
    spread = jnp.concatenate(
        [
            jnp.where(lane_block + j * pair == local, doubled, 0.0).astype(jnp.bfloat16)
            for j in range(weight_ref.shape[0] // LANES)
        ],
        axis=1,
    )
    return jnp.dot(spread, weight_ref[...], preferred_element_type=jnp.float32)


def up_cold_kernel(own_ref, other_ref, local_ref, weight_ref, out_ref):
    out_ref[...] = update(own_ref, other_ref, local_ref, weight_ref).astype(jnp.bfloat16)


def up_cost(count, table):
    return pl.CostEstimate(
        flops=2 * count * table.shape[0] * table.shape[1],
        bytes_accessed=2 * table.shape[0] * table.shape[1],
        transcendentals=0,
    )


def up_cold(own, other, local, table):
    count = own.shape[1]
    return pl.pallas_call(
        up_cold_kernel,
        in_specs=[whole()] * 4,
        out_specs=whole(),
        out_shape=jax.ShapeDtypeStruct((count, table.shape[1]), jnp.bfloat16),
        compiler_params=params(),
        cost_estimate=up_cost(count, table),
    )(own, other, local, table)


def up_hot_kernel(blocks, to_ref, own_ref, other_ref, local_ref, weight_ref, *refs):
    out_ref, buffer, sems = refs[-3:]
    product = update(own_ref, other_ref, local_ref, weight_ref)
    count = buffer.shape[1]
    copies = []
    for b in range(blocks):
        buffer[b] = product[b * count : (b + 1) * count].astype(jnp.bfloat16)
        copies.append(pltpu.make_async_copy(buffer.at[b], out_ref.at[to_ref[b]], sems.at[b]))
        copies[-1].start()
    for copy in copies:
        copy.wait()


def up_hot(targets, own, other, local, table, owners, earlier):
    blocks = targets.shape[0]
    count = own.shape[1] // blocks
    kept = [] if earlier is None else [earlier]
    return pl.pallas_call(
        functools.partial(up_hot_kernel, blocks),
        in_specs=[scalars()] + [whole()] * 4 + [pl.BlockSpec(memory_space=pl.ANY) for _ in kept],
        out_specs=pl.BlockSpec(memory_space=pl.ANY),
        scratch_shapes=[
            pltpu.VMEM((blocks, count, table.shape[1]), jnp.bfloat16),
            pltpu.SemaphoreType.DMA((blocks,)),
        ],
        out_shape=jax.ShapeDtypeStruct((owners, count, table.shape[1]), jnp.bfloat16),
        input_output_aliases={5: 0} if kept else {},
        compiler_params=params(),
        cost_estimate=up_cost(blocks * count, table),
    )(targets, own, other, local, table, *kept)


def finish_kernel(
    head, busy_ref, own_ref, other_ref, cold_ref, hot_ref, place_ref, scale_ref, cos_ref, sin_ref, out_ref
):
    count, width = own_ref.shape
    cold_total = cold_ref.shape[0]
    hot_total = hot_ref.shape[1]
    place = place_ref[...]
    from_cold = place == lax.broadcasted_iota(jnp.int32, (count, cold_total), 1)
    from_hot = place - cold_total == lax.broadcasted_iota(jnp.int32, (count, hot_total), 1)
    delta = jnp.dot(
        from_cold.astype(jnp.float32).astype(jnp.bfloat16), cold_ref[...], preferred_element_type=jnp.float32
    ) + jnp.dot(
        from_hot.astype(jnp.float32).astype(jnp.bfloat16), hot_ref[0], preferred_element_type=jnp.float32
    )
    keys = own_ref[...] + other_ref[...] + delta
    cosine = cos_ref[...]
    sine = sin_ref[...]
    for h in range(width // head):
        one = keys[:, h * head : (h + 1) * head]
        normed = (
            one
            * lax.rsqrt(jnp.mean(one * one, axis=-1, keepdims=True) + 1e-06)
            * scale_ref[...]
        )
        turned = pltpu.roll(normed, head // 2, 1)
        out_ref[:, h * head : (h + 1) * head] = (normed * cosine + turned * sine).astype(jnp.bfloat16)


def finish(busy, own, other, cold, hot, place, scale, cosine, sine):
    def full(x):
        return pl.BlockSpec(x.shape, lambda i, b: (0, 0))

    scale = scale.reshape(1, -1)
    return pl.pallas_call(
        functools.partial(finish_kernel, scale.shape[1]),
        grid_spec=pltpu.PrefetchScalarGridSpec(
            num_scalar_prefetch=1,
            grid=(1,),
            in_specs=[
                full(own),
                full(other),
                full(cold),
                pl.BlockSpec((1,) + hot.shape[1:], lambda i, b: (b[0], 0, 0)),
                full(place),
                full(scale),
                full(cosine),
                full(sine),
            ],
            out_specs=full(own),
        ),
        out_shape=jax.ShapeDtypeStruct(own.shape, jnp.bfloat16),
        compiler_params=params(),
    )(busy, own, other, cold, hot, place, scale, cosine, sine)


def after(value, *earlier):
    return lax.optimization_barrier((value,) + earlier)[0]


def rope_tables(head, cached_token_length):
    half = head // 2
    inv_freq = rope_theta ** (-(jnp.arange(half, dtype=jnp.float32) * 2.0) / head)
    angles = cached_token_length.astype(jnp.float32)[:, None] * inv_freq[None, :]
    cosine = jnp.cos(angles)
    sine = jnp.sin(angles)
    return jnp.concatenate([cosine, cosine], axis=1), jnp.concatenate([-sine, sine], axis=1)


def swap(x):
    return lax.ppermute(x, "tensor", [(0, 1), (1, 0)])


def on_device(
    tokens,
    base_key_matrix,
    adapter_down_weight,
    adapter_up_weight,
    key_norm_scale,
    request_adapter,
    adapter_slot_table,
    cached_token_length,
):
    row_count, half_width = tokens.shape
    stored, rank, _ = adapter_down_weight.shape
    owners = lax.axis_size("dp")
    me = lax.axis_index("dp")
    side = lax.axis_index("tensor")
    share = (row_count + owners + 2) // (owners + 3)
    hot_count = HOT_PARTS * share
    down_table = adapter_down_weight.reshape(stored * rank, half_width)
    up_table = adapter_up_weight.reshape(stored * rank, -1)
    features = up_table.shape[1]

    first_piece = hot_count // 2 // 16 * 16 if hot_count >= 32 else hot_count // 2
    pieces = (first_piece, hot_count - first_piece)
    cold_send, hot_a, hot_b, place, busy = pack(
        request_adapter, adapter_slot_table, tokens, stored, owners, share, pieces
    )
    here = me.reshape(1).astype(jnp.int32)

    ring = ring_order(owners)
    to_next = [(ring[i], ring[(i + 1) % owners]) for i in range(owners)]
    to_last = [(b, a) for a, b in to_next]
    distances = [0] + [d for s in range(1, owners // 2) for d in (-s, s)] + [owners // 2]
    sources = [[0] * owners for _ in ring]
    for spot, index in enumerate(ring):
        sources[index] = [ring[(spot + d) % owners] for d in distances]
    order = lax.dynamic_index_in_dim(jnp.array(sources, jnp.int32), me, 0, keepdims=False)

    def onward(piece):
        return lax.ppermute(piece, "dp", to_next)

    def back(piece):
        return lax.ppermute(piece, "dp", to_last)

    def product(rows):
        own, local = down(here, rows, down_table, rank)
        return own, swap(own), local

    half_way = owners // 2
    group = [onward(hot_a), onward(hot_b), back(hot_a), back(hot_b)]
    base = jnp.dot(tokens, base_key_matrix, preferred_element_type=jnp.float32)
    base_own = lax.dynamic_slice_in_dim(base, side * features, features, 1)
    base_other = swap(lax.dynamic_slice_in_dim(base, (1 - side) * features, features, 1))
    cosine, sine = rope_tables(key_norm_scale.shape[0], cached_token_length)
    part = product([hot_a, hot_b])
    hot_delta = up_hot(order[:1], *part, up_table, owners, None)
    todo = [hot_delta, base]
    got = None
    for step in range(1, half_way):
        group = list(lax.optimization_barrier((*group, *todo))[:4])
        if got is None:
            cold_send = after(cold_send, group[0])
            got = lax.all_to_all(
                cold_send.reshape(owners, share, half_width + EXTRA),
                "dp",
                split_axis=0,
                concat_axis=0,
                tiled=True,
            ).reshape(owners * share, half_width + EXTRA)
        if step < half_way - 1:
            onward_group = [onward(group[0]), onward(group[1]), back(group[2]), back(group[3])]
        else:
            onward_group = [onward(group[0]), back(group[3])]
        part = product(group)
        hot_delta = up_hot(
            order[2 * step - 1 : 2 * step + 1], *part, up_table, owners, hot_delta
        )
        todo = [hot_delta]
        group = onward_group
    own, other, local = product([got])
    cold_back = lax.all_to_all(
        up_cold(own, other, local, up_table).reshape(owners, share, features),
        "dp",
        split_axis=0,
        concat_axis=0,
        tiled=True,
    ).reshape(owners * share, features)
    group = list(lax.optimization_barrier((*group, *todo))[:2])
    hot_delta = up_hot(order[owners - 1 :], *product(group), up_table, owners, hot_delta)
    hot_back = lax.all_to_all(hot_delta, "dp", split_axis=0, concat_axis=0, tiled=True)
    return finish(
        busy.reshape(1), base_own, base_other, cold_back, hot_back, place, key_norm_scale, cosine, sine
    )


def solution(mesh):
    placed = (
        P(("groups", "dp"), "tensor"),
        P("tensor", None),
        P(("groups", "dp"), None, "tensor"),
        P(("groups", "dp"), None, "tensor"),
        P(),
        P(("groups", "dp")),
        P("groups"),
        P(("groups", "dp")),
    )
    return jax.shard_map(
        on_device,
        mesh=mesh,
        in_specs=placed,
        out_specs=P(("groups", "dp"), "tensor"),
        check_vma=False,
    )
```

time: 137 us -> 123 us (0.90)
  Pallas kernels: 54.5 us -> 24.5 us
  local copies, waits for them, and re-layouts: 10.6 us -> 17.8 us
  waiting for transfers between devices: 32.5 us -> 38.6 us
  starting transfers between devices: 31.3 us -> 35.4 us
    pallas_call x10 -> x13, Pallas kernels: 51.1 us -> 21.5 us  [the longest x6 9.16 us: down(): pl.pallas_call(functools.partial(down_kernel, rank, len(row_arrays)), in_...]
    unnamed x42 -> x24, local copies, waits for them, and re-layouts: 5.95 us -> 14.3 us
    all_to_all x1, waiting for transfers between devices: 0.01 us -> 7.44 us  [on_device(): lax.all_to_all(up_cold(own, other, local, up_table).reshape(owners, share...]
    ppermute x8 -> x14, starting transfers between devices: 13.2 us -> 20.2 us  [the longest x7 19.9 us: onward(): return lax.ppermute(piece, 'dp', to_next)]
    all_to_all x1, waiting for transfers between devices: 13.4 us -> 7.43 us  [on_device(): lax.all_to_all(hot_delta, 'dp', split_axis=0, concat_axis=0, tiled=True)]
    ppermute x7, waiting for transfers between devices: 1.26 us -> 5.58 us  [swap(): return lax.ppermute(x, 'tensor', [(0, 1), (1, 0)])]
    slice x3 -> x1, local copies, waits for them, and re-layouts: 2.43 us -> 0.07 us  [on_device(): order[2 * step - 1:2 * step + 1]]
    ppermute x8 -> x14, waiting for transfers between devices: 17.9 us -> 18.2 us  [the longest x7 11.6 us: onward(): return lax.ppermute(piece, 'dp', to_next)]
  transfers between devices with their start and end apart: 18 -> 24, of which waited for: 7 -> 10; matrix products, arithmetic and copies ran while one was open for 8% -> 8% of each run, Pallas kernels for 28% -> 15%
where the time goes in v3:
time: 123 us
  waiting for transfers between devices  38.6 us (31%)
  starting transfers between devices  35.4 us (29%)
  Pallas kernels  24.5 us (20%)
  local copies, waits for them, and re-layouts  17.8 us (14%)
  matrix products  5.48 us (4%)
    ppermute x7, starting transfers between devices, onward(): return lax.ppermute(piece, 'dp', to_next)  19.9 us
    unnamed x24, local copies, waits for them, and re-layouts  14.3 us
    ppermute x7, waiting for transfers between devices, onward(): return lax.ppermute(piece, 'dp', to_next)  11.6 us
    pallas_call x6, Pallas kernels, down(): pl.pallas_call(functools.partial(down_kernel, rank, len(row_arrays)), in_...  9.16 us
    pallas_call x5, Pallas kernels, up_hot(): pl.pallas_call(functools.partial(up_hot_kernel, blocks), in_specs=[scalar...  7.92 us
    all_to_all x1, waiting for transfers between devices, on_device(): lax.all_to_all(up_cold(own, other, local, up_table).reshape(owners, share...  7.44 us
    all_to_all x1, waiting for transfers between devices, on_device(): lax.all_to_all(hot_delta, 'dp', split_axis=0, concat_axis=0, tiled=True)  7.43 us
    ppermute x7, waiting for transfers between devices, back(): return lax.ppermute(piece, 'dp', to_last)  6.51 us
  transfers between devices with their start and end apart: 24, of which 10 were waited for; matrix products, arithmetic and copies ran while one was open for 8% of the time, Pallas kernels for 15%

profile of v3, /device:TPU:0, one launch (start us, length us, event | category | flops | bytes accessed | tf_op | source)
XLA Modules:
  0.0 122.7 jit_solution(7791419424225446142)
XLA Ops:
  0.0 3.3 %shard_map.91 = (bf16[192,2688]{1,0:T(8,128)(2,1)}, bf16[32,2688]{1,0:T(8,128)(2,1)}, bf16[40,2688]{1,0:T(8,128)(2,1)}, s32[256,1]{1,0:T(8,128)}, s32[1,1]{1,0:T(1,128)}) custom-call(s32[1,256]{1,0:T(1,128)} %bitcast.37, s32[1,128]{1,0:T(1,128)} %bitcast.38, bf16[256,2560]{1,0:T(8,128)(2,1)} %tokens_ref.1), custom_call_target="tpu_custom_call" | custom-call | tf_op jit(solution)/shard_map/pallas_call | solution.py:88
  3.3 3.0 %collective-permute-start.2 = (bf16[40,2688]{1,0:T(8,128)(2,1)}, bf16[40,2688]{1,0:T(8,128)(2,1)S(1)}, u32[]{:S(2)}, u32[]{:S(2)}) collective-permute-start(bf16[40,2688]{1,0:T(8,128)(2,1)} %get-tuple-element.40.refs_1_), channel_id=1, source_target_pairs={{0,4},{4,8},{8,12},{12,14},{14,10},{10,6},{6,2},{2,0},{1,5},{5,9},... | collective-permute-start | bytes 645128 | tf_op jit(solution)/shard_map/ppermute | solution.py:328
  6.3 2.0 %collective-permute-start.1 = (bf16[32,2688]{1,0:T(8,128)(2,1)}, bf16[32,2688]{1,0:T(8,128)(2,1)S(1)}, u32[]{:S(2)}, u32[]{:S(2)}) collective-permute-start(bf16[32,2688]{1,0:T(8,128)(2,1)} %get-tuple-element.39.refs_0_), channel_id=1, source_target_pairs={{0,4},{4,8},{8,12},{12,14},{14,10},{10,6},{6,2},{2,0},{1,5},{5,9},... | collective-permute-start | bytes 516104 | tf_op jit(solution)/shard_map/ppermute | solution.py:328
  8.3 2.5 %copy-done = bf16[16,64,2560]{2,1,0:T(8,128)(2,1)S(1)} copy-done((bf16[16,64,2560]{2,1,0:T(8,128)(2,1)S(1)}, bf16[16,64,2560]{2,1,0:T(8,128)(2,1)}, u32[]{:S(2)}) %copy-start) | copy-done | bytes 5242904
  14.3 5.5 %fusion.2 = f32[256,1024]{1,0:T(8,128)} fusion(bf16[256,2560]{1,0:T(8,128)(2,1)} %tokens_ref.1, bf16[2560,1024]{1,0:T(8,128)(2,1)} %param.10), kind=kOutput, calls=%fused_computation.13 | convolution fusion | flops 1342177280 | bytes 7602176 | tf_op jit(solution)/shard_map/dot_general | solution.py:339
  21.1 1.6 %shard_map.93.refs_0_ = bf16[8,72,512]{2,1,0:T(8,128)(2,1)} custom-call(s32[1]{0:T(128)} %bitcast.4.to_ref, f32[64,72]{1,0:T(8,128)S(1)} %get-tuple-element.41.own_ref, f32[64,72]{1,0:T(8,128)S(1)} %collective-permute-done.5.other_ref, f32[1,72]{1,0:T(1,128)S(1)} %get-tuple-element.42.local_ref, bf16[1024,512]{1,0:T(8,128)(2,1)S(1)} %bitcast.27), custom_call_target="tpu_custom_call" | custom-call | flops 75497472 | bytes 1048576 | tf_op jit(solution)/shard_map/pallas_call | solution.py:203
  22.7 6.3 %all-to-all-start = ((bf16[8,24,2688]{2,1,0:T(8,128)(2,1)}), bf16[8,24,2688]{2,1,0:T(8,128)(2,1)S(1)}, u32[]{:S(2)}, u32[]{:S(2)}) async-start(bf16[8,24,2688]{2,1,0:T(8,128)(2,1)} %bitcast.36), calls=%async_computation | async-start | bytes 2064384 | tf_op jit(solution)/shard_map/all_to_all | solution.py:351
  29.0 2.0 %collective-permute-start.7 = (bf16[32,2688]{1,0:T(8,128)(2,1)S(1)}, bf16[32,2688]{1,0:T(8,128)(2,1)S(1)}, u32[]{:S(2)}, u32[]{:S(2)}) collective-permute-start(bf16[32,2688]{1,0:T(8,128)(2,1)S(1)} %collective-permute-done.1.refs_0_), channel_id=1, source_target_pairs={{0,4},{4,8},{8,12},{12,14},{14,10},{10,6},{6,2},{2,0},{1,5},{5,9},... | collective-permute-start | bytes 516104 | tf_op jit(solution)/shard_map/ppermute | solution.py:328
  31.0 2.0 %collective-permute-start.8 = (bf16[40,2688]{1,0:T(8,128)(2,1)S(1)}, bf16[40,2688]{1,0:T(8,128)(2,1)S(1)}, u32[]{:S(2)}, u32[]{:S(2)}) collective-permute-start(bf16[40,2688]{1,0:T(8,128)(2,1)S(1)} %collective-permute-done.2.refs_1_), channel_id=1, source_target_pairs={{0,4},{4,8},{8,12},{12,14},{14,10},{10,6},{6,2},{2,0},{1,5},{5,9},... | collective-permute-start | bytes 645128 | tf_op jit(solution)/shard_map/ppermute | solution.py:328
  33.1 2.5 %copy-done.1 = bf16[16,64,2560]{2,1,0:T(8,128)(2,1)S(1)} copy-done((bf16[16,64,2560]{2,1,0:T(8,128)(2,1)S(1)}, bf16[16,64,2560]{2,1,0:T(8,128)(2,1)}, u32[]{:S(2)}) %copy-start.1) | copy-done | bytes 5242904
  40.0 11.6 %collective-permute-done.7.refs_0_ = bf16[32,2688]{1,0:T(8,128)(2,1)S(1)} collective-permute-done((bf16[32,2688]{1,0:T(8,128)(2,1)S(1)}, bf16[32,2688]{1,0:T(8,128)(2,1)S(1)}, u32[]{:S(2)}, u32[]{:S(2)}) %collective-permute-start.7) | collective-permute-done | bytes 172064 | tf_op jit(solution)/shard_map/ppermute | solution.py:328
  51.6 5.3 %collective-permute-done.9.refs_2_ = bf16[32,2688]{1,0:T(8,128)(2,1)S(1)} collective-permute-done((bf16[32,2688]{1,0:T(8,128)(2,1)S(1)}, bf16[32,2688]{1,0:T(8,128)(2,1)S(1)}, u32[]{:S(2)}, u32[]{:S(2)}) %collective-permute-start.9) | collective-permute-done | bytes 172064 | tf_op jit(solution)/shard_map/ppermute | solution.py:331
  56.9 7.0 %collective-permute-start.13 = (bf16[40,2688]{1,0:T(8,128)(2,1)S(1)}, bf16[40,2688]{1,0:T(8,128)(2,1)S(1)}, u32[]{:S(2)}, u32[]{:S(2)}) collective-permute-start(bf16[40,2688]{1,0:T(8,128)(2,1)S(1)} %collective-permute-done.8.refs_1_), channel_id=1, source_target_pairs={{0,4},{4,8},{8,12},{12,14},{14,10},{10,6},{6,2},{2,0},{1,5},{5,9},... | collective-permute-start | bytes 645128 | tf_op jit(solution)/shard_map/ppermute | solution.py:328
  64.0 2.0 %collective-permute-start.12 = (bf16[32,2688]{1,0:T(8,128)(2,1)S(1)}, bf16[32,2688]{1,0:T(8,128)(2,1)S(1)}, u32[]{:S(2)}, u32[]{:S(2)}) collective-permute-start(bf16[32,2688]{1,0:T(8,128)(2,1)S(1)} %collective-permute-done.7.refs_0_), channel_id=1, source_target_pairs={{0,4},{4,8},{8,12},{12,14},{14,10},{10,6},{6,2},{2,0},{1,5},{5,9},... | collective-permute-start | bytes 516104 | tf_op jit(solution)/shard_map/ppermute | solution.py:328
  66.0 2.5 %copy-done.2 = bf16[16,64,2560]{2,1,0:T(8,128)(2,1)S(1)} copy-done((bf16[16,64,2560]{2,1,0:T(8,128)(2,1)S(1)}, bf16[16,64,2560]{2,1,0:T(8,128)(2,1)}, u32[]{:S(2)}) %copy-start.2) | copy-done | bytes 5242904
  74.4 1.8 %collective-permute-start.17 = (bf16[32,2688]{1,0:T(8,128)(2,1)S(1)}, bf16[32,2688]{1,0:T(8,128)(2,1)S(1)}, u32[]{:S(2)}, u32[]{:S(2)}) collective-permute-start(bf16[32,2688]{1,0:T(8,128)(2,1)S(1)} %collective-permute-done.12.refs_0_), channel_id=1, source_target_pairs={{0,4},{4,8},{8,12},{12,14},{14,10},{10,6},{6,2},{2,0},{1,5},{5,9},... | collective-permute-start | bytes 516104 | tf_op jit(solution)/shard_map/ppermute | solution.py:328
  76.2 2.5 %copy-done.3 = bf16[16,64,2560]{2,1,0:T(8,128)(2,1)S(1)} copy-done((bf16[16,64,2560]{2,1,0:T(8,128)(2,1)S(1)}, bf16[16,64,2560]{2,1,0:T(8,128)(2,1)}, u32[]{:S(2)}) %copy-start.3) | copy-done | bytes 5242904
  87.5 4.2 %all-to-all-start.2 = ((bf16[8,72,512]{2,1,0:T(8,128)(2,1)}), bf16[8,72,512]{2,1,0:T(8,128)(2,1)S(1)}, u32[]{:S(2)}, u32[]{:S(2)}) async-start(bf16[8,72,512]{2,1,0:T(8,128)(2,1)} %shard_map.103), calls=%async_computation.2 | async-start | bytes 1179648 | tf_op jit(solution)/shard_map/all_to_all | solution.py:378
  91.7 2.1 %constant_dynamic-slice_fusion.1 = (f32[256,512]{1,0:T(8,128)}, f32[256,512]{1,0:T(8,128)S(1)}) fusion(f32[256,1024]{1,0:T(8,128)} %fusion.2, s32[]{:T(128)S(6)} %select_n.11, s32[]{:T(128)S(6)} %select_n.10), kind=kLoop, calls=%fused_computation.6 | loop fusion | bytes 2097160 | tf_op jit(solution)/shard_map/dynamic_slice | solution.py:341
  93.8 2.5 %copy-done.5 = bf16[16,64,2560]{2,1,0:T(8,128)(2,1)S(1)} copy-done((bf16[16,64,2560]{2,1,0:T(8,128)(2,1)S(1)}, bf16[16,64,2560]{2,1,0:T(8,128)(2,1)}, u32[]{:S(2)}) %copy-start.5) | copy-done | bytes 5242904
  100.5 7.4 %all-to-all-done.2.hot_ref = bf16[8,72,512]{2,1,0:T(8,128)(2,1)S(1)} async-done(((bf16[8,72,512]{2,1,0:T(8,128)(2,1)}), bf16[8,72,512]{2,1,0:T(8,128)(2,1)S(1)}, u32[]{:S(2)}, u32[]{:S(2)}) %all-to-all-start.2) | async-done | bytes 589856 | tf_op jit(solution)/shard_map/all_to_all | solution.py:378
  107.9 3.6 %all-to-all-start.1 = ((bf16[8,24,512]{2,1,0:T(8,128)(2,1)}), bf16[8,24,512]{2,1,0:T(8,128)(2,1)S(1)}, u32[]{:S(2)}, u32[]{:S(2)}) async-start(bf16[8,24,512]{2,1,0:T(8,128)(2,1)} %bitcast.9), calls=%async_computation.1 | async-start | bytes 393216 | tf_op jit(solution)/shard_map/all_to_all | solution.py:369
  112.2 7.4 %all-to-all-done.1 = bf16[8,24,512]{2,1,0:T(8,128)(2,1)S(1)} async-done(((bf16[8,24,512]{2,1,0:T(8,128)(2,1)}), bf16[8,24,512]{2,1,0:T(8,128)(2,1)S(1)}, u32[]{:S(2)}, u32[]{:S(2)}) %all-to-all-start.1) | async-done | bytes 196640 | tf_op jit(solution)/shard_map/all_to_all | solution.py:369
  119.7 3.0 %shard_map.104 = bf16[256,512]{1,0:T(8,128)(2,1)} custom-call(s32[1]{0:T(128)} %bitcast.2.busy_ref, f32[256,512]{1,0:T(8,128)S(1)} %get-tuple-element.70.own_ref, f32[256,512]{1,0:T(8,128)} %collective-permute-done.other_ref, bf16[192,512]{1,0:T(8,128)(2,1)S(1)} %bitcast.34, bf16[8,72,512]{2,1,0:T(8,128)(2,1)S(1)} %all-to-all-done.2.hot_ref, ...), custom_call_target="tpu_custom_call" | custom-call | tf_op jit(solution)/shard_map/pallas_call | solution.py:251
  (71 shorter events, 28.8 us)
Async XLA Ops:
  3.3 19.4 %collective-permute-start.2 = (bf16[40,2688]{1,0:T(8,128)(2,1)}, bf16[40,2688]{1,0:T(8,128)(2,1)S(1)}, u32[]{:S(2)}, u32[]{:S(2)}) collective-permute-start(bf16[40,2688]{1,0:T(8,128)(2,1)} %get-tuple-element.40.refs_1_), channel_id=1, source_target_pairs={{0,4},{4,8},{8,12},{12,14},{14,10},{10,6},{6,2},{2,0},{1,5},{5,9},... | collective-permute-start | bytes 645128 | tf_op jit(solution)/shard_map/ppermute | solution.py:328
  6.3 16.4 %collective-permute-start.4 = (bf16[40,2688]{1,0:T(8,128)(2,1)}, bf16[40,2688]{1,0:T(8,128)(2,1)S(1)}, u32[]{:S(2)}, u32[]{:S(2)}) collective-permute-start(bf16[40,2688]{1,0:T(8,128)(2,1)} %get-tuple-element.40.refs_1_), channel_id=1, source_target_pairs={{4,0},{8,4},{12,8},{14,12},{10,14},{6,10},{2,6},{0,2},{5,1},{9,5},... | collective-permute-start | bytes 645128 | tf_op jit(solution)/shard_map/ppermute | solution.py:331
  6.3 16.4 %collective-permute-start.1 = (bf16[32,2688]{1,0:T(8,128)(2,1)}, bf16[32,2688]{1,0:T(8,128)(2,1)S(1)}, u32[]{:S(2)}, u32[]{:S(2)}) collective-permute-start(bf16[32,2688]{1,0:T(8,128)(2,1)} %get-tuple-element.39.refs_0_), channel_id=1, source_target_pairs={{0,4},{4,8},{8,12},{12,14},{14,10},{10,6},{6,2},{2,0},{1,5},{5,9},... | collective-permute-start | bytes 516104 | tf_op jit(solution)/shard_map/ppermute | solution.py:328
  8.3 14.4 %collective-permute-start.3 = (bf16[32,2688]{1,0:T(8,128)(2,1)}, bf16[32,2688]{1,0:T(8,128)(2,1)S(1)}, u32[]{:S(2)}, u32[]{:S(2)}) collective-permute-start(bf16[32,2688]{1,0:T(8,128)(2,1)} %get-tuple-element.39.refs_0_), channel_id=1, source_target_pairs={{4,0},{8,4},{12,8},{14,12},{10,14},{6,10},{2,6},{0,2},{5,1},{9,5},... | collective-permute-start | bytes 516104 | tf_op jit(solution)/shard_map/ppermute | solution.py:331
  14.2 6.9 %collective-permute-start.5 = (f32[64,72]{1,0:T(8,128)S(1)}, f32[64,72]{1,0:T(8,128)S(1)}, u32[]{:S(2)}, u32[]{:S(2)}) collective-permute-start(f32[64,72]{1,0:T(8,128)S(1)} %get-tuple-element.41.own_ref), channel_id=1, source_target_pairs={{0,1},{1,0},{2,3},{3,2},{4,5},{5,4},{6,7},{7,6},{8,9},{9,8},{10,11... | collective-permute-start | bytes 55304 | tf_op jit(solution)/shard_map/ppermute | solution.py:287
  22.7 64.8 %all-to-all-start = ((bf16[8,24,2688]{2,1,0:T(8,128)(2,1)}), bf16[8,24,2688]{2,1,0:T(8,128)(2,1)S(1)}, u32[]{:S(2)}, u32[]{:S(2)}) async-start(bf16[8,24,2688]{2,1,0:T(8,128)(2,1)} %bitcast.36), calls=%async_computation | async-start | bytes 2064384 | tf_op jit(solution)/shard_map/all_to_all | solution.py:351
  29.0 22.7 %collective-permute-start.7 = (bf16[32,2688]{1,0:T(8,128)(2,1)S(1)}, bf16[32,2688]{1,0:T(8,128)(2,1)S(1)}, u32[]{:S(2)}, u32[]{:S(2)}) collective-permute-start(bf16[32,2688]{1,0:T(8,128)(2,1)S(1)} %collective-permute-done.1.refs_0_), channel_id=1, source_target_pairs={{0,4},{4,8},{8,12},{12,14},{14,10},{10,6},{6,2},{2,0},{1,5},{5,9},... | collective-permute-start | bytes 516104 | tf_op jit(solution)/shard_map/ppermute | solution.py:328
  31.0 25.9 %collective-permute-start.10 = (bf16[40,2688]{1,0:T(8,128)(2,1)S(1)}, bf16[40,2688]{1,0:T(8,128)(2,1)S(1)}, u32[]{:S(2)}, u32[]{:S(2)}) collective-permute-start(bf16[40,2688]{1,0:T(8,128)(2,1)S(1)} %collective-permute-done.4.refs_3_), channel_id=1, source_target_pairs={{4,0},{8,4},{12,8},{14,12},{10,14},{6,10},{2,6},{0,2},{5,1},{9,5},... | collective-permute-start | bytes 645128 | tf_op jit(solution)/shard_map/ppermute | solution.py:331
  31.0 25.9 %collective-permute-start.8 = (bf16[40,2688]{1,0:T(8,128)(2,1)S(1)}, bf16[40,2688]{1,0:T(8,128)(2,1)S(1)}, u32[]{:S(2)}, u32[]{:S(2)}) collective-permute-start(bf16[40,2688]{1,0:T(8,128)(2,1)S(1)} %collective-permute-done.2.refs_1_), channel_id=1, source_target_pairs={{0,4},{4,8},{8,12},{12,14},{14,10},{10,6},{6,2},{2,0},{1,5},{5,9},... | collective-permute-start | bytes 645128 | tf_op jit(solution)/shard_map/ppermute | solution.py:328
  33.0 23.9 %collective-permute-start.9 = (bf16[32,2688]{1,0:T(8,128)(2,1)S(1)}, bf16[32,2688]{1,0:T(8,128)(2,1)S(1)}, u32[]{:S(2)}, u32[]{:S(2)}) collective-permute-start(bf16[32,2688]{1,0:T(8,128)(2,1)S(1)} %collective-permute-done.3.refs_2_), channel_id=1, source_target_pairs={{4,0},{8,4},{12,8},{14,12},{10,14},{6,10},{2,6},{0,2},{5,1},{9,5},... | collective-permute-start | bytes 516104 | tf_op jit(solution)/shard_map/ppermute | solution.py:331
  37.1 1.3 %collective-permute-start.11 = (f32[64,144]{1,0:T(8,128)S(1)}, f32[64,144]{1,0:T(8,128)S(1)}, u32[]{:S(2)}, u32[]{:S(2)}) collective-permute-start(f32[64,144]{1,0:T(8,128)S(1)} %get-tuple-element.50.own_ref), channel_id=1, source_target_pairs={{0,1},{1,0},{2,3},{3,2},{4,5},{5,4},{6,7},{7,6},{8,9},{9,8},{10,11... | collective-permute-start | bytes 110600 | tf_op jit(solution)/shard_map/ppermute | solution.py:287
  56.9 17.2 %collective-permute-start.13 = (bf16[40,2688]{1,0:T(8,128)(2,1)S(1)}, bf16[40,2688]{1,0:T(8,128)(2,1)S(1)}, u32[]{:S(2)}, u32[]{:S(2)}) collective-permute-start(bf16[40,2688]{1,0:T(8,128)(2,1)S(1)} %collective-permute-done.8.refs_1_), channel_id=1, source_target_pairs={{0,4},{4,8},{8,12},{12,14},{14,10},{10,6},{6,2},{2,0},{1,5},{5,9},... | collective-permute-start | bytes 645128 | tf_op jit(solution)/shard_map/ppermute | solution.py:328
  64.0 10.2 %collective-permute-start.15 = (bf16[40,2688]{1,0:T(8,128)(2,1)S(1)}, bf16[40,2688]{1,0:T(8,128)(2,1)S(1)}, u32[]{:S(2)}, u32[]{:S(2)}) collective-permute-start(bf16[40,2688]{1,0:T(8,128)(2,1)S(1)} %collective-permute-done.10.refs_3_), channel_id=1, source_target_pairs={{4,0},{8,4},{12,8},{14,12},{10,14},{6,10},{2,6},{0,2},{5,1},{9,5},... | collective-permute-start | bytes 645128 | tf_op jit(solution)/shard_map/ppermute | solution.py:331
  64.0 9.0 %collective-permute-start.12 = (bf16[32,2688]{1,0:T(8,128)(2,1)S(1)}, bf16[32,2688]{1,0:T(8,128)(2,1)S(1)}, u32[]{:S(2)}, u32[]{:S(2)}) collective-permute-start(bf16[32,2688]{1,0:T(8,128)(2,1)S(1)} %collective-permute-done.7.refs_0_), channel_id=1, source_target_pairs={{0,4},{4,8},{8,12},{12,14},{14,10},{10,6},{6,2},{2,0},{1,5},{5,9},... | collective-permute-start | bytes 516104 | tf_op jit(solution)/shard_map/ppermute | solution.py:328
  66.0 8.2 %collective-permute-start.14 = (bf16[32,2688]{1,0:T(8,128)(2,1)S(1)}, bf16[32,2688]{1,0:T(8,128)(2,1)S(1)}, u32[]{:S(2)}, u32[]{:S(2)}) collective-permute-start(bf16[32,2688]{1,0:T(8,128)(2,1)S(1)} %collective-permute-done.9.refs_2_), channel_id=1, source_target_pairs={{4,0},{8,4},{12,8},{14,12},{10,14},{6,10},{2,6},{0,2},{5,1},{9,5},... | collective-permute-start | bytes 516104 | tf_op jit(solution)/shard_map/ppermute | solution.py:331
  70.0 1.3 %collective-permute-start.16 = (f32[64,144]{1,0:T(8,128)S(1)}, f32[64,144]{1,0:T(8,128)S(1)}, u32[]{:S(2)}, u32[]{:S(2)}) collective-permute-start(f32[64,144]{1,0:T(8,128)S(1)} %get-tuple-element.56.own_ref), channel_id=1, source_target_pairs={{0,1},{1,0},{2,3},{3,2},{4,5},{5,4},{6,7},{7,6},{8,9},{9,8},{10,11... | collective-permute-start | bytes 110600 | tf_op jit(solution)/shard_map/ppermute | solution.py:287
  74.2 9.0 %collective-permute-start.18 = (bf16[40,2688]{1,0:T(8,128)(2,1)S(1)}, bf16[40,2688]{1,0:T(8,128)(2,1)S(1)}, u32[]{:S(2)}, u32[]{:S(2)}) collective-permute-start(bf16[40,2688]{1,0:T(8,128)(2,1)S(1)} %collective-permute-done.15.refs_3_), channel_id=1, source_target_pairs={{4,0},{8,4},{12,8},{14,12},{10,14},{6,10},{2,6},{0,2},{5,1},{9,5},... | collective-permute-start | bytes 645128 | tf_op jit(solution)/shard_map/ppermute | solution.py:331
  74.4 8.7 %collective-permute-start.17 = (bf16[32,2688]{1,0:T(8,128)(2,1)S(1)}, bf16[32,2688]{1,0:T(8,128)(2,1)S(1)}, u32[]{:S(2)}, u32[]{:S(2)}) collective-permute-start(bf16[32,2688]{1,0:T(8,128)(2,1)S(1)} %collective-permute-done.12.refs_0_), channel_id=1, source_target_pairs={{0,4},{4,8},{8,12},{12,14},{14,10},{10,6},{6,2},{2,0},{1,5},{5,9},... | collective-permute-start | bytes 516104 | tf_op jit(solution)/shard_map/ppermute | solution.py:328
  80.2 1.3 %collective-permute-start.19 = (f32[64,144]{1,0:T(8,128)S(1)}, f32[64,144]{1,0:T(8,128)S(1)}, u32[]{:S(2)}, u32[]{:S(2)}) collective-permute-start(f32[64,144]{1,0:T(8,128)S(1)} %get-tuple-element.62.own_ref), channel_id=1, source_target_pairs={{0,1},{1,0},{2,3},{3,2},{4,5},{5,4},{6,7},{7,6},{8,9},{9,8},{10,11... | collective-permute-start | bytes 110600 | tf_op jit(solution)/shard_map/ppermute | solution.py:287
  84.7 1.3 %collective-permute-start.20 = (f32[64,72]{1,0:T(8,128)S(1)}, f32[64,72]{1,0:T(8,128)S(1)}, u32[]{:S(2)}, u32[]{:S(2)}) collective-permute-start(f32[64,72]{1,0:T(8,128)S(1)} %get-tuple-element.66.own_ref), channel_id=1, source_target_pairs={{0,1},{1,0},{2,3},{3,2},{4,5},{5,4},{6,7},{7,6},{8,9},{9,8},{10,11... | collective-permute-start | bytes 55304 | tf_op jit(solution)/shard_map/ppermute | solution.py:287
  87.5 20.4 %all-to-all-start.2 = ((bf16[8,72,512]{2,1,0:T(8,128)(2,1)}), bf16[8,72,512]{2,1,0:T(8,128)(2,1)S(1)}, u32[]{:S(2)}, u32[]{:S(2)}) async-start(bf16[8,72,512]{2,1,0:T(8,128)(2,1)} %shard_map.103), calls=%async_computation.2 | async-start | bytes 1179648 | tf_op jit(solution)/shard_map/all_to_all | solution.py:378
  93.8 18.4 %collective-permute-start = (f32[256,512]{1,0:T(8,128)}, f32[256,512]{1,0:T(8,128)}, u32[]{:S(2)}, u32[]{:S(2)}) collective-permute-start(f32[256,512]{1,0:T(8,128)} %get-tuple-element.69), channel_id=1, source_target_pairs={{0,1},{1,0},{2,3},{3,2},{4,5},{5,4},{6,7},{7,6},{8,9},{9,8},{10,11... | collective-permute-start | bytes 1572872 | tf_op jit(solution)/shard_map/ppermute | solution.py:287
  97.9 1.5 %collective-permute-start.6 = (f32[64,192]{1,0:T(8,128)S(1)}, f32[64,192]{1,0:T(8,128)S(1)}, u32[]{:S(2)}, u32[]{:S(2)}) collective-permute-start(f32[64,192]{1,0:T(8,128)S(1)} %get-tuple-element.45.own_ref), channel_id=1, source_target_pairs={{0,1},{1,0},{2,3},{3,2},{4,5},{5,4},{6,7},{7,6},{8,9},{9,8},{10,11... | collective-permute-start | bytes 147464 | tf_op jit(solution)/shard_map/ppermute | solution.py:287
  107.9 11.8 %all-to-all-start.1 = ((bf16[8,24,512]{2,1,0:T(8,128)(2,1)}), bf16[8,24,512]{2,1,0:T(8,128)(2,1)S(1)}, u32[]{:S(2)}, u32[]{:S(2)}) async-start(bf16[8,24,512]{2,1,0:T(8,128)(2,1)} %bitcast.9), calls=%async_computation.1 | async-start | bytes 393216 | tf_op jit(solution)/shard_map/all_to_all | solution.py:369
  (12 other events, 102.7 us)

commit v4 on v3

--- a/solution.py
+++ b/solution.py
@@ -39,12 +39,27 @@
     return jnp.sum(jnp.where(square, row, 0), axis=1, keepdims=True)
 
 
-def pack_kernel(
-    stored, owners, share, pieces, request_ref, table_ref, tokens_ref, cold_ref, *refs
-):
-    hot_refs, (place_ref, busy_ref) = refs[: len(pieces)], refs[len(pieces) :]
+def choose(pick, tokens_ref, owner_row, local_row, out_ref):
+    total, count = pick.shape
+    width = tokens_ref.shape[1]
+    out_ref[:, :width] = jnp.dot(
+        pick.astype(jnp.float32).astype(jnp.bfloat16),
+        tokens_ref[...],
+        preferred_element_type=jnp.float32,
+    ).astype(jnp.bfloat16)
+    owner = jnp.sum(jnp.where(pick, owner_row + 1, 0), axis=1, keepdims=True) - 1
+    local = jnp.sum(jnp.where(pick, local_row, 0), axis=1, keepdims=True)
+    lane = lax.broadcasted_iota(jnp.int32, (total, EXTRA), 1)
+    extra = jnp.where(lane == 0, owner, jnp.where(lane == 1, local, 0))
+    out_ref[:, width:] = extra.astype(jnp.float32).astype(jnp.bfloat16)
+
+
+def route_kernel(stored, owners, share, pieces, request_ref, table_ref, tokens_hbm, *refs):
+    hot_refs = refs[: len(pieces)]
+    place_ref, busy_ref, info_ref, tokens_ref, sem = refs[len(pieces) :]
+    fetch = pltpu.make_async_copy(tokens_hbm, tokens_ref, sem)
+    fetch.start()
     count = request_ref.shape[1]
-    width = tokens_ref.shape[1]
     request_col = to_column(request_ref[...])
     adapters = table_ref.shape[1]
     match = request_col == lax.broadcasted_iota(jnp.int32, (count, adapters), 1)
@@ -66,37 +81,49 @@
     busy_ref[...] = jnp.max(jnp.where(rank_row >= share, owner_row, 0), axis=1, keepdims=True)
     place_row = place(owner_row, rank_row)
     local_row = slot_row - owner_row * stored
-    tokens = tokens_ref[...]
-    outs, first = [(0, cold_total, cold_ref)], cold_total
+    info_ref[0:1, :] = place_row
+    info_ref[1:2, :] = owner_row
+    info_ref[2:3, :] = local_row
+    fetch.wait()
+    first = cold_total
     for total, out_ref in zip(pieces, hot_refs):
-        outs.append((first, total, out_ref))
+        pick = place_row - first == lax.broadcasted_iota(jnp.int32, (total, count), 0)
+        choose(pick, tokens_ref, owner_row, local_row, out_ref)
         first += total
-    for first, total, out_ref in outs:
-        pick = place_row - first == lax.broadcasted_iota(jnp.int32, (total, count), 0)
-        out_ref[:, :width] = jnp.dot(
-            pick.astype(jnp.float32).astype(jnp.bfloat16), tokens, preferred_element_type=jnp.float32
-        ).astype(jnp.bfloat16)
-        owner = jnp.sum(jnp.where(pick, owner_row + 1, 0), axis=1, keepdims=True) - 1
-        local = jnp.sum(jnp.where(pick, local_row, 0), axis=1, keepdims=True)
-        lane = lax.broadcasted_iota(jnp.int32, (total, EXTRA), 1)
-        extra = jnp.where(lane == 0, owner, jnp.where(lane == 1, local, 0))
-        out_ref[:, width:] = extra.astype(jnp.float32).astype(jnp.bfloat16)
-
-
-def pack(request, table, tokens, stored, owners, share, pieces):
+
+
+def route(request, table, tokens, stored, owners, share, pieces):
     count, width = tokens.shape
     return pl.pallas_call(
-        functools.partial(pack_kernel, stored, owners, share, pieces),
+        functools.partial(route_kernel, stored, owners, share, pieces),
         out_shape=(
-            jax.ShapeDtypeStruct((owners * share, width + EXTRA), jnp.bfloat16),
             *(jax.ShapeDtypeStruct((n, width + EXTRA), jnp.bfloat16) for n in pieces),
             jax.ShapeDtypeStruct((count, 1), jnp.int32),
             jax.ShapeDtypeStruct((1, 1), jnp.int32),
+            jax.ShapeDtypeStruct((3, count), jnp.int32),
         ),
-        in_specs=[whole()] * 3,
+        in_specs=[whole(), whole(), pl.BlockSpec(memory_space=pl.ANY)],
         out_specs=(whole(),) * (3 + len(pieces)),
+        scratch_shapes=[pltpu.VMEM((count, width), jnp.bfloat16), pltpu.SemaphoreType.DMA],
         compiler_params=params(ALL_VMEM),
     )(request.reshape(1, -1), table.reshape(1, -1), tokens)
+
+
+def pack_cold_kernel(info_ref, tokens_ref, out_ref):
+    total, count = out_ref.shape[0], tokens_ref.shape[0]
+    pick = info_ref[0:1, :] == lax.broadcasted_iota(jnp.int32, (total, count), 0)
+    choose(pick, tokens_ref, info_ref[1:2, :], info_ref[2:3, :], out_ref)
+
+
+def pack_cold(info, tokens, total):
+    width = tokens.shape[1]
+    return pl.pallas_call(
+        pack_cold_kernel,
+        out_shape=jax.ShapeDtypeStruct((total, width + EXTRA), jnp.bfloat16),
+        in_specs=[whole(), whole()],
+        out_specs=whole(),
+        compiler_params=params(),
+    )(info, tokens)
 
 
 def down_kernel(rank, parts, me_ref, *refs):
@@ -215,21 +242,36 @@
     )(targets, own, other, local, table, *kept)
 
 
-def finish_kernel(
-    head, busy_ref, own_ref, other_ref, cold_ref, hot_ref, place_ref, scale_ref, cos_ref, sin_ref, out_ref
-):
-    count, width = own_ref.shape
-    cold_total = cold_ref.shape[0]
-    hot_total = hot_ref.shape[1]
-    place = place_ref[...]
-    from_cold = place == lax.broadcasted_iota(jnp.int32, (count, cold_total), 1)
-    from_hot = place - cold_total == lax.broadcasted_iota(jnp.int32, (count, hot_total), 1)
+def gather_kernel(own_ref, other_ref, cold_ref, place_ref, out_ref):
+    count, cold_total = own_ref.shape[0], cold_ref.shape[0]
+    from_cold = place_ref[...] == lax.broadcasted_iota(jnp.int32, (count, cold_total), 1)
     delta = jnp.dot(
         from_cold.astype(jnp.float32).astype(jnp.bfloat16), cold_ref[...], preferred_element_type=jnp.float32
-    ) + jnp.dot(
-        from_hot.astype(jnp.float32).astype(jnp.bfloat16), hot_ref[0], preferred_element_type=jnp.float32
-    )
-    keys = own_ref[...] + other_ref[...] + delta
+    )
+    out_ref[...] = own_ref[...] + other_ref[...] + delta
+
+
+def gather_cold(own, other, cold, place):
+    return pl.pallas_call(
+        gather_kernel,
+        in_specs=[whole()] * 4,
+        out_specs=whole(),
+        out_shape=jax.ShapeDtypeStruct(own.shape, jnp.float32),
+        compiler_params=params(),
+    )(own, other, cold, place)
+
+
+def finish_kernel(
+    head, first, busy_ref, keys_ref, hot_ref, place_ref, scale_ref, cos_ref, sin_ref, out_ref
+):
+    count, width = keys_ref.shape
+    hot_total = hot_ref.shape[1]
+    from_hot = place_ref[...] - first == lax.broadcasted_iota(jnp.int32, (count, hot_total), 1)
+    keys = keys_ref[...] + jnp.dot(
+        from_hot.astype(jnp.float32).astype(jnp.bfloat16),
+        hot_ref[busy_ref[0]],
+        preferred_element_type=jnp.float32,
+    )
     cosine = cos_ref[...]
     sine = sin_ref[...]
     for h in range(width // head):
@@ -243,31 +285,14 @@
         out_ref[:, h * head : (h + 1) * head] = (normed * cosine + turned * sine).astype(jnp.bfloat16)
 
 
-def finish(busy, own, other, cold, hot, place, scale, cosine, sine):
-    def full(x):
-        return pl.BlockSpec(x.shape, lambda i, b: (0, 0))
-
-    scale = scale.reshape(1, -1)
-    return pl.pallas_call(
-        functools.partial(finish_kernel, scale.shape[1]),
-        grid_spec=pltpu.PrefetchScalarGridSpec(
-            num_scalar_prefetch=1,
-            grid=(1,),
-            in_specs=[
-                full(own),
-                full(other),
-                full(cold),
-                pl.BlockSpec((1,) + hot.shape[1:], lambda i, b: (b[0], 0, 0)),
-                full(place),
-                full(scale),
-                full(cosine),
-                full(sine),
-            ],
-            out_specs=full(own),
-        ),
-        out_shape=jax.ShapeDtypeStruct(own.shape, jnp.bfloat16),
-        compiler_params=params(),
-    )(busy, own, other, cold, hot, place, scale, cosine, sine)
+def finish(first, busy, keys, hot, place, scale, cosine, sine):
+    return pl.pallas_call(
+        functools.partial(finish_kernel, scale.shape[0], first),
+        in_specs=[scalars()] + [whole()] * 6,
+        out_specs=whole(),
+        out_shape=jax.ShapeDtypeStruct(keys.shape, jnp.bfloat16),
+        compiler_params=params(),
+    )(busy, keys, hot, place, scale.reshape(1, -1), cosine, sine)
 
 
 def after(value, *earlier):
@@ -310,9 +335,10 @@
 
     first_piece = hot_count // 2 // 16 * 16 if hot_count >= 32 else hot_count // 2
     pieces = (first_piece, hot_count - first_piece)
-    cold_send, hot_a, hot_b, place, busy = pack(
+    hot_a, hot_b, place, busy, info = route(
         request_adapter, adapter_slot_table, tokens, stored, owners, share, pieces
     )
+    cold_send = pack_cold(info, tokens, owners * share)
     here = me.reshape(1).astype(jnp.int32)
 
     ring = ring_order(owners)
@@ -334,51 +360,44 @@
         own, local = down(here, rows, down_table, rank)
         return own, swap(own), local
 
+    def exchange(rows):
+        split = rows.reshape(owners, -1, rows.shape[-1])
+        return lax.all_to_all(split, "dp", split_axis=0, concat_axis=0, tiled=True).reshape(rows.shape)
+
     half_way = owners // 2
     group = [onward(hot_a), onward(hot_b), back(hot_a), back(hot_b)]
-    base = jnp.dot(tokens, base_key_matrix, preferred_element_type=jnp.float32)
-    base_own = lax.dynamic_slice_in_dim(base, side * features, features, 1)
-    base_other = swap(lax.dynamic_slice_in_dim(base, (1 - side) * features, features, 1))
-    cosine, sine = rope_tables(key_norm_scale.shape[0], cached_token_length)
+    got = exchange(cold_send)
     part = product([hot_a, hot_b])
     hot_delta = up_hot(order[:1], *part, up_table, owners, None)
-    todo = [hot_delta, base]
-    got = None
+    todo = [hot_delta]
     for step in range(1, half_way):
         group = list(lax.optimization_barrier((*group, *todo))[:4])
-        if got is None:
-            cold_send = after(cold_send, group[0])
-            got = lax.all_to_all(
-                cold_send.reshape(owners, share, half_width + EXTRA),
-                "dp",
-                split_axis=0,
-                concat_axis=0,
-                tiled=True,
-            ).reshape(owners * share, half_width + EXTRA)
         if step < half_way - 1:
-            onward_group = [onward(group[0]), onward(group[1]), back(group[2]), back(group[3])]
+            following = [onward(group[0]), onward(group[1]), back(group[2]), back(group[3])]
         else:
-            onward_group = [onward(group[0]), back(group[3])]
-        part = product(group)
+            following = [onward(group[0]), back(group[3])]
         hot_delta = up_hot(
-            order[2 * step - 1 : 2 * step + 1], *part, up_table, owners, hot_delta
+            order[2 * step - 1 : 2 * step + 1], *product(group), up_table, owners, hot_delta
         )
         todo = [hot_delta]
-        group = onward_group
-    own, other, local = product([got])
-    cold_back = lax.all_to_all(
-        up_cold(own, other, local, up_table).reshape(owners, share, features),
-        "dp",
-        split_axis=0,
-        concat_axis=0,
-        tiled=True,
-    ).reshape(owners * share, features)
+        if step == 1:
+            base = jnp.dot(
+                after(tokens, group[0]), base_key_matrix, preferred_element_type=jnp.float32
+            )
+            base_own = lax.dynamic_slice_in_dim(base, side * features, features, 1)
+            base_other = swap(lax.dynamic_slice_in_dim(base, (1 - side) * features, features, 1))
+            todo += [base_own]
+        if step == max(half_way - 2, 1):
+            cold_delta = up_cold(*product([got]), up_table)
+            todo += [cold_delta]
+        group = following
+    cold_back = exchange(cold_delta)
     group = list(lax.optimization_barrier((*group, *todo))[:2])
     hot_delta = up_hot(order[owners - 1 :], *product(group), up_table, owners, hot_delta)
     hot_back = lax.all_to_all(hot_delta, "dp", split_axis=0, concat_axis=0, tiled=True)
-    return finish(
-        busy.reshape(1), base_own, base_other, cold_back, hot_back, place, key_norm_scale, cosine, sine
-    )
+    keys = gather_cold(base_own, base_other, cold_back, place)
+    cosine, sine = rope_tables(key_norm_scale.shape[0], cached_token_length)
+    return finish(owners * share, busy.reshape(1), keys, hot_back, place, key_norm_scale, cosine, sine)
 
 
 def solution(mesh):

time: 123 us -> 121 us (0.984)
  waiting for transfers between devices: 38.6 us -> 33.5 us
  Pallas kernels: 24.5 us -> 28.8 us
  matrix products: 5.48 us -> 1.51 us
  local copies, waits for them, and re-layouts: 17.8 us -> 19.1 us
    ppermute x7, waiting for transfers between devices: 11.6 us -> 2.63 us  [onward(): return lax.ppermute(piece, 'dp', to_next)]
    all_to_all x2, waiting for transfers between devices: 7.45 us -> 0.01 us  [exchange(): lax.all_to_all(split, 'dp', split_axis=0, concat_axis=0, tiled=True)]
    ppermute x7, starting transfers between devices: 19.9 us -> 13.1 us  [onward(): return lax.ppermute(piece, 'dp', to_next)]
    all_to_all x1, waiting for transfers between devices: 7.43 us -> 13.8 us  [on_device(): lax.all_to_all(hot_delta, 'dp', split_axis=0, concat_axis=0, tiled=True)]
    ppermute x7, starting transfers between devices: 0.34 us -> 6.32 us  [back(): return lax.ppermute(piece, 'dp', to_last)]
    ppermute x7, waiting for transfers between devices: 6.51 us -> 12 us  [back(): return lax.ppermute(piece, 'dp', to_last)]
    dot_general x1, matrix products: 5.48 us -> 1.51 us  [on_device(): jnp.dot(after(tokens, group[0]), base_key_matrix, preferred_element_type=...]
    pallas_call x6, Pallas kernels: 9.16 us -> 12.8 us  [down(): pl.pallas_call(functools.partial(down_kernel, rank, len(row_arrays)), in_...]
  transfers between devices with their start and end apart: 24 -> 24, of which waited for: 10 -> 9; matrix products, arithmetic and copies ran while one was open for 8% -> 4% of each run, Pallas kernels for 15% -> 18%
where the time goes in v4:
time: 121 us; the launch traced here: 120 us
  starting transfers between devices  36.4 us (30%)
  waiting for transfers between devices  33.5 us (28%)
  Pallas kernels  28.8 us (24%)
  local copies, waits for them, and re-layouts  19.1 us (16%)
  matrix products  1.51 us (1%)
    unnamed x44, local copies, waits for them, and re-layouts  16.2 us
    all_to_all x1, waiting for transfers between devices, on_device(): lax.all_to_all(hot_delta, 'dp', split_axis=0, concat_axis=0, tiled=True)  13.8 us
    ppermute x7, starting transfers between devices, onward(): return lax.ppermute(piece, 'dp', to_next)  13.1 us
    pallas_call x6, Pallas kernels, down(): pl.pallas_call(functools.partial(down_kernel, rank, len(row_arrays)), in_...  12.8 us
    ppermute x7, waiting for transfers between devices, back(): return lax.ppermute(piece, 'dp', to_last)  12 us
    all_to_all x2, starting transfers between devices, exchange(): lax.all_to_all(split, 'dp', split_axis=0, concat_axis=0, tiled=True)  11.3 us
    pallas_call x5, Pallas kernels, up_hot(): pl.pallas_call(functools.partial(up_hot_kernel, blocks), in_specs=[scalar...  7.91 us
    ppermute x7, starting transfers between devices, back(): return lax.ppermute(piece, 'dp', to_last)  6.32 us
  transfers between devices with their start and end apart: 24, of which 9 were waited for; matrix products, arithmetic and copies ran while one was open for 4% of the time, Pallas kernels for 18%

profile of v4, /device:TPU:0, one launch (start us, length us, event | category | flops | bytes accessed | tf_op | source)
XLA Modules:
  0.0 120.3 jit_solution(17522779749071791465)
XLA Ops:
  0.0 3.3 %shard_map.91 = (bf16[32,2688]{1,0:T(8,128)(2,1)}, bf16[40,2688]{1,0:T(8,128)(2,1)}, s32[256,1]{1,0:T(8,128)}, s32[1,1]{1,0:T(1,128)}, s32[3,256]{1,0:T(4,128)}) custom-call(s32[1,256]{1,0:T(1,128)} %bitcast.38, s32[1,128]{1,0:T(1,128)} %bitcast.39, bf16[256,2560]{1,0:T(8,128)(2,1)} %tokens_ref.1), custom_call_target="tpu_custom_call" | custom-call | tf_op jit(solution)/shard_map/pallas_call | solution.py:97
  6.9 7.2 %all-to-all-start = ((bf16[8,24,2688]{2,1,0:T(8,128)(2,1)}), bf16[8,24,2688]{2,1,0:T(8,128)(2,1)S(1)}, u32[]{:S(2)}, u32[]{:S(2)}) async-start(bf16[8,24,2688]{2,1,0:T(8,128)(2,1)} %bitcast.7), calls=%async_computation | async-start | bytes 2064384 | tf_op jit(solution)/shard_map/all_to_all | solution.py:365
  14.1 2.0 %collective-permute-start.2 = (bf16[32,2688]{1,0:T(8,128)(2,1)}, bf16[32,2688]{1,0:T(8,128)(2,1)}, u32[]{:S(2)}, u32[]{:S(2)}) collective-permute-start(bf16[32,2688]{1,0:T(8,128)(2,1)} %get-tuple-element.38.refs_0_), channel_id=1, source_target_pairs={{4,0},{8,4},{12,8},{14,12},{10,14},{6,10},{2,6},{0,2},{5,1},{9,5},... | collective-permute-start | bytes 516104 | tf_op jit(solution)/shard_map/ppermute | solution.py:357
  16.2 2.0 %collective-permute-start.3 = (bf16[40,2688]{1,0:T(8,128)(2,1)}, bf16[40,2688]{1,0:T(8,128)(2,1)}, u32[]{:S(2)}, u32[]{:S(2)}) collective-permute-start(bf16[40,2688]{1,0:T(8,128)(2,1)} %get-tuple-element.39.refs_1_), channel_id=1, source_target_pairs={{4,0},{8,4},{12,8},{14,12},{10,14},{6,10},{2,6},{0,2},{5,1},{9,5},... | collective-permute-start | bytes 645128 | tf_op jit(solution)/shard_map/ppermute | solution.py:357
  18.2 2.5 %copy-done = bf16[16,64,2560]{2,1,0:T(8,128)(2,1)S(1)} copy-done((bf16[16,64,2560]{2,1,0:T(8,128)(2,1)S(1)}, bf16[16,64,2560]{2,1,0:T(8,128)(2,1)}, u32[]{:S(2)}) %copy-start) | copy-done | bytes 5242904
  27.7 6.3 %collective-permute-done.2.refs_2_ = bf16[32,2688]{1,0:T(8,128)(2,1)} collective-permute-done((bf16[32,2688]{1,0:T(8,128)(2,1)}, bf16[32,2688]{1,0:T(8,128)(2,1)}, u32[]{:S(2)}, u32[]{:S(2)}) %collective-permute-start.2) | collective-permute-done | bytes 172064 | tf_op jit(solution)/shard_map/ppermute | solution.py:357
  34.1 1.8 %collective-permute-done.refs_0_ = bf16[32,2688]{1,0:T(8,128)(2,1)} collective-permute-done((bf16[32,2688]{1,0:T(8,128)(2,1)}, bf16[32,2688]{1,0:T(8,128)(2,1)}, u32[]{:S(2)}, u32[]{:S(2)}) %collective-permute-start) | collective-permute-done | bytes 172064 | tf_op jit(solution)/shard_map/ppermute | solution.py:354
  35.9 5.7 %collective-permute-done.3.refs_3_ = bf16[40,2688]{1,0:T(8,128)(2,1)} collective-permute-done((bf16[40,2688]{1,0:T(8,128)(2,1)}, bf16[40,2688]{1,0:T(8,128)(2,1)}, u32[]{:S(2)}, u32[]{:S(2)}) %collective-permute-start.3) | collective-permute-done | bytes 215072 | tf_op jit(solution)/shard_map/ppermute | solution.py:357
  41.5 7.0 %collective-permute-start.7 = (bf16[32,2688]{1,0:T(8,128)(2,1)}, bf16[32,2688]{1,0:T(8,128)(2,1)S(1)}, u32[]{:S(2)}, u32[]{:S(2)}) collective-permute-start(bf16[32,2688]{1,0:T(8,128)(2,1)} %collective-permute-done.refs_0_), channel_id=1, source_target_pairs={{0,4},{4,8},{8,12},{12,14},{14,10},{10,6},{6,2},{2,0},{1,5},{5,9},... | collective-permute-start | bytes 516104 | tf_op jit(solution)/shard_map/ppermute | solution.py:354
  48.6 2.0 %collective-permute-start.8 = (bf16[40,2688]{1,0:T(8,128)(2,1)}, bf16[40,2688]{1,0:T(8,128)(2,1)}, u32[]{:S(2)}, u32[]{:S(2)}) collective-permute-start(bf16[40,2688]{1,0:T(8,128)(2,1)} %collective-permute-done.1.refs_1_), channel_id=1, source_target_pairs={{0,4},{4,8},{8,12},{12,14},{14,10},{10,6},{6,2},{2,0},{1,5},{5,9},... | collective-permute-start | bytes 645128 | tf_op jit(solution)/shard_map/ppermute | solution.py:354
  50.6 2.5 %copy-done.1 = bf16[16,64,2560]{2,1,0:T(8,128)(2,1)S(1)} copy-done((bf16[16,64,2560]{2,1,0:T(8,128)(2,1)S(1)}, bf16[16,64,2560]{2,1,0:T(8,128)(2,1)}, u32[]{:S(2)}) %copy-start.1) | copy-done | bytes 5242904
  53.1 2.9 %shard_map.98 = (f32[64,144]{1,0:T(8,128)S(1)}, f32[1,144]{1,0:T(1,128)S(1)}) custom-call(s32[1]{0:T(128)} %bitcast.4.me_ref, bf16[32,2688]{1,0:T(8,128)(2,1)} %collective-permute-done.refs_0_, bf16[40,2688]{1,0:T(8,128)(2,1)} %collective-permute-done.1.refs_1_, bf16[32,2688]{1,0:T(8,128)(2,1)} %collective-permute-done.2.refs_2_, ...), custom_call_target="tpu_custom_call" | custom-call | flops 754974720 | bytes 5242880 | tf_op jit(solution)/shard_map/pallas_call | solution.py:155
  60.1 2.1 %collective-permute-start.13 = (bf16[40,2688]{1,0:T(8,128)(2,1)}, bf16[40,2688]{1,0:T(8,128)(2,1)S(1)}, u32[]{:S(2)}, u32[]{:S(2)}) collective-permute-start(bf16[40,2688]{1,0:T(8,128)(2,1)} %collective-permute-done.8.refs_1_), channel_id=1, source_target_pairs={{0,4},{4,8},{8,12},{12,14},{14,10},{10,6},{6,2},{2,0},{1,5},{5,9},... | collective-permute-start | bytes 645128 | tf_op jit(solution)/shard_map/ppermute | solution.py:354
  63.3 2.5 %copy-done.2 = bf16[16,64,2560]{2,1,0:T(8,128)(2,1)S(1)} copy-done((bf16[16,64,2560]{2,1,0:T(8,128)(2,1)S(1)}, bf16[16,64,2560]{2,1,0:T(8,128)(2,1)}, u32[]{:S(2)}) %copy-start.2) | copy-done | bytes 5242904
  68.8 1.9 %collective-permute-start.12 = (bf16[32,2688]{1,0:T(8,128)(2,1)S(1)}, bf16[32,2688]{1,0:T(8,128)(2,1)}, u32[]{:S(2)}, u32[]{:S(2)}) collective-permute-start(bf16[32,2688]{1,0:T(8,128)(2,1)S(1)} %copy-done.12), channel_id=1, source_target_pairs={{0,4},{4,8},{8,12},{12,14},{14,10},{10,6},{6,2},{2,0},{1,5},{5,9},... | collective-permute-start | bytes 516104 | tf_op jit(solution)/shard_map/ppermute | solution.py:354
  71.9 4.0 %all-to-all-start.1 = ((bf16[8,24,512]{2,1,0:T(8,128)(2,1)}), bf16[8,24,512]{2,1,0:T(8,128)(2,1)S(1)}, u32[]{:S(2)}, u32[]{:S(2)}) async-start(bf16[8,24,512]{2,1,0:T(8,128)(2,1)} %bitcast.9), calls=%async_computation.1 | async-start | bytes 393216 | tf_op jit(solution)/shard_map/all_to_all | solution.py:365
  76.0 2.5 %copy-done.3 = bf16[16,64,2560]{2,1,0:T(8,128)(2,1)S(1)} copy-done((bf16[16,64,2560]{2,1,0:T(8,128)(2,1)S(1)}, bf16[16,64,2560]{2,1,0:T(8,128)(2,1)}, u32[]{:S(2)}) %copy-start.3) | copy-done | bytes 5242904
  78.4 2.8 %shard_map.100 = (f32[64,144]{1,0:T(8,128)S(1)}, f32[1,144]{1,0:T(1,128)S(1)}) custom-call(s32[1]{0:T(128)} %bitcast.4.me_ref, bf16[32,2688]{1,0:T(8,128)(2,1)S(1)} %copy-done.12, bf16[40,2688]{1,0:T(8,128)(2,1)} %collective-permute-done.8.refs_1_, bf16[32,2688]{1,0:T(8,128)(2,1)} %collective-permute-done.9.refs_2_, ...), custom_call_target="tpu_custom_call" | custom-call | flops 754974720 | bytes 5242880 | tf_op jit(solution)/shard_map/pallas_call | solution.py:155
  84.2 2.1 %collective-permute-start.18 = (bf16[40,2688]{1,0:T(8,128)(2,1)S(1)}, bf16[40,2688]{1,0:T(8,128)(2,1)S(1)}, u32[]{:S(2)}, u32[]{:S(2)}) collective-permute-start(bf16[40,2688]{1,0:T(8,128)(2,1)S(1)} %collective-permute-done.15.refs_3_), channel_id=1, source_target_pairs={{4,0},{8,4},{12,8},{14,12},{10,14},{6,10},{2,6},{0,2},{5,1},{9,5},... | collective-permute-start | bytes 645128 | tf_op jit(solution)/shard_map/ppermute | solution.py:357
  86.4 2.5 %shard_map.102 = (f32[64,144]{1,0:T(8,128)S(1)}, f32[1,144]{1,0:T(1,128)S(1)}) custom-call(s32[1]{0:T(128)} %bitcast.4.me_ref, bf16[32,2688]{1,0:T(8,128)(2,1)} %collective-permute-done.12.refs_0_, bf16[40,2688]{1,0:T(8,128)(2,1)S(1)} %collective-permute-done.13.refs_1_, bf16[32,2688]{1,0:T(8,128)(2,1)} %collective-permute-done.14.refs_2_, ...), custom_call_target="tpu_custom_call" | custom-call | flops 754974720 | bytes 5242880 | tf_op jit(solution)/shard_map/pallas_call | solution.py:155
  95.5 1.6 %shard_map.105 = bf16[8,72,512]{2,1,0:T(8,128)(2,1)} custom-call(s32[1]{0:T(128)} %bitcast.11.to_ref, f32[64,72]{1,0:T(8,128)S(1)} %get-tuple-element.67.own_ref, f32[64,72]{1,0:T(8,128)S(1)} %collective-permute-done.20.other_ref, f32[1,72]{1,0:T(1,128)S(1)} %get-tuple-element.68.local_ref, ...), custom_call_target="tpu_custom_call", output_to_operand_aliasing={{}: (5, {})} | custom-call | flops 75497472 | bytes 1048576 | tf_op jit(solution)/shard_map/pallas_call | solution.py:230
  97.1 5.1 %all-to-all-start.2 = ((bf16[8,72,512]{2,1,0:T(8,128)(2,1)}), bf16[8,72,512]{2,1,0:T(8,128)(2,1)S(1)}, u32[]{:S(2)}, u32[]{:S(2)}) async-start(bf16[8,72,512]{2,1,0:T(8,128)(2,1)} %shard_map.105), calls=%async_computation.2 | async-start | bytes 1179648 | tf_op jit(solution)/shard_map/all_to_all | solution.py:397
  104.6 13.8 %all-to-all-done.2.hot_ref = bf16[8,72,512]{2,1,0:T(8,128)(2,1)S(1)} async-done(((bf16[8,72,512]{2,1,0:T(8,128)(2,1)}), bf16[8,72,512]{2,1,0:T(8,128)(2,1)S(1)}, u32[]{:S(2)}, u32[]{:S(2)}) %all-to-all-start.2) | async-done | bytes 589856 | tf_op jit(solution)/shard_map/all_to_all | solution.py:397
  118.4 1.9 %shard_map.106 = bf16[256,512]{1,0:T(8,128)(2,1)} custom-call(s32[1]{0:T(128)} %bitcast.2.busy_ref, f32[256,512]{1,0:T(8,128)S(1)} %shard_map.97.keys_ref, bf16[8,72,512]{2,1,0:T(8,128)(2,1)S(1)} %all-to-all-done.2.hot_ref, s32[256,1]{1,0:T(8,128)S(1)} %copy-done.9, f32[1,128]{1,0:T(1,128)S(1)} %bitcast.37, f32[256,128]{1,0:T(8,128)S(1)} %get-tuple-element.79.cos_ref, ...), custom_call_target="tpu_custom_call" | custom-call | tf_op jit(solution)/shard_map/pallas_call | solution.py:289
  (94 shorter events, 31.9 us)
Async XLA Ops:
  6.9 55.4 %all-to-all-start = ((bf16[8,24,2688]{2,1,0:T(8,128)(2,1)}), bf16[8,24,2688]{2,1,0:T(8,128)(2,1)S(1)}, u32[]{:S(2)}, u32[]{:S(2)}) async-start(bf16[8,24,2688]{2,1,0:T(8,128)(2,1)} %bitcast.7), calls=%async_computation | async-start | bytes 2064384 | tf_op jit(solution)/shard_map/all_to_all | solution.py:365
  14.1 20.0 %collective-permute-start.2 = (bf16[32,2688]{1,0:T(8,128)(2,1)}, bf16[32,2688]{1,0:T(8,128)(2,1)}, u32[]{:S(2)}, u32[]{:S(2)}) collective-permute-start(bf16[32,2688]{1,0:T(8,128)(2,1)} %get-tuple-element.38.refs_0_), channel_id=1, source_target_pairs={{4,0},{8,4},{12,8},{14,12},{10,14},{6,10},{2,6},{0,2},{5,1},{9,5},... | collective-permute-start | bytes 516104 | tf_op jit(solution)/shard_map/ppermute | solution.py:357
  16.1 19.7 %collective-permute-start = (bf16[32,2688]{1,0:T(8,128)(2,1)}, bf16[32,2688]{1,0:T(8,128)(2,1)}, u32[]{:S(2)}, u32[]{:S(2)}) collective-permute-start(bf16[32,2688]{1,0:T(8,128)(2,1)} %get-tuple-element.38.refs_0_), channel_id=1, source_target_pairs={{0,4},{4,8},{8,12},{12,14},{14,10},{10,6},{6,2},{2,0},{1,5},{5,9},... | collective-permute-start | bytes 516104 | tf_op jit(solution)/shard_map/ppermute | solution.py:354
  16.2 25.3 %collective-permute-start.3 = (bf16[40,2688]{1,0:T(8,128)(2,1)}, bf16[40,2688]{1,0:T(8,128)(2,1)}, u32[]{:S(2)}, u32[]{:S(2)}) collective-permute-start(bf16[40,2688]{1,0:T(8,128)(2,1)} %get-tuple-element.39.refs_1_), channel_id=1, source_target_pairs={{4,0},{8,4},{12,8},{14,12},{10,14},{6,10},{2,6},{0,2},{5,1},{9,5},... | collective-permute-start | bytes 645128 | tf_op jit(solution)/shard_map/ppermute | solution.py:357
  18.2 23.3 %collective-permute-start.1 = (bf16[40,2688]{1,0:T(8,128)(2,1)}, bf16[40,2688]{1,0:T(8,128)(2,1)}, u32[]{:S(2)}, u32[]{:S(2)}) collective-permute-start(bf16[40,2688]{1,0:T(8,128)(2,1)} %get-tuple-element.39.refs_1_), channel_id=1, source_target_pairs={{0,4},{4,8},{8,12},{12,14},{14,10},{10,6},{6,2},{2,0},{1,5},{5,9},... | collective-permute-start | bytes 645128 | tf_op jit(solution)/shard_map/ppermute | solution.py:354
  24.1 2.1 %collective-permute-start.4 = (f32[64,72]{1,0:T(8,128)S(1)}, f32[64,72]{1,0:T(8,128)S(1)}, u32[]{:S(2)}, u32[]{:S(2)}) collective-permute-start(f32[64,72]{1,0:T(8,128)S(1)} %get-tuple-element.40.own_ref), channel_id=1, source_target_pairs={{0,1},{1,0},{2,3},{3,2},{4,5},{5,4},{6,7},{7,6},{8,9},{9,8},{10,11... | collective-permute-start | bytes 55304 | tf_op jit(solution)/shard_map/ppermute | solution.py:312
  41.5 18.6 %collective-permute-start.7 = (bf16[32,2688]{1,0:T(8,128)(2,1)}, bf16[32,2688]{1,0:T(8,128)(2,1)S(1)}, u32[]{:S(2)}, u32[]{:S(2)}) collective-permute-start(bf16[32,2688]{1,0:T(8,128)(2,1)} %collective-permute-done.refs_0_), channel_id=1, source_target_pairs={{0,4},{4,8},{8,12},{12,14},{14,10},{10,6},{6,2},{2,0},{1,5},{5,9},... | collective-permute-start | bytes 516104 | tf_op jit(solution)/shard_map/ppermute | solution.py:354
  48.6 11.5 %collective-permute-start.9 = (bf16[32,2688]{1,0:T(8,128)(2,1)}, bf16[32,2688]{1,0:T(8,128)(2,1)}, u32[]{:S(2)}, u32[]{:S(2)}) collective-permute-start(bf16[32,2688]{1,0:T(8,128)(2,1)} %collective-permute-done.2.refs_2_), channel_id=1, source_target_pairs={{4,0},{8,4},{12,8},{14,12},{10,14},{6,10},{2,6},{0,2},{5,1},{9,5},... | collective-permute-start | bytes 516104 | tf_op jit(solution)/shard_map/ppermute | solution.py:357
  48.6 11.6 %collective-permute-start.8 = (bf16[40,2688]{1,0:T(8,128)(2,1)}, bf16[40,2688]{1,0:T(8,128)(2,1)}, u32[]{:S(2)}, u32[]{:S(2)}) collective-permute-start(bf16[40,2688]{1,0:T(8,128)(2,1)} %collective-permute-done.1.refs_1_), channel_id=1, source_target_pairs={{0,4},{4,8},{8,12},{12,14},{14,10},{10,6},{6,2},{2,0},{1,5},{5,9},... | collective-permute-start | bytes 645128 | tf_op jit(solution)/shard_map/ppermute | solution.py:354
  50.6 9.6 %collective-permute-start.10 = (bf16[40,2688]{1,0:T(8,128)(2,1)}, bf16[40,2688]{1,0:T(8,128)(2,1)}, u32[]{:S(2)}, u32[]{:S(2)}) collective-permute-start(bf16[40,2688]{1,0:T(8,128)(2,1)} %collective-permute-done.3.refs_3_), channel_id=1, source_target_pairs={{4,0},{8,4},{12,8},{14,12},{10,14},{6,10},{2,6},{0,2},{5,1},{9,5},... | collective-permute-start | bytes 645128 | tf_op jit(solution)/shard_map/ppermute | solution.py:357
  56.0 2.5 %collective-permute-start.11 = (f32[64,144]{1,0:T(8,128)S(1)}, f32[64,144]{1,0:T(8,128)S(1)}, u32[]{:S(2)}, u32[]{:S(2)}) collective-permute-start(f32[64,144]{1,0:T(8,128)S(1)} %get-tuple-element.51.own_ref), channel_id=1, source_target_pairs={{0,1},{1,0},{2,3},{3,2},{4,5},{5,4},{6,7},{7,6},{8,9},{9,8},{10,11... | collective-permute-start | bytes 110600 | tf_op jit(solution)/shard_map/ppermute | solution.py:312
  60.1 24.0 %collective-permute-start.13 = (bf16[40,2688]{1,0:T(8,128)(2,1)}, bf16[40,2688]{1,0:T(8,128)(2,1)S(1)}, u32[]{:S(2)}, u32[]{:S(2)}) collective-permute-start(bf16[40,2688]{1,0:T(8,128)(2,1)} %collective-permute-done.8.refs_1_), channel_id=1, source_target_pairs={{0,4},{4,8},{8,12},{12,14},{14,10},{10,6},{6,2},{2,0},{1,5},{5,9},... | collective-permute-start | bytes 645128 | tf_op jit(solution)/shard_map/ppermute | solution.py:354
  62.2 22.0 %collective-permute-start.15 = (bf16[40,2688]{1,0:T(8,128)(2,1)}, bf16[40,2688]{1,0:T(8,128)(2,1)S(1)}, u32[]{:S(2)}, u32[]{:S(2)}) collective-permute-start(bf16[40,2688]{1,0:T(8,128)(2,1)} %collective-permute-done.10.refs_3_), channel_id=1, source_target_pairs={{4,0},{8,4},{12,8},{14,12},{10,14},{6,10},{2,6},{0,2},{5,1},{9,5},... | collective-permute-start | bytes 645128 | tf_op jit(solution)/shard_map/ppermute | solution.py:357
  68.6 2.3 %collective-permute-start.6 = (f32[64,192]{1,0:T(8,128)S(1)}, f32[64,192]{1,0:T(8,128)S(1)}, u32[]{:S(2)}, u32[]{:S(2)}) collective-permute-start(f32[64,192]{1,0:T(8,128)S(1)} %get-tuple-element.45.own_ref), channel_id=1, source_target_pairs={{0,1},{1,0},{2,3},{3,2},{4,5},{5,4},{6,7},{7,6},{8,9},{9,8},{10,11... | collective-permute-start | bytes 147464 | tf_op jit(solution)/shard_map/ppermute | solution.py:312
  68.8 15.4 %collective-permute-start.12 = (bf16[32,2688]{1,0:T(8,128)(2,1)S(1)}, bf16[32,2688]{1,0:T(8,128)(2,1)}, u32[]{:S(2)}, u32[]{:S(2)}) collective-permute-start(bf16[32,2688]{1,0:T(8,128)(2,1)S(1)} %copy-done.12), channel_id=1, source_target_pairs={{0,4},{4,8},{8,12},{12,14},{14,10},{10,6},{6,2},{2,0},{1,5},{5,9},... | collective-permute-start | bytes 516104 | tf_op jit(solution)/shard_map/ppermute | solution.py:354
  70.7 13.5 %collective-permute-start.14 = (bf16[32,2688]{1,0:T(8,128)(2,1)}, bf16[32,2688]{1,0:T(8,128)(2,1)}, u32[]{:S(2)}, u32[]{:S(2)}) collective-permute-start(bf16[32,2688]{1,0:T(8,128)(2,1)} %collective-permute-done.9.refs_2_), channel_id=1, source_target_pairs={{4,0},{8,4},{12,8},{14,12},{10,14},{6,10},{2,6},{0,2},{5,1},{9,5},... | collective-permute-start | bytes 516104 | tf_op jit(solution)/shard_map/ppermute | solution.py:357
  71.9 25.1 %all-to-all-start.1 = ((bf16[8,24,512]{2,1,0:T(8,128)(2,1)}), bf16[8,24,512]{2,1,0:T(8,128)(2,1)S(1)}, u32[]{:S(2)}, u32[]{:S(2)}) async-start(bf16[8,24,512]{2,1,0:T(8,128)(2,1)} %bitcast.9), calls=%async_computation.1 | async-start | bytes 393216 | tf_op jit(solution)/shard_map/all_to_all | solution.py:365
  81.3 1.3 %collective-permute-start.16 = (f32[64,144]{1,0:T(8,128)S(1)}, f32[64,144]{1,0:T(8,128)S(1)}, u32[]{:S(2)}, u32[]{:S(2)}) collective-permute-start(f32[64,144]{1,0:T(8,128)S(1)} %get-tuple-element.57.own_ref), channel_id=1, source_target_pairs={{0,1},{1,0},{2,3},{3,2},{4,5},{5,4},{6,7},{7,6},{8,9},{9,8},{10,11... | collective-permute-start | bytes 110600 | tf_op jit(solution)/shard_map/ppermute | solution.py:312
  84.2 8.5 %collective-permute-start.18 = (bf16[40,2688]{1,0:T(8,128)(2,1)S(1)}, bf16[40,2688]{1,0:T(8,128)(2,1)S(1)}, u32[]{:S(2)}, u32[]{:S(2)}) collective-permute-start(bf16[40,2688]{1,0:T(8,128)(2,1)S(1)} %collective-permute-done.15.refs_3_), channel_id=1, source_target_pairs={{4,0},{8,4},{12,8},{14,12},{10,14},{6,10},{2,6},{0,2},{5,1},{9,5},... | collective-permute-start | bytes 645128 | tf_op jit(solution)/shard_map/ppermute | solution.py:357
  86.3 6.4 %collective-permute-start.17 = (bf16[32,2688]{1,0:T(8,128)(2,1)}, bf16[32,2688]{1,0:T(8,128)(2,1)S(1)}, u32[]{:S(2)}, u32[]{:S(2)}) collective-permute-start(bf16[32,2688]{1,0:T(8,128)(2,1)} %collective-permute-done.12.refs_0_), channel_id=1, source_target_pairs={{0,4},{4,8},{8,12},{12,14},{14,10},{10,6},{6,2},{2,0},{1,5},{5,9},... | collective-permute-start | bytes 516104 | tf_op jit(solution)/shard_map/ppermute | solution.py:354
  88.9 1.3 %collective-permute-start.19 = (f32[64,144]{1,0:T(8,128)S(1)}, f32[64,144]{1,0:T(8,128)S(1)}, u32[]{:S(2)}, u32[]{:S(2)}) collective-permute-start(f32[64,144]{1,0:T(8,128)S(1)} %get-tuple-element.63.own_ref), channel_id=1, source_target_pairs={{0,1},{1,0},{2,3},{3,2},{4,5},{5,4},{6,7},{7,6},{8,9},{9,8},{10,11... | collective-permute-start | bytes 110600 | tf_op jit(solution)/shard_map/ppermute | solution.py:312
  94.2 1.3 %collective-permute-start.20 = (f32[64,72]{1,0:T(8,128)S(1)}, f32[64,72]{1,0:T(8,128)S(1)}, u32[]{:S(2)}, u32[]{:S(2)}) collective-permute-start(f32[64,72]{1,0:T(8,128)S(1)} %get-tuple-element.67.own_ref), channel_id=1, source_target_pairs={{0,1},{1,0},{2,3},{3,2},{4,5},{5,4},{6,7},{7,6},{8,9},{9,8},{10,11... | collective-permute-start | bytes 55304 | tf_op jit(solution)/shard_map/ppermute | solution.py:312
  97.1 21.3 %all-to-all-start.2 = ((bf16[8,72,512]{2,1,0:T(8,128)(2,1)}), bf16[8,72,512]{2,1,0:T(8,128)(2,1)S(1)}, u32[]{:S(2)}, u32[]{:S(2)}) async-start(bf16[8,72,512]{2,1,0:T(8,128)(2,1)} %shard_map.105), calls=%async_computation.2 | async-start | bytes 1179648 | tf_op jit(solution)/shard_map/all_to_all | solution.py:397
  102.2 2.1 %collective-permute-start.5 = (f32[256,512]{1,0:T(8,128)}, f32[256,512]{1,0:T(8,128)S(1)}, u32[]{:S(2)}, u32[]{:S(2)}) collective-permute-start(f32[256,512]{1,0:T(8,128)} %get-tuple-element.69), channel_id=1, source_target_pairs={{0,1},{1,0},{2,3},{3,2},{4,5},{5,4},{6,7},{7,6},{8,9},{9,8},{10,11... | collective-permute-start | bytes 1572872 | tf_op jit(solution)/shard_map/ppermute | solution.py:312
  (22 other events, 179.3 us)

commit v5 on v4

v5 whole, which is shorter than its diff:
```python
import functools

import jax
import jax.numpy as jnp
from jax import lax
from jax.experimental import pallas as pl
from jax.experimental.pallas import tpu as pltpu
from jax.sharding import PartitionSpec as P

rope_theta = 1000000.0
LANES = 128
EXTRA = 128
HOT_PARTS = 3
ALL_VMEM = 60 * 1024 * 1024
LITTLE = pl.CostEstimate(flops=1, bytes_accessed=1, transcendentals=0)
SOME_VMEM = 32 * 1024 * 1024


def whole():
    return pl.BlockSpec(memory_space=pltpu.VMEM)


def scalars():
    return pl.BlockSpec(memory_space=pltpu.SMEM)


def params(limit=SOME_VMEM):
    return pltpu.CompilerParams(vmem_limit_bytes=limit)


def ring_order(owners):
    return [i for i in range(0, owners, 2)] + [i for i in range(owners - 1, 0, -2)]


def to_column(row):
    count = row.shape[1]
    square = lax.broadcasted_iota(jnp.int32, (count, count), 0) == lax.broadcasted_iota(
        jnp.int32, (count, count), 1
    )
    return jnp.sum(jnp.where(square, row, 0), axis=1, keepdims=True)


def spot_of(index, owners):
    return jnp.where(index % 2 == 0, index // 2, owners - 1 - index // 2)


def routing(pick, owner_row, local_row):
    owner = jnp.sum(jnp.where(pick, owner_row + 1, 0), axis=1, keepdims=True) - 1
    local = jnp.sum(jnp.where(pick, local_row, 0), axis=1, keepdims=True)
    lane = lax.broadcasted_iota(jnp.int32, (pick.shape[0], EXTRA), 1)
    return jnp.where(lane == 0, owner, jnp.where(lane == 1, local, 0)).astype(jnp.float32)


def route_kernel(stored, owners, share, me_ref, request_ref, table_ref, tokens_hbm, hot_ref, *refs):
    cold_refs = refs[:owners]
    place_ref, busy_ref, tokens_ref, sem = refs[owners:]
    fetch = pltpu.make_async_copy(tokens_hbm, tokens_ref, sem)
    fetch.start()
    count = request_ref.shape[1]
    request_col = to_column(request_ref[...])
    adapters = table_ref.shape[1]
    match = request_col == lax.broadcasted_iota(jnp.int32, (count, adapters), 1)
    slot_col = jnp.sum(jnp.where(match, table_ref[...], 0), axis=1, keepdims=True)
    row_id = lax.broadcasted_iota(jnp.int32, (count, count), 0)
    col_id = lax.broadcasted_iota(jnp.int32, (count, count), 1)
    slot_row = jnp.sum(jnp.where(row_id == col_id, slot_col, 0), axis=0, keepdims=True)
    owner_col = slot_col // stored
    owner_row = slot_row // stored
    same = owner_col == owner_row
    rank_col = jnp.sum(jnp.where(same & (col_id < row_id), 1, 0), axis=1, keepdims=True)
    rank_row = jnp.sum(jnp.where(same & (row_id < col_id), 1, 0), axis=0, keepdims=True)
    cold_total = owners * share

    def place(owner, rank):
        return jnp.where(rank < share, owner * share + rank, cold_total + rank - share)

    place_ref[...] = place(owner_col, rank_col)
    busy_ref[...] = jnp.max(jnp.where(rank_row >= share, owner_row, 0), axis=1, keepdims=True)
    place_row = place(owner_row, rank_row)
    local_row = slot_row - owner_row * stored
    fetch.wait()
    width = tokens_ref.shape[1]
    hot = place_row - cold_total == lax.broadcasted_iota(jnp.int32, (hot_ref.shape[0], count), 0)
    hot_ref[:, :width] = jnp.dot(
        hot.astype(jnp.float32).astype(jnp.bfloat16), tokens_ref[...], preferred_element_type=jnp.float32
    ).astype(jnp.bfloat16)
    hot_ref[:, width:] = routing(hot, owner_row, local_row).astype(jnp.bfloat16)
    distance = (spot_of(owner_row, owners) - spot_of(me_ref[0], owners) + owners) % owners
    place_row = jnp.where(rank_row < share, distance * share + rank_row, -1)
    pick = place_row == lax.broadcasted_iota(jnp.int32, (cold_total, count), 0)
    rows = jnp.dot(
        pick.astype(jnp.float32).astype(jnp.bfloat16), tokens_ref[...], preferred_element_type=jnp.float32
    )
    extra = routing(pick, owner_row, local_row)
    for k, out_ref in enumerate(cold_refs):
        out_ref[:, :width] = rows[k * share : (k + 1) * share].astype(jnp.bfloat16)
        out_ref[:, width:] = extra[k * share : (k + 1) * share].astype(jnp.bfloat16)


def route(me, request, table, tokens, stored, owners, share):
    count, width = tokens.shape
    packed = [HOT_PARTS * share] + [share] * owners
    outs = pl.pallas_call(
        functools.partial(route_kernel, stored, owners, share),
        out_shape=(
            *(jax.ShapeDtypeStruct((n, width + EXTRA), jnp.bfloat16) for n in packed),
            jax.ShapeDtypeStruct((count, 1), jnp.int32),
            jax.ShapeDtypeStruct((1, 1), jnp.int32),
        ),
        in_specs=[scalars(), whole(), whole(), pl.BlockSpec(memory_space=pl.ANY)],
        out_specs=(whole(),) * (len(packed) + 2),
        scratch_shapes=[pltpu.VMEM((count, width), jnp.bfloat16), pltpu.SemaphoreType.DMA],
        compiler_params=params(ALL_VMEM),
    )(me, request.reshape(1, -1), table.reshape(1, -1), tokens)
    return outs[0], outs[1 : owners + 1], outs[-2], outs[-1]


def fetch_rows(source, target, sems):
    pieces = sems.shape[0]
    size = source.shape[0] // pieces
    copies = []
    for k in range(pieces):
        part = pl.ds(k * size, size)
        copies.append(pltpu.make_async_copy(source.at[part], target.at[part], sems.at[k]))
        copies[-1].start()
    return copies, size


def base_kernel(side_ref, tokens_ref, weight_hbm, own_ref, other_ref, weight, sems):
    half = own_ref.shape[1]
    copies, size = fetch_rows(weight_hbm, weight, sems)
    total = None
    for k, copy in enumerate(copies):
        copy.wait()
        part = jnp.dot(
            tokens_ref[:, k * size : (k + 1) * size],
            weight[k * size : (k + 1) * size, :],
            preferred_element_type=jnp.float32,
        )
        total = part if total is None else total + part

    @pl.when(side_ref[0] == 0)
    def _():
        own_ref[...] = total[:, :half]
        other_ref[...] = total[:, half:]

    @pl.when(side_ref[0] != 0)
    def _():
        own_ref[...] = total[:, half:]
        other_ref[...] = total[:, :half]


def base_product(side, tokens, weight):
    half = jax.ShapeDtypeStruct((tokens.shape[0], weight.shape[1] // 2), jnp.float32)
    return pl.pallas_call(
        base_kernel,
        in_specs=[scalars(), whole(), pl.BlockSpec(memory_space=pltpu.HBM)],
        out_specs=(whole(), whole()),
        out_shape=(half, half),
        scratch_shapes=[pltpu.VMEM(weight.shape, weight.dtype), pltpu.SemaphoreType.DMA((5,))],
        compiler_params=params(),
        cost_estimate=LITTLE,
    )(side, tokens, weight)


def keep_kernel(table_ref, out_ref, sem):
    copy = pltpu.make_async_copy(table_ref, out_ref, sem)
    copy.start()
    copy.wait()


def keep(table):
    return pl.pallas_call(
        keep_kernel,
        in_specs=[pl.BlockSpec(memory_space=pl.ANY)],
        out_specs=whole(),
        out_shape=pltpu.VMEM(table.shape, table.dtype),
        scratch_shapes=[pltpu.SemaphoreType.DMA],
        compiler_params=params(),
        cost_estimate=LITTLE,
    )(table)


def down_kernel(rank, parts, me_ref, *refs):
    rows_refs = refs[:parts]
    weight_ref, out_ref, local_ref = refs[parts:]
    width = weight_ref.shape[1]
    extra = jnp.concatenate([r[:, width:].astype(jnp.float32) for r in rows_refs], axis=0).T
    local = jnp.where(extra[0:1] == me_ref[0].astype(jnp.float32), extra[1:2], -1.0)
    rows = jnp.concatenate([r[:, :width] for r in rows_refs], axis=0)
    block = 4 * rank
    out = jnp.zeros(out_ref.shape, jnp.float32)
    for first in range(0, weight_ref.shape[0], block):
        product = lax.dot_general(
            weight_ref[first : first + block, :],
            rows,
            (((1,), (1,)), ((), ())),
            preferred_element_type=jnp.float32,
        )
        for j in range(block // rank):
            mine = local == float(first // rank + j)
            out = out + jnp.where(mine, product[j * rank : (j + 1) * rank, :], 0.0)
    out_ref[...] = out
    local_ref[...] = local


def down(me, row_arrays, table, rank):
    count = sum(r.shape[0] for r in row_arrays)
    return pl.pallas_call(
        functools.partial(down_kernel, rank, len(row_arrays)),
        in_specs=[scalars()] + [whole()] * (len(row_arrays) + 1),
        out_specs=(whole(), whole()),
        out_shape=(
            jax.ShapeDtypeStruct((rank, count), jnp.float32),
            jax.ShapeDtypeStruct((1, count), jnp.float32),
        ),
        compiler_params=params(),
        cost_estimate=LITTLE,
    )(me, *row_arrays, table)


def update(own_ref, other_ref, local_ref, weight_ref):
    rank, count = own_ref.shape
    pair = LANES // rank
    shrunk = (own_ref[...] + other_ref[...]).astype(jnp.bfloat16).astype(jnp.float32)
    doubled = jnp.concatenate([shrunk] * pair, axis=0).T
    local = jnp.broadcast_to(local_ref[...], (LANES, count)).T.astype(jnp.int32)
    lane_block = lax.broadcasted_iota(jnp.int32, (count, LANES), 1) // rank
    spread = jnp.concatenate(
        [
            jnp.where(lane_block + j * pair == local, doubled, 0.0).astype(jnp.bfloat16)
            for j in range(weight_ref.shape[0] // LANES)
        ],
        axis=1,
    )
    return jnp.dot(spread, weight_ref[...], preferred_element_type=jnp.float32)


def up_kernel(units, kept, to_ref, own_ref, other_ref, local_ref, weight_ref, *refs):
    out_ref, buffer, sems = refs[kept:]
    product = update(own_ref, other_ref, local_ref, weight_ref)
    share, features = buffer.shape[1:]
    copies = []
    for k, (place, column) in enumerate(units):
        buffer[k] = product[k * share : (k + 1) * share].astype(jnp.bfloat16)
        target = out_ref.at[to_ref[place], :, pl.ds(column * features, features)]
        copies.append(pltpu.make_async_copy(buffer.at[k], target, sems.at[k]))
        copies[-1].start()
    for copy in copies:
        copy.wait()


def up(targets, units, own, other, local, table, out):
    given = [] if isinstance(out, jax.ShapeDtypeStruct) else [out]
    anywhere = pl.BlockSpec(memory_space=pl.ANY)
    share = own.shape[1] // len(units)
    return pl.pallas_call(
        functools.partial(up_kernel, units, len(given)),
        in_specs=[scalars()] + [whole()] * 4 + [anywhere] * len(given),
        out_specs=anywhere,
        scratch_shapes=[
            pltpu.VMEM((len(units), share, table.shape[1]), jnp.bfloat16),
            pltpu.SemaphoreType.DMA((len(units),)),
        ],
        out_shape=jax.ShapeDtypeStruct(out.shape, jnp.bfloat16),
        input_output_aliases={5: 0} if given else {},
        compiler_params=params(),
        cost_estimate=LITTLE,
    )(targets, own, other, local, table, *given)


def finish_kernel(
    head, busy_ref, own_ref, other_ref, back_ref, place_ref, scale_ref, cos_ref, sin_ref, out_ref
):
    count, width = own_ref.shape
    owners, share, _ = back_ref.shape
    pieces = [back_ref[o, :, HOT_PARTS * width :].astype(jnp.float32) for o in range(owners)]
    pieces += [
        back_ref[busy_ref[0], :, c * width : (c + 1) * width].astype(jnp.float32)
        for c in range(HOT_PARTS)
    ]
    back = jnp.concatenate(pieces, axis=0).astype(jnp.bfloat16)
    chosen = place_ref[...] == lax.broadcasted_iota(jnp.int32, (count, back.shape[0]), 1)
    keys = (own_ref[...] + other_ref[...]) + jnp.dot(
        chosen.astype(jnp.float32).astype(jnp.bfloat16), back, preferred_element_type=jnp.float32
    )
    cosine = cos_ref[...]
    sine = sin_ref[...]
    for h in range(width // head):
        one = keys[:, h * head : (h + 1) * head]
        normed = (
            one
            * lax.rsqrt(jnp.mean(one * one, axis=-1, keepdims=True) + 1e-06)
            * scale_ref[...]
        )
        turned = pltpu.roll(normed, head // 2, 1)
        out_ref[:, h * head : (h + 1) * head] = (normed * cosine + turned * sine).astype(jnp.bfloat16)


def finish(busy, own, other, back, place, scale, cosine, sine):
    return pl.pallas_call(
        functools.partial(finish_kernel, scale.shape[0]),
        in_specs=[scalars()] + [whole()] * 7,
        out_specs=whole(),
        out_shape=jax.ShapeDtypeStruct(own.shape, jnp.bfloat16),
        compiler_params=params(),
    )(busy, own, other, back, place, scale.reshape(1, -1), cosine, sine)


def after(value, *earlier):
    return lax.optimization_barrier((value,) + earlier)[0]


def rope_tables(head, cached_token_length):
    half = head // 2
    inv_freq = rope_theta ** (-(jnp.arange(half, dtype=jnp.float32) * 2.0) / head)
    angles = cached_token_length.astype(jnp.float32)[:, None] * inv_freq[None, :]
    cosine = jnp.cos(angles)
    sine = jnp.sin(angles)
    return jnp.concatenate([cosine, cosine], axis=1), jnp.concatenate([-sine, sine], axis=1)


def swap(x):
    return lax.ppermute(x, "tensor", [(0, 1), (1, 0)])


def on_device(
    tokens,
    base_key_matrix,
    adapter_down_weight,
    adapter_up_weight,
    key_norm_scale,
    request_adapter,
    adapter_slot_table,
    cached_token_length,
):
    row_count, half_width = tokens.shape
    stored, rank, _ = adapter_down_weight.shape
    owners = lax.axis_size("dp")
    me = lax.axis_index("dp")
    side = lax.axis_index("tensor")
    share = (row_count + owners + 2) // (owners + 3)
    hot_count = HOT_PARTS * share
    down_table = adapter_down_weight.reshape(stored * rank, half_width)
    up_table = adapter_up_weight.reshape(stored * rank, -1)
    features = up_table.shape[1]

    here = me.reshape(1).astype(jnp.int32)
    hot, cold, place, busy = route(
        here, request_adapter, adapter_slot_table, tokens, stored, owners, share
    )

    ring = ring_order(owners)
    half_way = owners // 2

    def along(rows, distance):
        return lax.ppermute(
            rows, "dp", [(ring[i], ring[(i + distance) % owners]) for i in range(owners)]
        )

    distances = [0] + [d for s in range(1, half_way) for d in (s, -s)] + [half_way]
    sources = [[0] * (2 * owners) for _ in ring]
    for spot, index in enumerate(ring):
        sources[index] = [ring[(spot - d) % owners] for d in distances + list(range(owners))]
    order = lax.dynamic_index_in_dim(jnp.array(sources, jnp.int32), me, 0, keepdims=False)

    def product(rows):
        own, local = down(here, rows, down_table, rank)
        return own, swap(own), local

    group = [along(hot, 1), along(hot, -1)]
    waves = {d: [d, owners - d] for d in range(1, half_way)}
    waves[1] = waves[1] + [half_way]
    got = {0: cold[0]}
    for d in waves[1]:
        got[d] = along(cold[d], d)
    cut = hot_count // 2 // 16 * 16 if hot_count >= 32 else hot_count // 2

    def hot_units(first, blocks):
        return [(first + k, column) for k in range(blocks) for column in range(HOT_PARTS)]

    def cold_units(chosen):
        return [(owners + d, HOT_PARTS) for d in chosen]

    delta = jax.ShapeDtypeStruct((owners, share, (HOT_PARTS + 1) * features), jnp.bfloat16)
    down_table = keep(down_table)
    todo = [got[d] for d in waves[1]] + [down_table]
    for step in range(1, half_way):
        group = list(lax.optimization_barrier((*group, *todo))[:2])
        if step < half_way - 1:
            following = [along(group[0], 1), along(group[1], -1)]
            for d in waves[step + 1]:
                got[d] = along(after(cold[d], group[0]), d)
        else:
            following = [along(group[0][:cut], 1), along(group[1][cut:], -1)]
        rows, units = list(group), hot_units(2 * step - 1, 2)
        if step == 1:
            rows, units = [hot] + rows, hot_units(0, 3)
        if step == half_way - 2:
            chosen = [d for d in range(owners) if d not in waves[half_way - 1]]
        elif step == half_way - 1:
            chosen = waves[step]
        else:
            chosen = []
        rows += [got[d] for d in chosen]
        rows = lax.optimization_barrier((*rows, group[0]))[:-1]
        delta = up(order, units + cold_units(chosen), *product(list(rows)), up_table, delta)
        todo = [delta] + [got[d] for d in waves.get(step + 1, [])]
        group = following
    group = list(lax.optimization_barrier((*group, delta))[:2])
    last = product(group)
    delta = up(order, hot_units(owners - 1, 1), *last, up_table, delta)
    back = lax.all_to_all(delta, "dp", split_axis=0, concat_axis=0, tiled=True)
    base_own, base_give = base_product(
        side.reshape(1).astype(jnp.int32), after(tokens, last[0]), base_key_matrix
    )
    cosine, sine = rope_tables(key_norm_scale.shape[0], cached_token_length)
    return finish(
        busy.reshape(1), base_own, swap(base_give), back, place, key_norm_scale, cosine, sine
    )


def solution(mesh):
    placed = (
        P(("groups", "dp"), "tensor"),
        P("tensor", None),
        P(("groups", "dp"), None, "tensor"),
        P(("groups", "dp"), None, "tensor"),
        P(),
        P(("groups", "dp")),
        P("groups"),
        P(("groups", "dp")),
    )
    return jax.shard_map(
        on_device,
        mesh=mesh,
        in_specs=placed,
        out_specs=P(("groups", "dp"), "tensor"),
        check_vma=False,
    )
```

time: 121 us -> 101 us (0.83)
  local copies, waits for them, and re-layouts: 19.1 us -> 10.6 us
  starting transfers between devices: 36.4 us -> 29.6 us
  Pallas kernels: 28.8 us -> 23.4 us
  waiting for transfers between devices: 33.5 us -> 35.7 us
  matrix products: 1.51 us -> 0 us
    all_to_all x3 -> x1, starting transfers between devices: 16.4 us -> 3.69 us  [on_device(): back = lax.all_to_all(delta, 'dp', split_axis=0, concat_axis=0, tiled=True)]
    unnamed x44 -> x28, local copies, waits for them, and re-layouts: 16.2 us -> 9.81 us
    ppermute x14 -> x15, starting transfers between devices: 19.4 us -> 25.4 us  [along(): lax.ppermute(rows, 'dp', [(ring[i], ring[(i + distance) % owners]) for i...]
    pallas_call x6 -> x4, Pallas kernels: 12.8 us -> 8.45 us  [down(): pl.pallas_call(functools.partial(down_kernel, rank, len(row_arrays)), in_...]
    ppermute x14 -> x15, waiting for transfers between devices: 14.6 us -> 16.5 us  [along(): lax.ppermute(rows, 'dp', [(ring[i], ring[(i + distance) % owners]) for i...]
    dynamic_slice x2 -> x0, local copies, waits for them, and re-layouts: 1.68 us -> none  [the longest x1 0.89 us: on_device(): lax.dynamic_slice_in_dim(base, (1 - side) * features, features, 1)]
    dot_general x1 -> x0, matrix products: 1.51 us -> none  [on_device(): jnp.dot(after(tokens, group[0]), base_key_matrix, preferred_element_type=...]
    slice x2, local copies, waits for them, and re-layouts: 1.24 us -> 0.03 us  [on_device(): following = [along(group[0][:cut], 1), along(group[1][cut:], -1)]]
  transfers between devices with their start and end apart: 24 -> 21, of which waited for: 9 -> 13; matrix products, arithmetic and copies ran while one was open for 4% -> 1% of each run, Pallas kernels for 18% -> 15%
where the time goes in v5:
time: 101 us; the launch traced here: 100 us
  waiting for transfers between devices  35.7 us (35%)
  starting transfers between devices  29.6 us (29%)
  Pallas kernels  23.4 us (23%)
  local copies, waits for them, and re-layouts  10.6 us (10%)
    ppermute x15, starting transfers between devices, along(): lax.ppermute(rows, 'dp', [(ring[i], ring[(i + distance) % owners]) for i...  25.4 us
    ppermute x15, waiting for transfers between devices, along(): lax.ppermute(rows, 'dp', [(ring[i], ring[(i + distance) % owners]) for i...  16.5 us
    all_to_all x1, waiting for transfers between devices, on_device(): back = lax.all_to_all(delta, 'dp', split_axis=0, concat_axis=0, tiled=True)  14 us
    unnamed x28, local copies, waits for them, and re-layouts  9.81 us
    pallas_call x4, Pallas kernels, down(): pl.pallas_call(functools.partial(down_kernel, rank, len(row_arrays)), in_...  8.45 us
    pallas_call x4, Pallas kernels, up(): pl.pallas_call(functools.partial(up_kernel, units, len(given)), in_specs=...  6.85 us
    ppermute x5, waiting for transfers between devices, swap(): return lax.ppermute(x, 'tensor', [(0, 1), (1, 0)])  5.24 us
    all_to_all x1, starting transfers between devices, on_device(): back = lax.all_to_all(delta, 'dp', split_axis=0, concat_axis=0, tiled=True)  3.69 us
  transfers between devices with their start and end apart: 21, of which 13 were waited for; matrix products, arithmetic and copies ran while one was open for 1% of the time, Pallas kernels for 15%

profile of v5, /device:TPU:0, one launch (start us, length us, event | category | flops | bytes accessed | tf_op | source)
XLA Modules:
  0.0 100.3 jit_solution(9207255649545679253)
XLA Ops:
  0.0 3.6 %shard_map.91 = (bf16[72,2688]{1,0:T(8,128)(2,1)}, bf16[24,2688]{1,0:T(8,128)(2,1)}, bf16[24,2688]{1,0:T(8,128)(2,1)}, bf16[24,2688]{1,0:T(8,128)(2,1)}, bf16[24...) custom-call(s32[1]{0:T(128)} %bitcast.me_ref, ...), custom_call_target="tpu_custom_call" | custom-call | tf_op jit(solution)/shard_map/pallas_call | solution.py:103
  3.6 3.1 %collective-permute-start = (bf16[72,2688]{1,0:T(8,128)(2,1)}, bf16[72,2688]{1,0:T(8,128)(2,1)S(1)}, u32[]{:S(2)}, u32[]{:S(2)}) collective-permute-start(bf16[72,2688]{1,0:T(8,128)(2,1)} %get-tuple-element.61.refs_0_), channel_id=1, source_target_pairs={{0,4},{4,8},{8,12},{12,14},{14,10},{10,6},{6,2},{2,0},{1,5},{5,9},... | collective-permute-start | bytes 1161224 | tf_op jit(solution)/shard_map/ppermute | solution.py:357
  6.7 2.0 %collective-permute-start.2 = (bf16[24,2688]{1,0:T(8,128)(2,1)}, bf16[24,2688]{1,0:T(8,128)(2,1)S(1)}, u32[]{:S(2)}, u32[]{:S(2)}) collective-permute-start(bf16[24,2688]{1,0:T(8,128)(2,1)} %get-tuple-element.56), channel_id=1, source_target_pairs={{0,4},{4,8},{8,12},{12,14},{14,10},{10,6},{6,2},{2,0},{1,5},{5,9},... | collective-permute-start | bytes 387080 | tf_op jit(solution)/shard_map/ppermute | solution.py:357
  8.7 5.0 %collective-permute-start.4 = (bf16[24,2688]{1,0:T(8,128)(2,1)}, bf16[24,2688]{1,0:T(8,128)(2,1)S(1)}, u32[]{:S(2)}, u32[]{:S(2)}) collective-permute-start(bf16[24,2688]{1,0:T(8,128)(2,1)} %get-tuple-element.58), channel_id=1, source_target_pairs={{0,14},{4,10},{8,6},{12,2},{14,0},{10,4},{6,8},{2,12},{1,15},{5,11... | collective-permute-start | bytes 387080 | tf_op jit(solution)/shard_map/ppermute | solution.py:357
  13.7 2.5 %copy-done.4 = bf16[16,64,2560]{2,1,0:T(8,128)(2,1)S(1)} copy-done((bf16[16,64,2560]{2,1,0:T(8,128)(2,1)S(1)}, bf16[16,64,2560]{2,1,0:T(8,128)(2,1)}, u32[]{:S(2)}) %copy-start.4) | copy-done | bytes 5242904
  16.5 2.3 %copy-done = bf16[1024,2560]{1,0:T(8,128)(2,1)} copy-done((bf16[1024,2560]{1,0:T(8,128)(2,1)}, bf16[1024,2560]{1,0:T(8,128)(2,1)S(1)}, u32[]{:S(2)}) %copy-start) | copy-done | bytes 5242904
  20.1 4.5 %collective-permute-done.4.refs_5_ = bf16[24,2688]{1,0:T(8,128)(2,1)S(1)} collective-permute-done((bf16[24,2688]{1,0:T(8,128)(2,1)}, bf16[24,2688]{1,0:T(8,128)(2,1)S(1)}, u32[]{:S(2)}, u32[]{:S(2)}) %collective-permute-start.4) | collective-permute-done | bytes 129056 | tf_op jit(solution)/shard_map/ppermute | solution.py:357
  24.6 2.2 %collective-permute-start.5 = (bf16[72,2688]{1,0:T(8,128)(2,1)S(1)}, bf16[72,2688]{1,0:T(8,128)(2,1)S(1)}, u32[]{:S(2)}, u32[]{:S(2)}) collective-permute-start(bf16[72,2688]{1,0:T(8,128)(2,1)S(1)} %collective-permute-done.refs_1_), channel_id=1, source_target_pairs={{0,4},{4,8},{8,12},{12,14},{14,10},{10,6},{6,2},{2,0},{1,5},{5,9},... | collective-permute-start | bytes 1161224 | tf_op jit(solution)/shard_map/ppermute | solution.py:357
  26.8 3.2 %collective-permute-start.8 = (bf16[24,2688]{1,0:T(8,128)(2,1)}, bf16[24,2688]{1,0:T(8,128)(2,1)}, u32[]{:S(2)}, u32[]{:S(2)}) collective-permute-start(bf16[24,2688]{1,0:T(8,128)(2,1)} %get-tuple-element.67), channel_id=1, source_target_pairs={{0,8},{4,12},{8,14},{12,10},{14,6},{10,2},{6,0},{2,4},{1,9},{5,13}... | collective-permute-start | bytes 387080 | tf_op jit(solution)/shard_map/ppermute | solution.py:357
  30.1 2.5 %copy-done.1 = bf16[1024,2560]{1,0:T(8,128)(2,1)S(1)} copy-done((bf16[1024,2560]{1,0:T(8,128)(2,1)S(1)}, bf16[1024,2560]{1,0:T(8,128)(2,1)}, u32[]{:S(2)}) %copy-start.1) | copy-done | bytes 5242904
  35.5 1.7 %shard_map.94.refs_0_ = bf16[8,24,2048]{2,1,0:T(8,128)(2,1)} custom-call(s32[16]{0:T(128)S(1)} %dynamic-slice_bitcast_fusion.to_ref, f32[64,216]{1,0:T(8,128)S(1)} %get-tuple-element.64.own_ref, f32[64,216]{1,0:T(8,128)S(1)} %collective-permute-done.7.other_ref, f32[1,216]{1,0:T(1,128)S(1)} %get-tuple-element.65.local_ref, bf16[1024,512]{1,0:T(8,128)(2,1)S(1)} %bitcast.10), custom_call_target="tpu_custom_call" | custom-call | flops 1 | bytes 1 | tf_op jit(solution)/shard_map/pallas_call | solution.py:257
  37.3 2.6 %collective-permute-done.8.refs_4_ = bf16[24,2688]{1,0:T(8,128)(2,1)} collective-permute-done((bf16[24,2688]{1,0:T(8,128)(2,1)}, bf16[24,2688]{1,0:T(8,128)(2,1)}, u32[]{:S(2)}, u32[]{:S(2)}) %collective-permute-start.8) | collective-permute-done | bytes 129056 | tf_op jit(solution)/shard_map/ppermute | solution.py:357
  39.8 2.8 %collective-permute-done.9.refs_6_ = bf16[24,2688]{1,0:T(8,128)(2,1)} collective-permute-done((bf16[24,2688]{1,0:T(8,128)(2,1)}, bf16[24,2688]{1,0:T(8,128)(2,1)}, u32[]{:S(2)}, u32[]{:S(2)}) %collective-permute-start.9) | collective-permute-done | bytes 129056 | tf_op jit(solution)/shard_map/ppermute | solution.py:357
  46.4 2.1 %collective-permute-start.14 = (bf16[24,2688]{1,0:T(8,128)(2,1)S(1)}, bf16[24,2688]{1,0:T(8,128)(2,1)S(1)}, u32[]{:S(2)}, u32[]{:S(2)}) collective-permute-start(bf16[24,2688]{1,0:T(8,128)(2,1)S(1)} %copy-done.12), channel_id=1, source_target_pairs={{0,10},{4,6},{8,2},{12,0},{14,4},{10,8},{6,12},{2,14},{1,11},{5,7}... | collective-permute-start | bytes 387080 | tf_op jit(solution)/shard_map/ppermute | solution.py:357
  48.5 3.8 %shard_map.95 = (f32[64,288]{1,0:T(8,128)S(1)}, f32[1,288]{1,0:T(1,128)S(1)}) custom-call(s32[1]{0:T(128)} %bitcast.me_ref, bf16[72,2688]{1,0:T(8,128)(2,1)S(1)} %collective-permute-done.5.refs_0_, bf16[72,2688]{1,0:T(8,128)(2,1)S(1)} %collective-permute-done.6.refs_1_, bf16[24,2688]{1,0:T(8,128)(2,1)S(1)} %copy-done.9, ...), custom_call_target="tpu_custom_call" | custom-call | flops 1 | bytes 1 | tf_op jit(solution)/shard_map/pallas_call | solution.py:209
  53.7 1.9 %shard_map.96.refs_0_ = bf16[8,24,2048]{2,1,0:T(8,128)(2,1)} custom-call(s32[16]{0:T(128)S(1)} %dynamic-slice_bitcast_fusion.to_ref, f32[64,288]{1,0:T(8,128)S(1)} %get-tuple-element.81.own_ref, f32[64,288]{1,0:T(8,128)S(1)} %collective-permute-done.12.other_ref, f32[1,288]{1,0:T(1,128)S(1)} %get-tuple-element.82.local_ref, ...), custom_call_target="tpu_custom_call", output_to_operand_aliasing={{}: (5, {})} | custom-call | flops 1 | bytes 1 | tf_op jit(solution)/shard_map/pallas_call | solution.py:257
  55.6 4.5 %collective-permute-done.13.refs_2_ = bf16[24,2688]{1,0:T(8,128)(2,1)S(1)} collective-permute-done((bf16[24,2688]{1,0:T(8,128)(2,1)S(1)}, bf16[24,2688]{1,0:T(8,128)(2,1)S(1)}, u32[]{:S(2)}, u32[]{:S(2)}) %collective-permute-start.13) | collective-permute-done | bytes 129056 | tf_op jit(solution)/shard_map/ppermute | solution.py:357
  60.2 3.9 %collective-permute-start.16 = (bf16[40,2688]{1,0:T(8,128)(2,1)S(1)}, bf16[40,2688]{1,0:T(8,128)(2,1)S(1)}, u32[]{:S(2)}, u32[]{:S(2)}) collective-permute-start(bf16[40,2688]{1,0:T(8,128)(2,1)S(1)} %slice.7), channel_id=1, source_target_pairs={{0,2},{4,0},{8,4},{12,8},{14,12},{10,14},{6,10},{2,6},{1,3},{5,1},... | collective-permute-start | bytes 645128 | tf_op jit(solution)/shard_map/ppermute | solution.py:357
  67.0 1.7 %shard_map.98.refs_0_ = bf16[8,24,2048]{2,1,0:T(8,128)(2,1)} custom-call(s32[16]{0:T(128)S(1)} %dynamic-slice_bitcast_fusion.to_ref, f32[64,192]{1,0:T(8,128)S(1)} %get-tuple-element.93.own_ref, f32[64,192]{1,0:T(8,128)S(1)} %collective-permute-done.17.other_ref, f32[1,192]{1,0:T(1,128)S(1)} %get-tuple-element.94.local_ref, ...), custom_call_target="tpu_custom_call", output_to_operand_aliasing={{}: (5, {})} | custom-call | flops 1 | bytes 1 | tf_op jit(solution)/shard_map/pallas_call | solution.py:257
  73.9 3.7 %all-to-all-start = ((bf16[8,24,2048]{2,1,0:T(8,128)(2,1)}), bf16[8,24,2048]{2,1,0:T(8,128)(2,1)S(1)}, u32[]{:S(2)}, u32[]{:S(2)}) async-start(bf16[8,24,2048]{2,1,0:T(8,128)(2,1)} %shard_map.101), calls=%async_computation | async-start | bytes 1572864 | tf_op jit(solution)/shard_map/all_to_all | solution.py:413
  77.6 2.5 %copy-done.5 = bf16[2560,1024]{1,0:T(8,128)(2,1)S(1)} copy-done((bf16[2560,1024]{1,0:T(8,128)(2,1)S(1)}, bf16[2560,1024]{1,0:T(8,128)(2,1)}, u32[]{:S(2)}) %copy-start.5) | copy-done | bytes 5242904
  80.1 2.2 %shard_map.100 = (f32[256,512]{1,0:T(8,128)S(1)}, f32[256,512]{1,0:T(8,128)S(1)}) custom-call(s32[1]{0:T(128)} %bitcast.4.side_ref, bf16[256,2560]{1,0:T(8,128)(2,1)S(1)} %copy-done.6, bf16[2560,1024]{1,0:T(8,128)(2,1)S(1)} %copy-done.5), custom_call_target="tpu_custom_call" | custom-call | flops 1 | bytes 1 | tf_op jit(solution)/shard_map/pallas_call | solution.py:155
  84.3 14.0 %all-to-all-done.back_ref = bf16[8,24,2048]{2,1,0:T(8,128)(2,1)S(1)} async-done(((bf16[8,24,2048]{2,1,0:T(8,128)(2,1)}), bf16[8,24,2048]{2,1,0:T(8,128)(2,1)S(1)}, u32[]{:S(2)}, u32[]{:S(2)}) %all-to-all-start) | async-done | bytes 786464 | tf_op jit(solution)/shard_map/all_to_all | solution.py:413
  98.3 2.0 %shard_map.102 = bf16[256,512]{1,0:T(8,128)(2,1)} custom-call(s32[1]{0:T(128)} %bitcast.3.busy_ref, f32[256,512]{1,0:T(8,128)S(1)} %get-tuple-element.99.own_ref, f32[256,512]{1,0:T(8,128)S(1)} %collective-permute-done.18.other_ref, bf16[8,24,2048]{2,1,0:T(8,128)(2,1)S(1)} %all-to-all-done.back_ref, s32[256,1]{1,0:T(8,128)S(1)} %copy-done.8, ...), custom_call_target="tpu_custom_call" | custom-call | tf_op jit(solution)/shard_map/pallas_call | solution.py:301
  (65 shorter events, 19.7 us)
Async XLA Ops:
  3.6 21.0 %collective-permute-start = (bf16[72,2688]{1,0:T(8,128)(2,1)}, bf16[72,2688]{1,0:T(8,128)(2,1)S(1)}, u32[]{:S(2)}, u32[]{:S(2)}) collective-permute-start(bf16[72,2688]{1,0:T(8,128)(2,1)} %get-tuple-element.61.refs_0_), channel_id=1, source_target_pairs={{0,4},{4,8},{8,12},{12,14},{14,10},{10,6},{6,2},{2,0},{1,5},{5,9},... | collective-permute-start | bytes 1161224 | tf_op jit(solution)/shard_map/ppermute | solution.py:357
  6.7 17.9 %collective-permute-start.1 = (bf16[72,2688]{1,0:T(8,128)(2,1)}, bf16[72,2688]{1,0:T(8,128)(2,1)S(1)}, u32[]{:S(2)}, u32[]{:S(2)}) collective-permute-start(bf16[72,2688]{1,0:T(8,128)(2,1)} %get-tuple-element.61.refs_0_), channel_id=1, source_target_pairs={{0,2},{4,0},{8,4},{12,8},{14,12},{10,14},{6,10},{2,6},{1,3},{5,1},... | collective-permute-start | bytes 1161224 | tf_op jit(solution)/shard_map/ppermute | solution.py:357
  6.7 12.5 %collective-permute-start.2 = (bf16[24,2688]{1,0:T(8,128)(2,1)}, bf16[24,2688]{1,0:T(8,128)(2,1)S(1)}, u32[]{:S(2)}, u32[]{:S(2)}) collective-permute-start(bf16[24,2688]{1,0:T(8,128)(2,1)} %get-tuple-element.56), channel_id=1, source_target_pairs={{0,4},{4,8},{8,12},{12,14},{14,10},{10,6},{6,2},{2,0},{1,5},{5,9},... | collective-permute-start | bytes 387080 | tf_op jit(solution)/shard_map/ppermute | solution.py:357
  8.7 11.4 %collective-permute-start.3 = (bf16[24,2688]{1,0:T(8,128)(2,1)}, bf16[24,2688]{1,0:T(8,128)(2,1)S(1)}, u32[]{:S(2)}, u32[]{:S(2)}) collective-permute-start(bf16[24,2688]{1,0:T(8,128)(2,1)} %get-tuple-element.57), channel_id=1, source_target_pairs={{0,2},{4,0},{8,4},{12,8},{14,12},{10,14},{6,10},{2,6},{1,3},{5,1},... | collective-permute-start | bytes 387080 | tf_op jit(solution)/shard_map/ppermute | solution.py:357
  8.7 15.9 %collective-permute-start.4 = (bf16[24,2688]{1,0:T(8,128)(2,1)}, bf16[24,2688]{1,0:T(8,128)(2,1)S(1)}, u32[]{:S(2)}, u32[]{:S(2)}) collective-permute-start(bf16[24,2688]{1,0:T(8,128)(2,1)} %get-tuple-element.58), channel_id=1, source_target_pairs={{0,14},{4,10},{8,6},{12,2},{14,0},{10,4},{6,8},{2,12},{1,15},{5,11... | collective-permute-start | bytes 387080 | tf_op jit(solution)/shard_map/ppermute | solution.py:357
  16.2 32.4 %copy-start.9 = (bf16[24,2688]{1,0:T(8,128)(2,1)S(1)}, bf16[24,2688]{1,0:T(8,128)(2,1)}, u32[]{:S(2)}) copy-start(bf16[24,2688]{1,0:T(8,128)(2,1)} %get-tuple-element.75.refs_2_) | copy-start | bytes 387076
  24.6 18.0 %collective-permute-start.5 = (bf16[72,2688]{1,0:T(8,128)(2,1)S(1)}, bf16[72,2688]{1,0:T(8,128)(2,1)S(1)}, u32[]{:S(2)}, u32[]{:S(2)}) collective-permute-start(bf16[72,2688]{1,0:T(8,128)(2,1)S(1)} %collective-permute-done.refs_1_), channel_id=1, source_target_pairs={{0,4},{4,8},{8,12},{12,14},{14,10},{10,6},{6,2},{2,0},{1,5},{5,9},... | collective-permute-start | bytes 1161224 | tf_op jit(solution)/shard_map/ppermute | solution.py:357
  26.8 15.8 %collective-permute-start.6 = (bf16[72,2688]{1,0:T(8,128)(2,1)S(1)}, bf16[72,2688]{1,0:T(8,128)(2,1)S(1)}, u32[]{:S(2)}, u32[]{:S(2)}) collective-permute-start(bf16[72,2688]{1,0:T(8,128)(2,1)S(1)} %collective-permute-done.1.refs_2_), channel_id=1, source_target_pairs={{0,2},{4,0},{8,4},{12,8},{14,12},{10,14},{6,10},{2,6},{1,3},{5,1},... | collective-permute-start | bytes 1161224 | tf_op jit(solution)/shard_map/ppermute | solution.py:357
  26.8 13.0 %collective-permute-start.8 = (bf16[24,2688]{1,0:T(8,128)(2,1)}, bf16[24,2688]{1,0:T(8,128)(2,1)}, u32[]{:S(2)}, u32[]{:S(2)}) collective-permute-start(bf16[24,2688]{1,0:T(8,128)(2,1)} %get-tuple-element.67), channel_id=1, source_target_pairs={{0,8},{4,12},{8,14},{12,10},{14,6},{10,2},{6,0},{2,4},{1,9},{5,13}... | collective-permute-start | bytes 387080 | tf_op jit(solution)/shard_map/ppermute | solution.py:357
  30.0 12.6 %collective-permute-start.9 = (bf16[24,2688]{1,0:T(8,128)(2,1)}, bf16[24,2688]{1,0:T(8,128)(2,1)}, u32[]{:S(2)}, u32[]{:S(2)}) collective-permute-start(bf16[24,2688]{1,0:T(8,128)(2,1)} %get-tuple-element.69), channel_id=1, source_target_pairs={{0,6},{4,2},{8,0},{12,4},{14,8},{10,12},{6,14},{2,10},{1,7},{5,3},... | collective-permute-start | bytes 387080 | tf_op jit(solution)/shard_map/ppermute | solution.py:357
  34.2 1.3 %collective-permute-start.7 = (f32[64,216]{1,0:T(8,128)S(1)}, f32[64,216]{1,0:T(8,128)S(1)}, u32[]{:S(2)}, u32[]{:S(2)}) collective-permute-start(f32[64,216]{1,0:T(8,128)S(1)} %get-tuple-element.64.own_ref), channel_id=1, source_target_pairs={{0,1},{1,0},{2,3},{3,2},{4,5},{5,4},{6,7},{7,6},{8,9},{9,8},{10,11... | collective-permute-start | bytes 165896 | tf_op jit(solution)/shard_map/ppermute | solution.py:324
  42.7 17.5 %collective-permute-start.10 = (bf16[72,2688]{1,0:T(8,128)(2,1)S(1)}, bf16[72,2688]{1,0:T(8,128)(2,1)S(1)}, u32[]{:S(2)}, u32[]{:S(2)}) collective-permute-start(bf16[72,2688]{1,0:T(8,128)(2,1)S(1)} %collective-permute-done.5.refs_0_), channel_id=1, source_target_pairs={{0,4},{4,8},{8,12},{12,14},{14,10},{10,6},{6,2},{2,0},{1,5},{5,9},... | collective-permute-start | bytes 1161224 | tf_op jit(solution)/shard_map/ppermute | solution.py:357
  43.1 17.1 %collective-permute-start.11 = (bf16[72,2688]{1,0:T(8,128)(2,1)S(1)}, bf16[72,2688]{1,0:T(8,128)(2,1)S(1)}, u32[]{:S(2)}, u32[]{:S(2)}) collective-permute-start(bf16[72,2688]{1,0:T(8,128)(2,1)S(1)} %collective-permute-done.6.refs_1_), channel_id=1, source_target_pairs={{0,2},{4,0},{8,4},{12,8},{14,12},{10,14},{6,10},{2,6},{1,3},{5,1},... | collective-permute-start | bytes 1161224 | tf_op jit(solution)/shard_map/ppermute | solution.py:357
  44.7 15.5 %collective-permute-start.13 = (bf16[24,2688]{1,0:T(8,128)(2,1)S(1)}, bf16[24,2688]{1,0:T(8,128)(2,1)S(1)}, u32[]{:S(2)}, u32[]{:S(2)}) collective-permute-start(bf16[24,2688]{1,0:T(8,128)(2,1)S(1)} %copy-done.13), channel_id=1, source_target_pairs={{0,12},{4,14},{8,10},{12,6},{14,2},{10,0},{6,4},{2,8},{1,13},{5,15... | collective-permute-start | bytes 387080 | tf_op jit(solution)/shard_map/ppermute | solution.py:357
  46.4 13.8 %collective-permute-start.14 = (bf16[24,2688]{1,0:T(8,128)(2,1)S(1)}, bf16[24,2688]{1,0:T(8,128)(2,1)S(1)}, u32[]{:S(2)}, u32[]{:S(2)}) collective-permute-start(bf16[24,2688]{1,0:T(8,128)(2,1)S(1)} %copy-done.12), channel_id=1, source_target_pairs={{0,10},{4,6},{8,2},{12,0},{14,4},{10,8},{6,12},{2,14},{1,11},{5,7}... | collective-permute-start | bytes 387080 | tf_op jit(solution)/shard_map/ppermute | solution.py:357
  52.4 1.4 %collective-permute-start.12 = (f32[64,288]{1,0:T(8,128)S(1)}, f32[64,288]{1,0:T(8,128)S(1)}, u32[]{:S(2)}, u32[]{:S(2)}) collective-permute-start(f32[64,288]{1,0:T(8,128)S(1)} %get-tuple-element.81.own_ref), channel_id=1, source_target_pairs={{0,1},{1,0},{2,3},{3,2},{4,5},{5,4},{6,7},{7,6},{8,9},{9,8},{10,11... | collective-permute-start | bytes 221192 | tf_op jit(solution)/shard_map/ppermute | solution.py:324
  60.2 9.4 %collective-permute-start.16 = (bf16[40,2688]{1,0:T(8,128)(2,1)S(1)}, bf16[40,2688]{1,0:T(8,128)(2,1)S(1)}, u32[]{:S(2)}, u32[]{:S(2)}) collective-permute-start(bf16[40,2688]{1,0:T(8,128)(2,1)S(1)} %slice.7), channel_id=1, source_target_pairs={{0,2},{4,0},{8,4},{12,8},{14,12},{10,14},{6,10},{2,6},{1,3},{5,1},... | collective-permute-start | bytes 645128 | tf_op jit(solution)/shard_map/ppermute | solution.py:357
  64.1 5.5 %collective-permute-start.15 = (bf16[32,2688]{1,0:T(8,128)(2,1)S(1)}, bf16[32,2688]{1,0:T(8,128)(2,1)S(1)}, u32[]{:S(2)}, u32[]{:S(2)}) collective-permute-start(bf16[32,2688]{1,0:T(8,128)(2,1)S(1)} %slice.6), channel_id=1, source_target_pairs={{0,4},{4,8},{8,12},{12,14},{14,10},{10,6},{6,2},{2,0},{1,5},{5,9},... | collective-permute-start | bytes 516104 | tf_op jit(solution)/shard_map/ppermute | solution.py:357
  65.7 1.3 %collective-permute-start.17 = (f32[64,192]{1,0:T(8,128)S(1)}, f32[64,192]{1,0:T(8,128)S(1)}, u32[]{:S(2)}, u32[]{:S(2)}) collective-permute-start(f32[64,192]{1,0:T(8,128)S(1)} %get-tuple-element.93.own_ref), channel_id=1, source_target_pairs={{0,1},{1,0},{2,3},{3,2},{4,5},{5,4},{6,7},{7,6},{8,9},{9,8},{10,11... | collective-permute-start | bytes 147464 | tf_op jit(solution)/shard_map/ppermute | solution.py:324
  71.1 1.3 %collective-permute-start.19 = (f32[64,72]{1,0:T(8,128)S(1)}, f32[64,72]{1,0:T(8,128)S(1)}, u32[]{:S(2)}, u32[]{:S(2)}) collective-permute-start(f32[64,72]{1,0:T(8,128)S(1)} %get-tuple-element.97.own_ref), channel_id=1, source_target_pairs={{0,1},{1,0},{2,3},{3,2},{4,5},{5,4},{6,7},{7,6},{8,9},{9,8},{10,11... | collective-permute-start | bytes 55304 | tf_op jit(solution)/shard_map/ppermute | solution.py:324
  73.9 24.4 %copy-start.8 = (s32[256,1]{1,0:T(8,128)S(1)}, s32[256,1]{1,0:T(8,128)}, u32[]{:S(2)}) copy-start(s32[256,1]{1,0:T(8,128)} %get-tuple-element.102.place_ref) | copy-start | bytes 3076
  73.9 24.4 %copy-start.10 = (f32[128]{0:T(128)S(1)}, f32[128]{0:T(128)}, u32[]{:S(2)}) copy-start(f32[128]{0:T(128)} %param.13) | copy-start | bytes 1540
  73.9 24.4 %all-to-all-start = ((bf16[8,24,2048]{2,1,0:T(8,128)(2,1)}), bf16[8,24,2048]{2,1,0:T(8,128)(2,1)S(1)}, u32[]{:S(2)}, u32[]{:S(2)}) async-start(bf16[8,24,2048]{2,1,0:T(8,128)(2,1)} %shard_map.101), calls=%async_computation | async-start | bytes 1572864 | tf_op jit(solution)/shard_map/all_to_all | solution.py:413
  82.3 2.0 %collective-permute-start.18 = (f32[256,512]{1,0:T(8,128)S(1)}, f32[256,512]{1,0:T(8,128)S(1)}, u32[]{:S(2)}, u32[]{:S(2)}) collective-permute-start(f32[256,512]{1,0:T(8,128)S(1)} %get-tuple-element.100), channel_id=1, source_target_pairs={{0,1},{1,0},{2,3},{3,2},{4,5},{5,4},{6,7},{7,6},{8,9},{9,8},{10,11... | collective-permute-start | bytes 1572872 | tf_op jit(solution)/shard_map/ppermute | solution.py:324
  (11 other events, 103.9 us)

commit v6 on v5

--- a/solution.py
+++ b/solution.py
@@ -44,57 +44,45 @@
     return jnp.where(index % 2 == 0, index // 2, owners - 1 - index // 2)
 
 
-def routing(pick, owner_row, local_row):
-    owner = jnp.sum(jnp.where(pick, owner_row + 1, 0), axis=1, keepdims=True) - 1
-    local = jnp.sum(jnp.where(pick, local_row, 0), axis=1, keepdims=True)
-    lane = lax.broadcasted_iota(jnp.int32, (pick.shape[0], EXTRA), 1)
-    return jnp.where(lane == 0, owner, jnp.where(lane == 1, local, 0)).astype(jnp.float32)
-
-
 def route_kernel(stored, owners, share, me_ref, request_ref, table_ref, tokens_hbm, hot_ref, *refs):
     cold_refs = refs[:owners]
     place_ref, busy_ref, tokens_ref, sem = refs[owners:]
     fetch = pltpu.make_async_copy(tokens_hbm, tokens_ref, sem)
     fetch.start()
     count = request_ref.shape[1]
-    request_col = to_column(request_ref[...])
     adapters = table_ref.shape[1]
-    match = request_col == lax.broadcasted_iota(jnp.int32, (count, adapters), 1)
-    slot_col = jnp.sum(jnp.where(match, table_ref[...], 0), axis=1, keepdims=True)
+    table_col = to_column(table_ref[...])
+    match = request_ref[...] == lax.broadcasted_iota(jnp.int32, (adapters, count), 0)
+    slot_row = jnp.sum(jnp.where(match, table_col, 0), axis=0, keepdims=True)
+    slot_col = to_column(slot_row)
+    owner_col = slot_col // stored
+    owner_row = slot_row // stored
     row_id = lax.broadcasted_iota(jnp.int32, (count, count), 0)
     col_id = lax.broadcasted_iota(jnp.int32, (count, count), 1)
-    slot_row = jnp.sum(jnp.where(row_id == col_id, slot_col, 0), axis=0, keepdims=True)
-    owner_col = slot_col // stored
-    owner_row = slot_row // stored
-    same = owner_col == owner_row
-    rank_col = jnp.sum(jnp.where(same & (col_id < row_id), 1, 0), axis=1, keepdims=True)
-    rank_row = jnp.sum(jnp.where(same & (row_id < col_id), 1, 0), axis=0, keepdims=True)
+    earlier = (owner_col == owner_row) & (row_id < col_id)
+    rank_row = jnp.sum(jnp.where(earlier, 1, 0), axis=0, keepdims=True)
     cold_total = owners * share
-
-    def place(owner, rank):
-        return jnp.where(rank < share, owner * share + rank, cold_total + rank - share)
-
-    place_ref[...] = place(owner_col, rank_col)
+    place_ref[...] = jnp.where(
+        rank_row < share, owner_row * share + rank_row, cold_total + rank_row - share
+    )
     busy_ref[...] = jnp.max(jnp.where(rank_row >= share, owner_row, 0), axis=1, keepdims=True)
-    place_row = place(owner_row, rank_row)
-    local_row = slot_row - owner_row * stored
+    distance = (spot_of(owner_row, owners) - spot_of(me_ref[0], owners) + owners) % owners
+    position = jnp.where(rank_row < share, distance * share, cold_total - share) + rank_row
+    total = cold_total + hot_ref.shape[0]
+    pick = position == lax.broadcasted_iota(jnp.int32, (total, count), 0)
+    pick = pick.astype(jnp.float32).astype(jnp.bfloat16)
+    lane = lax.broadcasted_iota(jnp.int32, (count, EXTRA), 1)
+    beside = jnp.where(lane == 0, owner_col + 1, jnp.where(lane == 1, slot_col - owner_col * stored, 0))
+    beside = beside.astype(jnp.float32).astype(jnp.bfloat16)
+    width = tokens_ref.shape[1]
+    extra = jnp.dot(pick, beside, preferred_element_type=jnp.float32)
     fetch.wait()
-    width = tokens_ref.shape[1]
-    hot = place_row - cold_total == lax.broadcasted_iota(jnp.int32, (hot_ref.shape[0], count), 0)
-    hot_ref[:, :width] = jnp.dot(
-        hot.astype(jnp.float32).astype(jnp.bfloat16), tokens_ref[...], preferred_element_type=jnp.float32
-    ).astype(jnp.bfloat16)
-    hot_ref[:, width:] = routing(hot, owner_row, local_row).astype(jnp.bfloat16)
-    distance = (spot_of(owner_row, owners) - spot_of(me_ref[0], owners) + owners) % owners
-    place_row = jnp.where(rank_row < share, distance * share + rank_row, -1)
-    pick = place_row == lax.broadcasted_iota(jnp.int32, (cold_total, count), 0)
-    rows = jnp.dot(
-        pick.astype(jnp.float32).astype(jnp.bfloat16), tokens_ref[...], preferred_element_type=jnp.float32
-    )
-    extra = routing(pick, owner_row, local_row)
-    for k, out_ref in enumerate(cold_refs):
-        out_ref[:, :width] = rows[k * share : (k + 1) * share].astype(jnp.bfloat16)
-        out_ref[:, width:] = extra[k * share : (k + 1) * share].astype(jnp.bfloat16)
+    rows = jnp.dot(pick, tokens_ref[...], preferred_element_type=jnp.float32)
+    firsts = [cold_total] + [k * share for k in range(owners)]
+    for first, out_ref in zip(firsts, (hot_ref, *cold_refs)):
+        size = out_ref.shape[0]
+        out_ref[:, :width] = rows[first : first + size].astype(jnp.bfloat16)
+        out_ref[:, width:] = extra[first : first + size].astype(jnp.bfloat16)
 
 
 def route(me, request, table, tokens, stored, owners, share):
@@ -104,7 +92,7 @@
         functools.partial(route_kernel, stored, owners, share),
         out_shape=(
             *(jax.ShapeDtypeStruct((n, width + EXTRA), jnp.bfloat16) for n in packed),
-            jax.ShapeDtypeStruct((count, 1), jnp.int32),
+            jax.ShapeDtypeStruct((1, count), jnp.int32),
             jax.ShapeDtypeStruct((1, 1), jnp.int32),
         ),
         in_specs=[scalars(), whole(), whole(), pl.BlockSpec(memory_space=pl.ANY)],
@@ -126,9 +114,10 @@
     return copies, size
 
 
-def base_kernel(side_ref, tokens_ref, weight_hbm, own_ref, other_ref, weight, sems):
+def base_kernel(side_ref, tokens_ref, place_ref, weight_hbm, own_ref, other_ref, column_ref, weight, sems):
     half = own_ref.shape[1]
     copies, size = fetch_rows(weight_hbm, weight, sems)
+    column_ref[...] = to_column(place_ref[...])
     total = None
     for k, copy in enumerate(copies):
         copy.wait()
@@ -150,17 +139,18 @@
         other_ref[...] = total[:, :half]
 
 
-def base_product(side, tokens, weight):
+def base_product(side, tokens, place, weight):
+    column = jax.ShapeDtypeStruct((tokens.shape[0], 1), jnp.int32)
     half = jax.ShapeDtypeStruct((tokens.shape[0], weight.shape[1] // 2), jnp.float32)
     return pl.pallas_call(
         base_kernel,
-        in_specs=[scalars(), whole(), pl.BlockSpec(memory_space=pltpu.HBM)],
-        out_specs=(whole(), whole()),
-        out_shape=(half, half),
+        in_specs=[scalars(), whole(), whole(), pl.BlockSpec(memory_space=pltpu.HBM)],
+        out_specs=(whole(),) * 3,
+        out_shape=(half, half, column),
         scratch_shapes=[pltpu.VMEM(weight.shape, weight.dtype), pltpu.SemaphoreType.DMA((5,))],
         compiler_params=params(),
         cost_estimate=LITTLE,
-    )(side, tokens, weight)
+    )(side, tokens, place, weight)
 
 
 def keep_kernel(table_ref, out_ref, sem):
@@ -186,7 +176,7 @@
     weight_ref, out_ref, local_ref = refs[parts:]
     width = weight_ref.shape[1]
     extra = jnp.concatenate([r[:, width:].astype(jnp.float32) for r in rows_refs], axis=0).T
-    local = jnp.where(extra[0:1] == me_ref[0].astype(jnp.float32), extra[1:2], -1.0)
+    local = jnp.where(extra[0:1] == (me_ref[0] + 1).astype(jnp.float32), extra[1:2], -1.0)
     rows = jnp.concatenate([r[:, :width] for r in rows_refs], axis=0)
     block = 4 * rank
     out = jnp.zeros(out_ref.shape, jnp.float32)
@@ -270,15 +260,16 @@
 
 
 def finish_kernel(
-    head, busy_ref, own_ref, other_ref, back_ref, place_ref, scale_ref, cos_ref, sin_ref, out_ref
+    head, busy_ref, far_ref, own_ref, other_ref, back_ref, last_ref, place_ref, scale_ref, cos_ref, sin_ref, out_ref
 ):
     count, width = own_ref.shape
     owners, share, _ = back_ref.shape
     pieces = [back_ref[o, :, HOT_PARTS * width :].astype(jnp.float32) for o in range(owners)]
-    pieces += [
-        back_ref[busy_ref[0], :, c * width : (c + 1) * width].astype(jnp.float32)
-        for c in range(HOT_PARTS)
-    ]
+    from_far = busy_ref[0] == far_ref[0]
+    for c in range(HOT_PARTS):
+        columns = slice(c * width, (c + 1) * width)
+        near = back_ref[busy_ref[0], :, columns].astype(jnp.float32)
+        pieces.append(jnp.where(from_far, last_ref[0, :, columns].astype(jnp.float32), near))
     back = jnp.concatenate(pieces, axis=0).astype(jnp.bfloat16)
     chosen = place_ref[...] == lax.broadcasted_iota(jnp.int32, (count, back.shape[0]), 1)
     keys = (own_ref[...] + other_ref[...]) + jnp.dot(
@@ -297,14 +288,14 @@
         out_ref[:, h * head : (h + 1) * head] = (normed * cosine + turned * sine).astype(jnp.bfloat16)
 
 
-def finish(busy, own, other, back, place, scale, cosine, sine):
+def finish(busy, far, own, other, back, last, place, scale, cosine, sine):
     return pl.pallas_call(
         functools.partial(finish_kernel, scale.shape[0]),
-        in_specs=[scalars()] + [whole()] * 7,
+        in_specs=[scalars()] * 2 + [whole()] * 8,
         out_specs=whole(),
         out_shape=jax.ShapeDtypeStruct(own.shape, jnp.bfloat16),
         compiler_params=params(),
-    )(busy, own, other, back, place, scale.reshape(1, -1), cosine, sine)
+    )(busy, far, own, other, back, last, place, scale.reshape(1, -1), cosine, sine)
 
 
 def after(value, *earlier):
@@ -370,7 +361,7 @@
 
     group = [along(hot, 1), along(hot, -1)]
     waves = {d: [d, owners - d] for d in range(1, half_way)}
-    waves[1] = waves[1] + [half_way]
+    waves[half_way - 1] = waves[half_way - 1] + [half_way]
     got = {0: cold[0]}
     for d in waves[1]:
         got[d] = along(cold[d], d)
@@ -407,16 +398,30 @@
         delta = up(order, units + cold_units(chosen), *product(list(rows)), up_table, delta)
         todo = [delta] + [got[d] for d in waves.get(step + 1, [])]
         group = following
-    group = list(lax.optimization_barrier((*group, delta))[:2])
+    *group, delta = lax.optimization_barrier((*group, delta))
+    back = lax.all_to_all(delta, "dp", split_axis=0, concat_axis=0, tiled=True)
     last = product(group)
-    delta = up(order, hot_units(owners - 1, 1), *last, up_table, delta)
-    back = lax.all_to_all(delta, "dp", split_axis=0, concat_axis=0, tiled=True)
-    base_own, base_give = base_product(
-        side.reshape(1).astype(jnp.int32), after(tokens, last[0]), base_key_matrix
+    far_delta = jax.ShapeDtypeStruct((1, share, HOT_PARTS * features), jnp.bfloat16)
+    far_delta = up(
+        jnp.zeros((1,), jnp.int32), [(0, c) for c in range(HOT_PARTS)], *last, up_table, far_delta
+    )
+    tokens = after(tokens, far_delta)
+    far_delta = along(far_delta, half_way)
+    base_own, base_give, place = base_product(
+        side.reshape(1).astype(jnp.int32), tokens, place, base_key_matrix
     )
     cosine, sine = rope_tables(key_norm_scale.shape[0], cached_token_length)
     return finish(
-        busy.reshape(1), base_own, swap(base_give), back, place, key_norm_scale, cosine, sine
+        busy.reshape(1),
+        order[owners - 1 : owners],
+        base_own,
+        swap(base_give),
+        back,
+        far_delta,
+        place,
+        key_norm_scale,
+        cosine,
+        sine,
     )
 
 

time: 101 us -> 97.8 us (0.968)
  waiting for transfers between devices: 35.7 us -> 26.7 us
  local copies, waits for them, and re-layouts: 10.6 us -> 13.7 us
  starting transfers between devices: 29.6 us -> 31.6 us
    all_to_all x1, waiting for transfers between devices: 14 us -> 1.13 us  [on_device(): back = lax.all_to_all(delta, 'dp', split_axis=0, concat_axis=0, tiled=True)]
    ppermute x15 -> x16, waiting for transfers between devices: 16.5 us -> 22.4 us  [along(): lax.ppermute(rows, 'dp', [(ring[i], ring[(i + distance) % owners]) for i...]
    unnamed x28 -> x32, local copies, waits for them, and re-layouts: 9.81 us -> 12.3 us
    ppermute x5, waiting for transfers between devices: 5.24 us -> 3.2 us  [swap(): return lax.ppermute(x, 'tensor', [(0, 1), (1, 0)])]
    ppermute x15 -> x16, starting transfers between devices: 25.4 us -> 27 us  [along(): lax.ppermute(rows, 'dp', [(ring[i], ring[(i + distance) % owners]) for i...]
  transfers between devices with their start and end apart: 21 -> 22, of which waited for: 13 -> 11; matrix products, arithmetic and copies ran while one was open for 1% -> 2% of each run, Pallas kernels for 15% -> 19%
where the time goes in v6:
time: 97.8 us; the launch traced here: 97.3 us
  starting transfers between devices  31.6 us (32%)
  waiting for transfers between devices  26.7 us (27%)
  Pallas kernels  24.4 us (25%)
  local copies, waits for them, and re-layouts  13.7 us (14%)
    ppermute x16, starting transfers between devices, along(): lax.ppermute(rows, 'dp', [(ring[i], ring[(i + distance) % owners]) for i...  27 us
    ppermute x16, waiting for transfers between devices, along(): lax.ppermute(rows, 'dp', [(ring[i], ring[(i + distance) % owners]) for i...  22.4 us
    unnamed x32, local copies, waits for them, and re-layouts  12.3 us
    pallas_call x4, Pallas kernels, down(): pl.pallas_call(functools.partial(down_kernel, rank, len(row_arrays)), in_...  9.01 us
    pallas_call x4, Pallas kernels, up(): pl.pallas_call(functools.partial(up_kernel, units, len(given)), in_specs=...  6.48 us
    all_to_all x1, starting transfers between devices, on_device(): back = lax.all_to_all(delta, 'dp', split_axis=0, concat_axis=0, tiled=True)  4.06 us
    pallas_call x1, Pallas kernels, route(): pl.pallas_call(functools.partial(route_kernel, stored, owners, share), ou...  3.57 us
    ppermute x5, waiting for transfers between devices, swap(): return lax.ppermute(x, 'tensor', [(0, 1), (1, 0)])  3.2 us
  transfers between devices with their start and end apart: 22, of which 11 were waited for; matrix products, arithmetic and copies ran while one was open for 2% of the time, Pallas kernels for 19%

profile of v6, /device:TPU:0, one launch (start us, length us, event | category | flops | bytes accessed | tf_op | source)
XLA Modules:
  0.0 97.3 jit_solution(15623008329280807004)
XLA Ops:
  0.0 3.6 %shard_map.91 = (bf16[72,2688]{1,0:T(8,128)(2,1)}, bf16[24,2688]{1,0:T(8,128)(2,1)}, bf16[24,2688]{1,0:T(8,128)(2,1)}, bf16[24,2688]{1,0:T(8,128)(2,1)}, bf16[24...) custom-call(s32[1]{0:T(128)} %bitcast.me_ref, ...), custom_call_target="tpu_custom_call" | custom-call | tf_op jit(solution)/shard_map/pallas_call | solution.py:91
  3.6 3.1 %collective-permute-start = (bf16[72,2688]{1,0:T(8,128)(2,1)}, bf16[72,2688]{1,0:T(8,128)(2,1)S(1)}, u32[]{:S(2)}, u32[]{:S(2)}) collective-permute-start(bf16[72,2688]{1,0:T(8,128)(2,1)} %get-tuple-element.63.refs_0_), channel_id=1, source_target_pairs={{0,4},{4,8},{8,12},{12,14},{14,10},{10,6},{6,2},{2,0},{1,5},{5,9},... | collective-permute-start | bytes 1161224 | tf_op jit(solution)/shard_map/ppermute | solution.py:348
  6.7 2.0 %collective-permute-start.2 = (bf16[24,2688]{1,0:T(8,128)(2,1)}, bf16[24,2688]{1,0:T(8,128)(2,1)S(1)}, u32[]{:S(2)}, u32[]{:S(2)}) collective-permute-start(bf16[24,2688]{1,0:T(8,128)(2,1)} %get-tuple-element.59), channel_id=1, source_target_pairs={{0,4},{4,8},{8,12},{12,14},{14,10},{10,6},{6,2},{2,0},{1,5},{5,9},... | collective-permute-start | bytes 387080 | tf_op jit(solution)/shard_map/ppermute | solution.py:348
  8.7 2.5 %copy-done.5 = bf16[16,64,2560]{2,1,0:T(8,128)(2,1)S(1)} copy-done((bf16[16,64,2560]{2,1,0:T(8,128)(2,1)S(1)}, bf16[16,64,2560]{2,1,0:T(8,128)(2,1)}, u32[]{:S(2)}) %copy-start.5) | copy-done | bytes 5242904
  11.6 2.3 %copy-done = bf16[1024,2560]{1,0:T(8,128)(2,1)} copy-done((bf16[1024,2560]{1,0:T(8,128)(2,1)}, bf16[1024,2560]{1,0:T(8,128)(2,1)S(1)}, u32[]{:S(2)}) %copy-start) | copy-done | bytes 5242904
  13.9 4.6 %collective-permute-done.2.refs_3_ = bf16[24,2688]{1,0:T(8,128)(2,1)S(1)} collective-permute-done((bf16[24,2688]{1,0:T(8,128)(2,1)}, bf16[24,2688]{1,0:T(8,128)(2,1)S(1)}, u32[]{:S(2)}, u32[]{:S(2)}) %collective-permute-start.2) | collective-permute-done | bytes 129056 | tf_op jit(solution)/shard_map/ppermute | solution.py:348
  22.1 2.6 %collective-permute-start.7 = (bf16[24,2688]{1,0:T(8,128)(2,1)}, bf16[24,2688]{1,0:T(8,128)(2,1)S(1)}, u32[]{:S(2)}, u32[]{:S(2)}) collective-permute-start(bf16[24,2688]{1,0:T(8,128)(2,1)} %get-tuple-element.69), channel_id=1, source_target_pairs={{0,8},{4,12},{8,14},{12,10},{14,6},{10,2},{6,0},{2,4},{1,9},{5,13}... | collective-permute-start | bytes 387080 | tf_op jit(solution)/shard_map/ppermute | solution.py:348
  25.0 2.5 %copy-done.1 = bf16[1024,2560]{1,0:T(8,128)(2,1)S(1)} copy-done((bf16[1024,2560]{1,0:T(8,128)(2,1)S(1)}, bf16[1024,2560]{1,0:T(8,128)(2,1)}, u32[]{:S(2)}) %copy-start.1) | copy-done | bytes 5242904
  32.2 2.5 %collective-permute-done.7.refs_4_ = bf16[24,2688]{1,0:T(8,128)(2,1)S(1)} collective-permute-done((bf16[24,2688]{1,0:T(8,128)(2,1)}, bf16[24,2688]{1,0:T(8,128)(2,1)S(1)}, u32[]{:S(2)}, u32[]{:S(2)}) %collective-permute-start.7) | collective-permute-done | bytes 129056 | tf_op jit(solution)/shard_map/ppermute | solution.py:348
  36.3 1.8 %collective-permute-start.10 = (bf16[72,2688]{1,0:T(8,128)(2,1)S(1)}, bf16[72,2688]{1,0:T(8,128)(2,1)S(1)}, u32[]{:S(2)}, u32[]{:S(2)}) collective-permute-start(bf16[72,2688]{1,0:T(8,128)(2,1)S(1)} %collective-permute-done.5.refs_1_), channel_id=1, source_target_pairs={{0,2},{4,0},{8,4},{12,8},{14,12},{10,14},{6,10},{2,6},{1,3},{5,1},... | collective-permute-start | bytes 1161224 | tf_op jit(solution)/shard_map/ppermute | solution.py:348
  39.7 3.8 %shard_map.95 = (f32[64,264]{1,0:T(8,128)S(1)}, f32[1,264]{1,0:T(1,128)S(1)}) custom-call(s32[1]{0:T(128)} %bitcast.me_ref, bf16[72,2688]{1,0:T(8,128)(2,1)S(1)} %collective-permute-done.4.refs_0_, bf16[72,2688]{1,0:T(8,128)(2,1)S(1)} %collective-permute-done.5.refs_1_, bf16[24,2688]{1,0:T(8,128)(2,1)S(1)} %copy-done.9, ...), custom_call_target="tpu_custom_call" | custom-call | flops 1 | bytes 1 | tf_op jit(solution)/shard_map/pallas_call | solution.py:199
  45.2 2.3 %collective-permute-start.13 = (bf16[24,2688]{1,0:T(8,128)(2,1)S(1)}, bf16[24,2688]{1,0:T(8,128)(2,1)S(1)}, u32[]{:S(2)}, u32[]{:S(2)}) collective-permute-start(bf16[24,2688]{1,0:T(8,128)(2,1)S(1)} %copy-done.14), channel_id=1, source_target_pairs={{0,10},{4,6},{8,2},{12,0},{14,4},{10,8},{6,12},{2,14},{1,11},{5,7}... | collective-permute-start | bytes 387080 | tf_op jit(solution)/shard_map/ppermute | solution.py:348
  49.0 1.8 %shard_map.96.refs_0_ = bf16[8,24,2048]{2,1,0:T(8,128)(2,1)} custom-call(s32[16]{0:T(128)S(1)} %get-tuple-element.109.to_ref, f32[64,264]{1,0:T(8,128)S(1)} %get-tuple-element.82.own_ref, f32[64,264]{1,0:T(8,128)S(1)} %collective-permute-done.11.other_ref, f32[1,264]{1,0:T(1,128)S(1)} %get-tuple-element.83.local_ref, ...), custom_call_target="tpu_custom_call", output_to_operand_aliasing={{}: (5, {})} | custom-call | flops 1 | bytes 1 | tf_op jit(solution)/shard_map/pallas_call | solution.py:247
  50.8 8.6 %collective-permute-done.12.refs_2_ = bf16[24,2688]{1,0:T(8,128)(2,1)S(1)} collective-permute-done((bf16[24,2688]{1,0:T(8,128)(2,1)S(1)}, bf16[24,2688]{1,0:T(8,128)(2,1)S(1)}, u32[]{:S(2)}, u32[]{:S(2)}) %collective-permute-start.12) | collective-permute-done | bytes 129056 | tf_op jit(solution)/shard_map/ppermute | solution.py:348
  59.8 3.0 %collective-permute-start.15 = (bf16[32,2688]{1,0:T(8,128)(2,1)S(1)}, bf16[32,2688]{1,0:T(8,128)(2,1)S(1)}, u32[]{:S(2)}, u32[]{:S(2)}) collective-permute-start(bf16[32,2688]{1,0:T(8,128)(2,1)S(1)} %slice.14), channel_id=1, source_target_pairs={{0,4},{4,8},{8,12},{12,14},{14,10},{10,6},{6,2},{2,0},{1,5},{5,9},... | collective-permute-start | bytes 516104 | tf_op jit(solution)/shard_map/ppermute | solution.py:348
  65.7 1.8 %shard_map.98 = bf16[8,24,2048]{2,1,0:T(8,128)(2,1)} custom-call(s32[16]{0:T(128)S(1)} %get-tuple-element.109.to_ref, f32[64,216]{1,0:T(8,128)S(1)} %get-tuple-element.97.own_ref, f32[64,216]{1,0:T(8,128)S(1)} %collective-permute-done.17.other_ref, f32[1,216]{1,0:T(1,128)S(1)} %get-tuple-element.98.local_ref, ...), custom_call_target="tpu_custom_call", output_to_operand_aliasing={{}: (5, {})} | custom-call | flops 1 | bytes 1 | tf_op jit(solution)/shard_map/pallas_call | solution.py:247
  68.3 4.1 %all-to-all-start = ((bf16[8,24,2048]{2,1,0:T(8,128)(2,1)}), bf16[8,24,2048]{2,1,0:T(8,128)(2,1)S(1)}, u32[]{:S(2)}, u32[]{:S(2)}) async-start(bf16[8,24,2048]{2,1,0:T(8,128)(2,1)} %shard_map.98), calls=%async_computation | async-start | bytes 1572864 | tf_op jit(solution)/shard_map/all_to_all | solution.py:402
  72.3 2.5 %copy-done.3 = bf16[1024,2560]{1,0:T(8,128)(2,1)S(1)} copy-done((bf16[1024,2560]{1,0:T(8,128)(2,1)S(1)}, bf16[1024,2560]{1,0:T(8,128)(2,1)}, u32[]{:S(2)}) %copy-start.3) | copy-done | bytes 5242904
  74.8 2.1 %shard_map.99 = (f32[64,72]{1,0:T(8,128)}, f32[1,72]{1,0:T(1,128)S(1)}) custom-call(s32[1]{0:T(128)} %bitcast.me_ref, bf16[32,2688]{1,0:T(8,128)(2,1)S(1)} %collective-permute-done.15.refs_0_, bf16[40,2688]{1,0:T(8,128)(2,1)S(1)} %collective-permute-done.16.refs_1_, bf16[1024,2560]{1,0:T(8,128)(2,1)S(1)} %copy-done.3), custom_call_target="tpu_custom_call" | custom-call | flops 1 | bytes 1 | tf_op jit(solution)/shard_map/pallas_call | solution.py:199
  79.6 2.5 %copy-done.6 = bf16[2560,1024]{1,0:T(8,128)(2,1)S(1)} copy-done((bf16[2560,1024]{1,0:T(8,128)(2,1)S(1)}, bf16[2560,1024]{1,0:T(8,128)(2,1)}, u32[]{:S(2)}) %copy-start.6) | copy-done | bytes 5242904
  82.0 2.3 %shard_map.101 = (f32[256,512]{1,0:T(8,128)S(1)}, f32[256,512]{1,0:T(8,128)S(1)}, s32[256,1]{1,0:T(8,128)S(1)}) custom-call(s32[1]{0:T(128)} %bitcast.5.side_ref, bf16[256,2560]{1,0:T(8,128)(2,1)S(1)} %copy-done.7, s32[1,256]{1,0:T(1,128)S(1)} %copy-done.10, bf16[2560,1024]{1,0:T(8,128)(2,1)S(1)} %copy-done.6), custom_call_target="tpu_custom_call" | custom-call | flops 1 | bytes 1 | tf_op jit(solution)/shard_map/pallas_call | solution.py:145
  85.9 4.8 %collective-permute-start.20 = (bf16[1,24,1536]{2,1,0:T(8,128)(2,1)S(1)}, bf16[1,24,1536]{2,1,0:T(8,128)(2,1)S(1)}, u32[]{:S(2)}, u32[]{:S(2)}) collective-permute-start(bf16[1,24,1536]{2,1,0:T(8,128)(2,1)S(1)} %shard_map.100), channel_id=1, source_target_pairs={{0,14},{4,10},{8,6},{12,2},{14,0},{10,4},{6,8},{2,12},{1,15},{5,11... | collective-permute-start | bytes 221192 | tf_op jit(solution)/shard_map/ppermute | solution.py:348
  90.8 2.7 %collective-permute-done.20.last_ref = bf16[1,24,1536]{2,1,0:T(8,128)(2,1)S(1)} collective-permute-done((bf16[1,24,1536]{2,1,0:T(8,128)(2,1)S(1)}, bf16[1,24,1536]{2,1,0:T(8,128)(2,1)S(1)}, u32[]{:S(2)}, u32[]{:S(2)}) %collective-permute-start.20) | collective-permute-done | bytes 73760 | tf_op jit(solution)/shard_map/ppermute | solution.py:348
  94.7 2.6 %shard_map.102 = bf16[256,512]{1,0:T(8,128)(2,1)} custom-call(s32[1]{0:T(128)} %bitcast.3.busy_ref, s32[1]{0:T(128)} %bitcast.4.far_ref, f32[256,512]{1,0:T(8,128)S(1)} %get-tuple-element.105.own_ref, f32[256,512]{1,0:T(8,128)S(1)} %collective-permute-done.19.other_ref, bf16[8,24,2048]{2,1,0:T(8,128)(2,1)S(1)} %all-to-all-done.back_ref, ...), custom_call_target="tpu_custom_call" | custom-call | tf_op jit(solution)/shard_map/pallas_call | solution.py:292
  (72 shorter events, 24.7 us)
Async XLA Ops:
  3.6 16.5 %collective-permute-start = (bf16[72,2688]{1,0:T(8,128)(2,1)}, bf16[72,2688]{1,0:T(8,128)(2,1)S(1)}, u32[]{:S(2)}, u32[]{:S(2)}) collective-permute-start(bf16[72,2688]{1,0:T(8,128)(2,1)} %get-tuple-element.63.refs_0_), channel_id=1, source_target_pairs={{0,4},{4,8},{8,12},{12,14},{14,10},{10,6},{6,2},{2,0},{1,5},{5,9},... | collective-permute-start | bytes 1161224 | tf_op jit(solution)/shard_map/ppermute | solution.py:348
  6.7 13.4 %collective-permute-start.1 = (bf16[72,2688]{1,0:T(8,128)(2,1)}, bf16[72,2688]{1,0:T(8,128)(2,1)S(1)}, u32[]{:S(2)}, u32[]{:S(2)}) collective-permute-start(bf16[72,2688]{1,0:T(8,128)(2,1)} %get-tuple-element.63.refs_0_), channel_id=1, source_target_pairs={{0,2},{4,0},{8,4},{12,8},{14,12},{10,14},{6,10},{2,6},{1,3},{5,1},... | collective-permute-start | bytes 1161224 | tf_op jit(solution)/shard_map/ppermute | solution.py:348
  6.7 11.9 %collective-permute-start.2 = (bf16[24,2688]{1,0:T(8,128)(2,1)}, bf16[24,2688]{1,0:T(8,128)(2,1)S(1)}, u32[]{:S(2)}, u32[]{:S(2)}) collective-permute-start(bf16[24,2688]{1,0:T(8,128)(2,1)} %get-tuple-element.59), channel_id=1, source_target_pairs={{0,4},{4,8},{8,12},{12,14},{14,10},{10,6},{6,2},{2,0},{1,5},{5,9},... | collective-permute-start | bytes 387080 | tf_op jit(solution)/shard_map/ppermute | solution.py:348
  8.7 11.4 %collective-permute-start.3 = (bf16[24,2688]{1,0:T(8,128)(2,1)}, bf16[24,2688]{1,0:T(8,128)(2,1)S(1)}, u32[]{:S(2)}, u32[]{:S(2)}) collective-permute-start(bf16[24,2688]{1,0:T(8,128)(2,1)} %get-tuple-element.60), channel_id=1, source_target_pairs={{0,2},{4,0},{8,4},{12,8},{14,12},{10,14},{6,10},{2,6},{1,3},{5,1},... | collective-permute-start | bytes 387080 | tf_op jit(solution)/shard_map/ppermute | solution.py:348
  11.2 19.3 %copy-start.4 = (bf16[16,64,512]{2,1,0:T(8,128)(2,1)S(1)}, bf16[16,64,512]{2,1,0:T(8,128)(2,1)}, u32[]{:S(2)}) copy-start(bf16[16,64,512]{2,1,0:T(8,128)(2,1)} %param.12) | copy-start | bytes 3145732
  11.2 28.6 %copy-start.9 = (bf16[24,2688]{1,0:T(8,128)(2,1)S(1)}, bf16[24,2688]{1,0:T(8,128)(2,1)}, u32[]{:S(2)}) copy-start(bf16[24,2688]{1,0:T(8,128)(2,1)} %get-tuple-element.77.refs_2_) | copy-start | bytes 387076
  20.1 16.2 %collective-permute-start.4 = (bf16[72,2688]{1,0:T(8,128)(2,1)S(1)}, bf16[72,2688]{1,0:T(8,128)(2,1)S(1)}, u32[]{:S(2)}, u32[]{:S(2)}) collective-permute-start(bf16[72,2688]{1,0:T(8,128)(2,1)S(1)} %collective-permute-done.refs_1_), channel_id=1, source_target_pairs={{0,4},{4,8},{8,12},{12,14},{14,10},{10,6},{6,2},{2,0},{1,5},{5,9},... | collective-permute-start | bytes 1161224 | tf_op jit(solution)/shard_map/ppermute | solution.py:348
  21.7 14.6 %collective-permute-start.5 = (bf16[72,2688]{1,0:T(8,128)(2,1)S(1)}, bf16[72,2688]{1,0:T(8,128)(2,1)S(1)}, u32[]{:S(2)}, u32[]{:S(2)}) collective-permute-start(bf16[72,2688]{1,0:T(8,128)(2,1)S(1)} %collective-permute-done.1.refs_2_), channel_id=1, source_target_pairs={{0,2},{4,0},{8,4},{12,8},{14,12},{10,14},{6,10},{2,6},{1,3},{5,1},... | collective-permute-start | bytes 1161224 | tf_op jit(solution)/shard_map/ppermute | solution.py:348
  22.1 12.6 %collective-permute-start.7 = (bf16[24,2688]{1,0:T(8,128)(2,1)}, bf16[24,2688]{1,0:T(8,128)(2,1)S(1)}, u32[]{:S(2)}, u32[]{:S(2)}) collective-permute-start(bf16[24,2688]{1,0:T(8,128)(2,1)} %get-tuple-element.69), channel_id=1, source_target_pairs={{0,8},{4,12},{8,14},{12,10},{14,6},{10,2},{6,0},{2,4},{1,9},{5,13}... | collective-permute-start | bytes 387080 | tf_op jit(solution)/shard_map/ppermute | solution.py:348
  24.7 11.6 %collective-permute-start.8 = (bf16[24,2688]{1,0:T(8,128)(2,1)}, bf16[24,2688]{1,0:T(8,128)(2,1)}, u32[]{:S(2)}, u32[]{:S(2)}) collective-permute-start(bf16[24,2688]{1,0:T(8,128)(2,1)} %get-tuple-element.71), channel_id=1, source_target_pairs={{0,6},{4,2},{8,0},{12,4},{14,8},{10,12},{6,14},{2,10},{1,7},{5,3},... | collective-permute-start | bytes 387080 | tf_op jit(solution)/shard_map/ppermute | solution.py:348
  29.1 1.3 %collective-permute-start.6 = (f32[64,216]{1,0:T(8,128)S(1)}, f32[64,216]{1,0:T(8,128)S(1)}, u32[]{:S(2)}, u32[]{:S(2)}) collective-permute-start(f32[64,216]{1,0:T(8,128)S(1)} %get-tuple-element.66.own_ref), channel_id=1, source_target_pairs={{0,1},{1,0},{2,3},{3,2},{4,5},{5,4},{6,7},{7,6},{8,9},{9,8},{10,11... | collective-permute-start | bytes 165896 | tf_op jit(solution)/shard_map/ppermute | solution.py:315
  36.3 23.1 %collective-permute-start.10 = (bf16[72,2688]{1,0:T(8,128)(2,1)S(1)}, bf16[72,2688]{1,0:T(8,128)(2,1)S(1)}, u32[]{:S(2)}, u32[]{:S(2)}) collective-permute-start(bf16[72,2688]{1,0:T(8,128)(2,1)S(1)} %collective-permute-done.5.refs_1_), channel_id=1, source_target_pairs={{0,2},{4,0},{8,4},{12,8},{14,12},{10,14},{6,10},{2,6},{1,3},{5,1},... | collective-permute-start | bytes 1161224 | tf_op jit(solution)/shard_map/ppermute | solution.py:348
  38.1 21.3 %collective-permute-start.9 = (bf16[72,2688]{1,0:T(8,128)(2,1)S(1)}, bf16[72,2688]{1,0:T(8,128)(2,1)S(1)}, u32[]{:S(2)}, u32[]{:S(2)}) collective-permute-start(bf16[72,2688]{1,0:T(8,128)(2,1)S(1)} %collective-permute-done.4.refs_0_), channel_id=1, source_target_pairs={{0,4},{4,8},{8,12},{12,14},{14,10},{10,6},{6,2},{2,0},{1,5},{5,9},... | collective-permute-start | bytes 1161224 | tf_op jit(solution)/shard_map/ppermute | solution.py:348
  43.5 4.0 %collective-permute-start.11 = (f32[64,264]{1,0:T(8,128)S(1)}, f32[64,264]{1,0:T(8,128)S(1)}, u32[]{:S(2)}, u32[]{:S(2)}) collective-permute-start(f32[64,264]{1,0:T(8,128)S(1)} %get-tuple-element.82.own_ref), channel_id=1, source_target_pairs={{0,1},{1,0},{2,3},{3,2},{4,5},{5,4},{6,7},{7,6},{8,9},{9,8},{10,11... | collective-permute-start | bytes 202760 | tf_op jit(solution)/shard_map/ppermute | solution.py:315
  43.6 15.8 %collective-permute-start.12 = (bf16[24,2688]{1,0:T(8,128)(2,1)S(1)}, bf16[24,2688]{1,0:T(8,128)(2,1)S(1)}, u32[]{:S(2)}, u32[]{:S(2)}) collective-permute-start(bf16[24,2688]{1,0:T(8,128)(2,1)S(1)} %copy-done.15), channel_id=1, source_target_pairs={{0,12},{4,14},{8,10},{12,6},{14,2},{10,0},{6,4},{2,8},{1,13},{5,15... | collective-permute-start | bytes 387080 | tf_op jit(solution)/shard_map/ppermute | solution.py:348
  45.2 14.2 %collective-permute-start.13 = (bf16[24,2688]{1,0:T(8,128)(2,1)S(1)}, bf16[24,2688]{1,0:T(8,128)(2,1)S(1)}, u32[]{:S(2)}, u32[]{:S(2)}) collective-permute-start(bf16[24,2688]{1,0:T(8,128)(2,1)S(1)} %copy-done.14), channel_id=1, source_target_pairs={{0,10},{4,6},{8,2},{12,0},{14,4},{10,8},{6,12},{2,14},{1,11},{5,7}... | collective-permute-start | bytes 387080 | tf_op jit(solution)/shard_map/ppermute | solution.py:348
  47.5 11.9 %collective-permute-start.14 = (bf16[24,2688]{1,0:T(8,128)(2,1)S(1)}, bf16[24,2688]{1,0:T(8,128)(2,1)S(1)}, u32[]{:S(2)}, u32[]{:S(2)}) collective-permute-start(bf16[24,2688]{1,0:T(8,128)(2,1)S(1)} %copy-done.13), channel_id=1, source_target_pairs={{0,14},{4,10},{8,6},{12,2},{14,0},{10,4},{6,8},{2,12},{1,15},{5,11... | collective-permute-start | bytes 387080 | tf_op jit(solution)/shard_map/ppermute | solution.py:348
  59.4 8.8 %collective-permute-start.16 = (bf16[40,2688]{1,0:T(8,128)(2,1)S(1)}, bf16[40,2688]{1,0:T(8,128)(2,1)S(1)}, u32[]{:S(2)}, u32[]{:S(2)}) collective-permute-start(bf16[40,2688]{1,0:T(8,128)(2,1)S(1)} %slice.15), channel_id=1, source_target_pairs={{0,2},{4,0},{8,4},{12,8},{14,12},{10,14},{6,10},{2,6},{1,3},{5,1},... | collective-permute-start | bytes 645128 | tf_op jit(solution)/shard_map/ppermute | solution.py:348
  59.8 7.7 %collective-permute-start.15 = (bf16[32,2688]{1,0:T(8,128)(2,1)S(1)}, bf16[32,2688]{1,0:T(8,128)(2,1)S(1)}, u32[]{:S(2)}, u32[]{:S(2)}) collective-permute-start(bf16[32,2688]{1,0:T(8,128)(2,1)S(1)} %slice.14), channel_id=1, source_target_pairs={{0,4},{4,8},{8,12},{12,14},{14,10},{10,6},{6,2},{2,0},{1,5},{5,9},... | collective-permute-start | bytes 516104 | tf_op jit(solution)/shard_map/ppermute | solution.py:348
  64.4 1.3 %collective-permute-start.17 = (f32[64,216]{1,0:T(8,128)S(1)}, f32[64,216]{1,0:T(8,128)S(1)}, u32[]{:S(2)}, u32[]{:S(2)}) collective-permute-start(f32[64,216]{1,0:T(8,128)S(1)} %get-tuple-element.97.own_ref), channel_id=1, source_target_pairs={{0,1},{1,0},{2,3},{3,2},{4,5},{5,4},{6,7},{7,6},{8,9},{9,8},{10,11... | collective-permute-start | bytes 165896 | tf_op jit(solution)/shard_map/ppermute | solution.py:315
  68.3 26.4 %all-to-all-start = ((bf16[8,24,2048]{2,1,0:T(8,128)(2,1)}), bf16[8,24,2048]{2,1,0:T(8,128)(2,1)S(1)}, u32[]{:S(2)}, u32[]{:S(2)}) async-start(bf16[8,24,2048]{2,1,0:T(8,128)(2,1)} %shard_map.98), calls=%async_computation | async-start | bytes 1572864 | tf_op jit(solution)/shard_map/all_to_all | solution.py:402
  76.9 1.4 %collective-permute-start.18 = (f32[64,72]{1,0:T(8,128)}, f32[64,72]{1,0:T(8,128)S(1)}, u32[]{:S(2)}, u32[]{:S(2)}) collective-permute-start(f32[64,72]{1,0:T(8,128)} %get-tuple-element.101.own_ref), channel_id=1, source_target_pairs={{0,1},{1,0},{2,3},{3,2},{4,5},{5,4},{6,7},{7,6},{8,9},{9,8},{10,11... | collective-permute-start | bytes 55304 | tf_op jit(solution)/shard_map/ppermute | solution.py:315
  84.4 9.1 %collective-permute-start.19 = (f32[256,512]{1,0:T(8,128)S(1)}, f32[256,512]{1,0:T(8,128)S(1)}, u32[]{:S(2)}, u32[]{:S(2)}) collective-permute-start(f32[256,512]{1,0:T(8,128)S(1)} %get-tuple-element.106), channel_id=1, source_target_pairs={{0,1},{1,0},{2,3},{3,2},{4,5},{5,4},{6,7},{7,6},{8,9},{9,8},{10,11... | collective-permute-start | bytes 1572872 | tf_op jit(solution)/shard_map/ppermute | solution.py:315
  85.9 7.6 %collective-permute-start.20 = (bf16[1,24,1536]{2,1,0:T(8,128)(2,1)S(1)}, bf16[1,24,1536]{2,1,0:T(8,128)(2,1)S(1)}, u32[]{:S(2)}, u32[]{:S(2)}) collective-permute-start(bf16[1,24,1536]{2,1,0:T(8,128)(2,1)S(1)} %shard_map.100), channel_id=1, source_target_pairs={{0,14},{4,10},{8,6},{12,2},{14,0},{10,4},{6,8},{2,12},{1,15},{5,11... | collective-permute-start | bytes 221192 | tf_op jit(solution)/shard_map/ppermute | solution.py:348
  (14 other events, 141.1 us)

commit v7 on v6

--- a/solution.py
+++ b/solution.py
@@ -10,6 +10,7 @@
 rope_theta = 1000000.0
 LANES = 128
 EXTRA = 128
+COLD, HOT, REST = 0, 1, 2
 HOT_PARTS = 3
 ALL_VMEM = 60 * 1024 * 1024
 LITTLE = pl.CostEstimate(flops=1, bytes_accessed=1, transcendentals=0)
@@ -72,26 +73,37 @@
     pick = position == lax.broadcasted_iota(jnp.int32, (total, count), 0)
     pick = pick.astype(jnp.float32).astype(jnp.bfloat16)
     lane = lax.broadcasted_iota(jnp.int32, (count, EXTRA), 1)
-    beside = jnp.where(lane == 0, owner_col + 1, jnp.where(lane == 1, slot_col - owner_col * stored, 0))
-    beside = beside.astype(jnp.float32).astype(jnp.bfloat16)
+    local_col = slot_col - owner_col * stored
+
+    def beside(pick, first):
+        codes = jnp.where(lane == first, owner_col + 1, jnp.where(lane == first + 1, local_col, 0))
+        codes = codes.astype(jnp.float32).astype(jnp.bfloat16)
+        return jnp.dot(pick, codes, preferred_element_type=jnp.float32)
+
+    hot_extra = jnp.zeros((share, EXTRA), jnp.float32)
+    for part in range(HOT_PARTS):
+        piece = position - (cold_total + part * share) == lax.broadcasted_iota(
+            jnp.int32, (share, count), 0
+        )
+        hot_extra = hot_extra + beside(piece.astype(jnp.float32).astype(jnp.bfloat16), 2 + 2 * part)
     width = tokens_ref.shape[1]
-    extra = jnp.dot(pick, beside, preferred_element_type=jnp.float32)
+    extra = beside(pick, 0)
     fetch.wait()
     rows = jnp.dot(pick, tokens_ref[...], preferred_element_type=jnp.float32)
-    firsts = [cold_total] + [k * share for k in range(owners)]
-    for first, out_ref in zip(firsts, (hot_ref, *cold_refs)):
-        size = out_ref.shape[0]
-        out_ref[:, :width] = rows[first : first + size].astype(jnp.bfloat16)
-        out_ref[:, width:] = extra[first : first + size].astype(jnp.bfloat16)
+    hot_ref[...] = rows[cold_total:].astype(jnp.bfloat16)
+    for k, out_ref in enumerate(cold_refs):
+        span = slice(k * share, (k + 1) * share)
+        out_ref[:, :width] = rows[span].astype(jnp.bfloat16)
+        out_ref[:, width:] = (extra[span] + hot_extra).astype(jnp.bfloat16)
 
 
 def route(me, request, table, tokens, stored, owners, share):
     count, width = tokens.shape
-    packed = [HOT_PARTS * share] + [share] * owners
+    packed = [(HOT_PARTS * share, width)] + [(share, width + EXTRA)] * owners
     outs = pl.pallas_call(
         functools.partial(route_kernel, stored, owners, share),
         out_shape=(
-            *(jax.ShapeDtypeStruct((n, width + EXTRA), jnp.bfloat16) for n in packed),
+            *(jax.ShapeDtypeStruct(shape, jnp.bfloat16) for shape in packed),
             jax.ShapeDtypeStruct((1, count), jnp.int32),
             jax.ShapeDtypeStruct((1, 1), jnp.int32),
         ),
@@ -171,13 +183,24 @@
     )(table)
 
 
-def down_kernel(rank, parts, me_ref, *refs):
-    rows_refs = refs[:parts]
-    weight_ref, out_ref, local_ref = refs[parts:]
+def down_kernel(rank, blocks, guides, me_ref, *refs):
+    guide_refs, refs = refs[:guides], refs[guides:]
+    row_count = sum(1 for kind, _ in blocks if kind != COLD)
+    rows_refs = list(refs[:row_count])
+    weight_ref, out_ref, local_ref = refs[row_count:]
     width = weight_ref.shape[1]
-    extra = jnp.concatenate([r[:, width:].astype(jnp.float32) for r in rows_refs], axis=0).T
-    local = jnp.where(extra[0:1] == (me_ref[0] + 1).astype(jnp.float32), extra[1:2], -1.0)
-    rows = jnp.concatenate([r[:, :width] for r in rows_refs], axis=0)
+    routing = [r[:, width:].astype(jnp.float32).T for r in guide_refs]
+    local, rows = [], []
+    for kind, guide in blocks:
+        if kind == COLD:
+            rows.append(guide_refs[guide][:, :width])
+        else:
+            rows.append(rows_refs.pop(0)[...])
+        for k in {COLD: [0], HOT: range(2, 2 + 2 * HOT_PARTS, 2), REST: []}[kind]:
+            mine = routing[guide][k : k + 1] == (me_ref[0] + 1).astype(jnp.float32)
+            local.append(jnp.where(mine, routing[guide][k + 1 : k + 2], -1.0))
+    local = jnp.concatenate(local, axis=1)
+    rows = jnp.concatenate(rows, axis=0)
     block = 4 * rank
     out = jnp.zeros(out_ref.shape, jnp.float32)
     for first in range(0, weight_ref.shape[0], block):
@@ -194,11 +217,12 @@
     local_ref[...] = local
 
 
-def down(me, row_arrays, table, rank):
-    count = sum(r.shape[0] for r in row_arrays)
+def down(me, blocks, guides, row_arrays, table, rank):
+    share = guides[0].shape[0]
+    count = share * sum(kind == COLD for kind, _ in blocks) + sum(r.shape[0] for r in row_arrays)
     return pl.pallas_call(
-        functools.partial(down_kernel, rank, len(row_arrays)),
-        in_specs=[scalars()] + [whole()] * (len(row_arrays) + 1),
+        functools.partial(down_kernel, rank, blocks, len(guides)),
+        in_specs=[scalars()] + [whole()] * (len(guides) + len(row_arrays) + 1),
         out_specs=(whole(), whole()),
         out_shape=(
             jax.ShapeDtypeStruct((rank, count), jnp.float32),
@@ -206,7 +230,7 @@
         ),
         compiler_params=params(),
         cost_estimate=LITTLE,
-    )(me, *row_arrays, table)
+    )(me, *guides, *row_arrays, table)
 
 
 def update(own_ref, other_ref, local_ref, weight_ref):
@@ -355,8 +379,11 @@
         sources[index] = [ring[(spot - d) % owners] for d in distances + list(range(owners))]
     order = lax.dynamic_index_in_dim(jnp.array(sources, jnp.int32), me, 0, keepdims=False)
 
-    def product(rows):
-        own, local = down(here, rows, down_table, rank)
+    def product(blocks, rows):
+        distances_of = sorted({d for _, d in blocks})
+        blocks = [(kind, distances_of.index(d)) for kind, d in blocks]
+        guides = lax.optimization_barrier((*(got[d] for d in distances_of), rows[0]))[:-1]
+        own, local = down(here, blocks, list(guides), rows, down_table, rank)
         return own, swap(own), local
 
     group = [along(hot, 1), along(hot, -1)]
@@ -385,22 +412,22 @@
         else:
             following = [along(group[0][:cut], 1), along(group[1][cut:], -1)]
         rows, units = list(group), hot_units(2 * step - 1, 2)
+        blocks = [(HOT, step), (HOT, owners - step)]
         if step == 1:
-            rows, units = [hot] + rows, hot_units(0, 3)
+            rows, units, blocks = [hot] + rows, hot_units(0, 3), [(HOT, 0)] + blocks
         if step == half_way - 2:
             chosen = [d for d in range(owners) if d not in waves[half_way - 1]]
         elif step == half_way - 1:
             chosen = waves[step]
         else:
             chosen = []
-        rows += [got[d] for d in chosen]
-        rows = lax.optimization_barrier((*rows, group[0]))[:-1]
-        delta = up(order, units + cold_units(chosen), *product(list(rows)), up_table, delta)
+        blocks += [(COLD, d) for d in chosen]
+        delta = up(order, units + cold_units(chosen), *product(blocks, rows), up_table, delta)
         todo = [delta] + [got[d] for d in waves.get(step + 1, [])]
         group = following
     *group, delta = lax.optimization_barrier((*group, delta))
     back = lax.all_to_all(delta, "dp", split_axis=0, concat_axis=0, tiled=True)
-    last = product(group)
+    last = product([(HOT, half_way), (REST, half_way)], list(group))
     far_delta = jax.ShapeDtypeStruct((1, share, HOT_PARTS * features), jnp.bfloat16)
     far_delta = up(
         jnp.zeros((1,), jnp.int32), [(0, c) for c in range(HOT_PARTS)], *last, up_table, far_delta

time: 97.8 us -> 96 us (0.982)
  Pallas kernels: 24.4 us -> 21.9 us
  local copies, waits for them, and re-layouts: 13.7 us -> 15.3 us
    unnamed x32 -> x36, local copies, waits for them, and re-layouts: 12.3 us -> 13.9 us
    pallas_call x4, Pallas kernels: 9.01 us -> 7.48 us  [down(): pl.pallas_call(functools.partial(down_kernel, rank, blocks, len(guides)),...]
    ppermute x16, starting transfers between devices: 27 us -> 26 us  [along(): lax.ppermute(rows, 'dp', [(ring[i], ring[(i + distance) % owners]) for i...]
  transfers between devices with their start and end apart: 22 -> 22, of which waited for: 11 -> 11; matrix products, arithmetic and copies ran while one was open for 2% -> 2% of each run, Pallas kernels for 19% -> 17%
where the time goes in v7:
time: 96 us; the launch traced here: 95.6 us
  starting transfers between devices  30.7 us (32%)
  waiting for transfers between devices  26.7 us (28%)
  Pallas kernels  21.9 us (23%)
  local copies, waits for them, and re-layouts  15.3 us (16%)
    ppermute x16, starting transfers between devices, along(): lax.ppermute(rows, 'dp', [(ring[i], ring[(i + distance) % owners]) for i...  26 us
    ppermute x16, waiting for transfers between devices, along(): lax.ppermute(rows, 'dp', [(ring[i], ring[(i + distance) % owners]) for i...  22 us
    unnamed x36, local copies, waits for them, and re-layouts  13.9 us
    pallas_call x4, Pallas kernels, down(): pl.pallas_call(functools.partial(down_kernel, rank, blocks, len(guides)),...  7.48 us
    pallas_call x4, Pallas kernels, up(): pl.pallas_call(functools.partial(up_kernel, units, len(given)), in_specs=...  5.7 us
    all_to_all x1, starting transfers between devices, on_device(): back = lax.all_to_all(delta, 'dp', split_axis=0, concat_axis=0, tiled=True)  4.15 us
    pallas_call x1, Pallas kernels, route(): pl.pallas_call(functools.partial(route_kernel, stored, owners, share), ou...  3.57 us
    ppermute x5, waiting for transfers between devices, swap(): return lax.ppermute(x, 'tensor', [(0, 1), (1, 0)])  2.98 us
  transfers between devices with their start and end apart: 22, of which 11 were waited for; matrix products, arithmetic and copies ran while one was open for 2% of the time, Pallas kernels for 17%

profile of v7, /device:TPU:0, one launch (start us, length us, event | category | flops | bytes accessed | tf_op | source)
XLA Modules:
  0.0 95.6 jit_solution(14098266336409651475)
XLA Ops:
  0.0 3.6 %shard_map.91 = (bf16[72,2560]{1,0:T(8,128)(2,1)}, bf16[24,2688]{1,0:T(8,128)(2,1)}, bf16[24,2688]{1,0:T(8,128)(2,1)}, bf16[24,2688]{1,0:T(8,128)(2,1)}, bf16[24...) custom-call(s32[1]{0:T(128)} %bitcast.me_ref, ...), custom_call_target="tpu_custom_call" | custom-call | tf_op jit(solution)/shard_map/pallas_call | solution.py:103
  3.6 3.1 %collective-permute-start = (bf16[72,2560]{1,0:T(8,128)(2,1)}, bf16[72,2560]{1,0:T(8,128)(2,1)S(1)}, u32[]{:S(2)}, u32[]{:S(2)}) collective-permute-start(bf16[72,2560]{1,0:T(8,128)(2,1)} %get-tuple-element.56.refs_3_), channel_id=1, source_target_pairs={{0,4},{4,8},{8,12},{12,14},{14,10},{10,6},{6,2},{2,0},{1,5},{5,9},... | collective-permute-start | bytes 1105928 | tf_op jit(solution)/shard_map/ppermute | solution.py:372
  6.7 2.0 %collective-permute-start.2 = (bf16[24,2688]{1,0:T(8,128)(2,1)}, bf16[24,2688]{1,0:T(8,128)(2,1)S(1)}, u32[]{:S(2)}, u32[]{:S(2)}) collective-permute-start(bf16[24,2688]{1,0:T(8,128)(2,1)} %get-tuple-element.57), channel_id=1, source_target_pairs={{0,4},{4,8},{8,12},{12,14},{14,10},{10,6},{6,2},{2,0},{1,5},{5,9},... | collective-permute-start | bytes 387080 | tf_op jit(solution)/shard_map/ppermute | solution.py:372
  8.7 2.5 %copy-done.5 = bf16[16,64,2560]{2,1,0:T(8,128)(2,1)S(1)} copy-done((bf16[16,64,2560]{2,1,0:T(8,128)(2,1)S(1)}, bf16[16,64,2560]{2,1,0:T(8,128)(2,1)}, u32[]{:S(2)}) %copy-start.5) | copy-done | bytes 5242904
  11.6 2.3 %copy-done = bf16[1024,2560]{1,0:T(8,128)(2,1)} copy-done((bf16[1024,2560]{1,0:T(8,128)(2,1)}, bf16[1024,2560]{1,0:T(8,128)(2,1)S(1)}, u32[]{:S(2)}) %copy-start) | copy-done | bytes 5242904
  13.9 4.2 %collective-permute-done.2.refs_1_ = bf16[24,2688]{1,0:T(8,128)(2,1)S(1)} collective-permute-done((bf16[24,2688]{1,0:T(8,128)(2,1)}, bf16[24,2688]{1,0:T(8,128)(2,1)S(1)}, u32[]{:S(2)}, u32[]{:S(2)}) %collective-permute-start.2) | collective-permute-done | bytes 129056 | tf_op jit(solution)/shard_map/ppermute | solution.py:372
  21.7 2.6 %collective-permute-start.7 = (bf16[24,2688]{1,0:T(8,128)(2,1)}, bf16[24,2688]{1,0:T(8,128)(2,1)S(1)}, u32[]{:S(2)}, u32[]{:S(2)}) collective-permute-start(bf16[24,2688]{1,0:T(8,128)(2,1)} %get-tuple-element.68), channel_id=1, source_target_pairs={{0,8},{4,12},{8,14},{12,10},{14,6},{10,2},{6,0},{2,4},{1,9},{5,13}... | collective-permute-start | bytes 387080 | tf_op jit(solution)/shard_map/ppermute | solution.py:372
  24.7 2.5 %copy-done.1 = bf16[1024,2560]{1,0:T(8,128)(2,1)S(1)} copy-done((bf16[1024,2560]{1,0:T(8,128)(2,1)S(1)}, bf16[1024,2560]{1,0:T(8,128)(2,1)}, u32[]{:S(2)}) %copy-start.1) | copy-done | bytes 5242904
  31.8 2.1 %collective-permute-done.7.refs_2_ = bf16[24,2688]{1,0:T(8,128)(2,1)S(1)} collective-permute-done((bf16[24,2688]{1,0:T(8,128)(2,1)}, bf16[24,2688]{1,0:T(8,128)(2,1)S(1)}, u32[]{:S(2)}, u32[]{:S(2)}) %collective-permute-start.7) | collective-permute-done | bytes 129056 | tf_op jit(solution)/shard_map/ppermute | solution.py:372
  35.4 2.8 %collective-permute-start.10 = (bf16[72,2560]{1,0:T(8,128)(2,1)S(1)}, bf16[72,2560]{1,0:T(8,128)(2,1)S(1)}, u32[]{:S(2)}, u32[]{:S(2)}) collective-permute-start(bf16[72,2560]{1,0:T(8,128)(2,1)S(1)} %collective-permute-done.4.refs_5_), channel_id=1, source_target_pairs={{0,4},{4,8},{8,12},{12,14},{14,10},{10,6},{6,2},{2,0},{1,5},{5,9},... | collective-permute-start | bytes 1105928 | tf_op jit(solution)/shard_map/ppermute | solution.py:372
  38.2 2.9 %shard_map.95 = (f32[64,264]{1,0:T(8,128)S(1)}, f32[1,264]{1,0:T(1,128)S(1)}) custom-call(s32[1]{0:T(128)} %bitcast.me_ref, bf16[24,2688]{1,0:T(8,128)(2,1)S(1)} %copy-done.8, bf16[24,2688]{1,0:T(8,128)(2,1)S(1)} %collective-permute-done.2.refs_1_, bf16[24,2688]{1,0:T(8,128)(2,1)S(1)} %collective-permute-done.7.refs_2_, ...), custom_call_target="tpu_custom_call" | custom-call | flops 1 | bytes 1 | tf_op jit(solution)/shard_map/pallas_call | solution.py:223
  41.1 2.0 %collective-permute-start.13 = (bf16[24,2688]{1,0:T(8,128)(2,1)S(1)}, bf16[24,2688]{1,0:T(8,128)(2,1)S(1)}, u32[]{:S(2)}, u32[]{:S(2)}) collective-permute-start(bf16[24,2688]{1,0:T(8,128)(2,1)S(1)} %copy-done.17), channel_id=1, source_target_pairs={{0,12},{4,14},{8,10},{12,6},{14,2},{10,0},{6,4},{2,8},{1,13},{5,15... | collective-permute-start | bytes 387080 | tf_op jit(solution)/shard_map/ppermute | solution.py:372
  43.2 1.8 %collective-permute-start.14 = (bf16[24,2688]{1,0:T(8,128)(2,1)S(1)}, bf16[24,2688]{1,0:T(8,128)(2,1)S(1)}, u32[]{:S(2)}, u32[]{:S(2)}) collective-permute-start(bf16[24,2688]{1,0:T(8,128)(2,1)S(1)} %copy-done.16), channel_id=1, source_target_pairs={{0,10},{4,6},{8,2},{12,0},{14,4},{10,8},{6,12},{2,14},{1,11},{5,7}... | collective-permute-start | bytes 387080 | tf_op jit(solution)/shard_map/ppermute | solution.py:372
  46.6 1.8 %shard_map.96.refs_0_ = bf16[8,24,2048]{2,1,0:T(8,128)(2,1)} custom-call(s32[16]{0:T(128)S(1)} %get-tuple-element.103.to_ref, f32[64,264]{1,0:T(8,128)S(1)} %get-tuple-element.79.own_ref, f32[64,264]{1,0:T(8,128)S(1)} %collective-permute-done.12.other_ref, f32[1,264]{1,0:T(1,128)S(1)} %get-tuple-element.80.local_ref, ...), custom_call_target="tpu_custom_call", output_to_operand_aliasing={{}: (5, {})} | custom-call | flops 1 | bytes 1 | tf_op jit(solution)/shard_map/pallas_call | solution.py:271
  48.4 9.1 %collective-permute-done.13.refs_0_ = bf16[24,2688]{1,0:T(8,128)(2,1)S(1)} collective-permute-done((bf16[24,2688]{1,0:T(8,128)(2,1)S(1)}, bf16[24,2688]{1,0:T(8,128)(2,1)S(1)}, u32[]{:S(2)}, u32[]{:S(2)}) %collective-permute-start.13) | collective-permute-done | bytes 129056 | tf_op jit(solution)/shard_map/ppermute | solution.py:372
  58.6 2.0 %collective-permute-start.15 = (bf16[32,2560]{1,0:T(8,128)(2,1)S(1)}, bf16[32,2560]{1,0:T(8,128)(2,1)S(1)}, u32[]{:S(2)}, u32[]{:S(2)}) collective-permute-start(bf16[32,2560]{1,0:T(8,128)(2,1)S(1)} %slice.14), channel_id=1, source_target_pairs={{0,4},{4,8},{8,12},{12,14},{14,10},{10,6},{6,2},{2,0},{1,5},{5,9},... | collective-permute-start | bytes 491528 | tf_op jit(solution)/shard_map/ppermute | solution.py:372
  63.5 1.7 %shard_map.98 = bf16[8,24,2048]{2,1,0:T(8,128)(2,1)} custom-call(s32[16]{0:T(128)S(1)} %get-tuple-element.103.to_ref, f32[64,216]{1,0:T(8,128)S(1)} %get-tuple-element.90.own_ref, f32[64,216]{1,0:T(8,128)S(1)} %collective-permute-done.17.other_ref, f32[1,216]{1,0:T(1,128)S(1)} %get-tuple-element.91.local_ref, ...), custom_call_target="tpu_custom_call", output_to_operand_aliasing={{}: (5, {})} | custom-call | flops 1 | bytes 1 | tf_op jit(solution)/shard_map/pallas_call | solution.py:271
  66.6 4.1 %all-to-all-start = ((bf16[8,24,2048]{2,1,0:T(8,128)(2,1)}), bf16[8,24,2048]{2,1,0:T(8,128)(2,1)S(1)}, u32[]{:S(2)}, u32[]{:S(2)}) async-start(bf16[8,24,2048]{2,1,0:T(8,128)(2,1)} %shard_map.98), calls=%async_computation | async-start | bytes 1572864 | tf_op jit(solution)/shard_map/all_to_all | solution.py:429
  70.8 2.5 %copy-done.3 = bf16[1024,2560]{1,0:T(8,128)(2,1)S(1)} copy-done((bf16[1024,2560]{1,0:T(8,128)(2,1)S(1)}, bf16[1024,2560]{1,0:T(8,128)(2,1)}, u32[]{:S(2)}) %copy-start.3) | copy-done | bytes 5242904
  77.5 2.5 %copy-done.6 = bf16[2560,1024]{1,0:T(8,128)(2,1)S(1)} copy-done((bf16[2560,1024]{1,0:T(8,128)(2,1)S(1)}, bf16[2560,1024]{1,0:T(8,128)(2,1)}, u32[]{:S(2)}) %copy-start.6) | copy-done | bytes 5242904
  79.9 2.3 %shard_map.101 = (f32[256,512]{1,0:T(8,128)S(1)}, f32[256,512]{1,0:T(8,128)S(1)}, s32[256,1]{1,0:T(8,128)S(1)}) custom-call(s32[1]{0:T(128)} %bitcast.5.side_ref, bf16[256,2560]{1,0:T(8,128)(2,1)S(1)} %copy-done.7, s32[1,256]{1,0:T(1,128)S(1)} %copy-done.12, bf16[2560,1024]{1,0:T(8,128)(2,1)S(1)} %copy-done.6), custom_call_target="tpu_custom_call" | custom-call | flops 1 | bytes 1 | tf_op jit(solution)/shard_map/pallas_call | solution.py:157
  83.7 4.8 %collective-permute-start.20 = (bf16[1,24,1536]{2,1,0:T(8,128)(2,1)S(1)}, bf16[1,24,1536]{2,1,0:T(8,128)(2,1)S(1)}, u32[]{:S(2)}, u32[]{:S(2)}) collective-permute-start(bf16[1,24,1536]{2,1,0:T(8,128)(2,1)S(1)} %shard_map.100), channel_id=1, source_target_pairs={{0,14},{4,10},{8,6},{12,2},{14,0},{10,4},{6,8},{2,12},{1,15},{5,11... | collective-permute-start | bytes 221192 | tf_op jit(solution)/shard_map/ppermute | solution.py:372
  88.7 2.7 %collective-permute-done.20.last_ref = bf16[1,24,1536]{2,1,0:T(8,128)(2,1)S(1)} collective-permute-done((bf16[1,24,1536]{2,1,0:T(8,128)(2,1)S(1)}, bf16[1,24,1536]{2,1,0:T(8,128)(2,1)S(1)}, u32[]{:S(2)}, u32[]{:S(2)}) %collective-permute-start.20) | collective-permute-done | bytes 73760 | tf_op jit(solution)/shard_map/ppermute | solution.py:372
  93.1 2.5 %shard_map.102 = bf16[256,512]{1,0:T(8,128)(2,1)} custom-call(s32[1]{0:T(128)} %bitcast.3.busy_ref, s32[1]{0:T(128)} %bitcast.4.far_ref, f32[256,512]{1,0:T(8,128)S(1)} %get-tuple-element.99.own_ref, f32[256,512]{1,0:T(8,128)S(1)} %collective-permute-done.19.other_ref, bf16[8,24,2048]{2,1,0:T(8,128)(2,1)S(1)} %all-to-all-done.back_ref, ...), custom_call_target="tpu_custom_call" | custom-call | tf_op jit(solution)/shard_map/pallas_call | solution.py:316
  (76 shorter events, 24.7 us)
Async XLA Ops:
  3.6 16.1 %collective-permute-start = (bf16[72,2560]{1,0:T(8,128)(2,1)}, bf16[72,2560]{1,0:T(8,128)(2,1)S(1)}, u32[]{:S(2)}, u32[]{:S(2)}) collective-permute-start(bf16[72,2560]{1,0:T(8,128)(2,1)} %get-tuple-element.56.refs_3_), channel_id=1, source_target_pairs={{0,4},{4,8},{8,12},{12,14},{14,10},{10,6},{6,2},{2,0},{1,5},{5,9},... | collective-permute-start | bytes 1105928 | tf_op jit(solution)/shard_map/ppermute | solution.py:372
  6.7 13.0 %collective-permute-start.1 = (bf16[72,2560]{1,0:T(8,128)(2,1)}, bf16[72,2560]{1,0:T(8,128)(2,1)S(1)}, u32[]{:S(2)}, u32[]{:S(2)}) collective-permute-start(bf16[72,2560]{1,0:T(8,128)(2,1)} %get-tuple-element.56.refs_3_), channel_id=1, source_target_pairs={{0,2},{4,0},{8,4},{12,8},{14,12},{10,14},{6,10},{2,6},{1,3},{5,1},... | collective-permute-start | bytes 1105928 | tf_op jit(solution)/shard_map/ppermute | solution.py:372
  6.7 11.5 %collective-permute-start.2 = (bf16[24,2688]{1,0:T(8,128)(2,1)}, bf16[24,2688]{1,0:T(8,128)(2,1)S(1)}, u32[]{:S(2)}, u32[]{:S(2)}) collective-permute-start(bf16[24,2688]{1,0:T(8,128)(2,1)} %get-tuple-element.57), channel_id=1, source_target_pairs={{0,4},{4,8},{8,12},{12,14},{14,10},{10,6},{6,2},{2,0},{1,5},{5,9},... | collective-permute-start | bytes 387080 | tf_op jit(solution)/shard_map/ppermute | solution.py:372
  8.7 11.0 %collective-permute-start.3 = (bf16[24,2688]{1,0:T(8,128)(2,1)}, bf16[24,2688]{1,0:T(8,128)(2,1)S(1)}, u32[]{:S(2)}, u32[]{:S(2)}) collective-permute-start(bf16[24,2688]{1,0:T(8,128)(2,1)} %get-tuple-element.58), channel_id=1, source_target_pairs={{0,2},{4,0},{8,4},{12,8},{14,12},{10,14},{6,10},{2,6},{1,3},{5,1},... | collective-permute-start | bytes 387080 | tf_op jit(solution)/shard_map/ppermute | solution.py:372
  11.2 18.9 %copy-start.4 = (bf16[16,64,512]{2,1,0:T(8,128)(2,1)S(1)}, bf16[16,64,512]{2,1,0:T(8,128)(2,1)}, u32[]{:S(2)}) copy-start(bf16[16,64,512]{2,1,0:T(8,128)(2,1)} %param.12) | copy-start | bytes 3145732
  19.7 15.7 %collective-permute-start.4 = (bf16[72,2560]{1,0:T(8,128)(2,1)S(1)}, bf16[72,2560]{1,0:T(8,128)(2,1)S(1)}, u32[]{:S(2)}, u32[]{:S(2)}) collective-permute-start(bf16[72,2560]{1,0:T(8,128)(2,1)S(1)} %collective-permute-done.refs_4_), channel_id=1, source_target_pairs={{0,4},{4,8},{8,12},{12,14},{14,10},{10,6},{6,2},{2,0},{1,5},{5,9},... | collective-permute-start | bytes 1105928 | tf_op jit(solution)/shard_map/ppermute | solution.py:372
  21.3 14.1 %collective-permute-start.5 = (bf16[72,2560]{1,0:T(8,128)(2,1)S(1)}, bf16[72,2560]{1,0:T(8,128)(2,1)S(1)}, u32[]{:S(2)}, u32[]{:S(2)}) collective-permute-start(bf16[72,2560]{1,0:T(8,128)(2,1)S(1)} %collective-permute-done.1.refs_5_), channel_id=1, source_target_pairs={{0,2},{4,0},{8,4},{12,8},{14,12},{10,14},{6,10},{2,6},{1,3},{5,1},... | collective-permute-start | bytes 1105928 | tf_op jit(solution)/shard_map/ppermute | solution.py:372
  21.7 12.2 %collective-permute-start.7 = (bf16[24,2688]{1,0:T(8,128)(2,1)}, bf16[24,2688]{1,0:T(8,128)(2,1)S(1)}, u32[]{:S(2)}, u32[]{:S(2)}) collective-permute-start(bf16[24,2688]{1,0:T(8,128)(2,1)} %get-tuple-element.68), channel_id=1, source_target_pairs={{0,8},{4,12},{8,14},{12,10},{14,6},{10,2},{6,0},{2,4},{1,9},{5,13}... | collective-permute-start | bytes 387080 | tf_op jit(solution)/shard_map/ppermute | solution.py:372
  24.3 11.1 %collective-permute-start.8 = (bf16[24,2688]{1,0:T(8,128)(2,1)}, bf16[24,2688]{1,0:T(8,128)(2,1)S(1)}, u32[]{:S(2)}, u32[]{:S(2)}) collective-permute-start(bf16[24,2688]{1,0:T(8,128)(2,1)} %get-tuple-element.70), channel_id=1, source_target_pairs={{0,6},{4,2},{8,0},{12,4},{14,8},{10,12},{6,14},{2,10},{1,7},{5,3},... | collective-permute-start | bytes 387080 | tf_op jit(solution)/shard_map/ppermute | solution.py:372
  28.7 1.3 %collective-permute-start.6 = (f32[64,216]{1,0:T(8,128)S(1)}, f32[64,216]{1,0:T(8,128)S(1)}, u32[]{:S(2)}, u32[]{:S(2)}) collective-permute-start(f32[64,216]{1,0:T(8,128)S(1)} %get-tuple-element.65.own_ref), channel_id=1, source_target_pairs={{0,1},{1,0},{2,3},{3,2},{4,5},{5,4},{6,7},{7,6},{8,9},{9,8},{10,11... | collective-permute-start | bytes 165896 | tf_op jit(solution)/shard_map/ppermute | solution.py:339
  35.4 22.1 %collective-permute-start.10 = (bf16[72,2560]{1,0:T(8,128)(2,1)S(1)}, bf16[72,2560]{1,0:T(8,128)(2,1)S(1)}, u32[]{:S(2)}, u32[]{:S(2)}) collective-permute-start(bf16[72,2560]{1,0:T(8,128)(2,1)S(1)} %collective-permute-done.4.refs_5_), channel_id=1, source_target_pairs={{0,4},{4,8},{8,12},{12,14},{14,10},{10,6},{6,2},{2,0},{1,5},{5,9},... | collective-permute-start | bytes 1105928 | tf_op jit(solution)/shard_map/ppermute | solution.py:372
  38.2 19.4 %collective-permute-start.11 = (bf16[72,2560]{1,0:T(8,128)(2,1)S(1)}, bf16[72,2560]{1,0:T(8,128)(2,1)S(1)}, u32[]{:S(2)}, u32[]{:S(2)}) collective-permute-start(bf16[72,2560]{1,0:T(8,128)(2,1)S(1)} %collective-permute-done.5.refs_6_), channel_id=1, source_target_pairs={{0,2},{4,0},{8,4},{12,8},{14,12},{10,14},{6,10},{2,6},{1,3},{5,1},... | collective-permute-start | bytes 1105928 | tf_op jit(solution)/shard_map/ppermute | solution.py:372
  41.1 4.0 %collective-permute-start.12 = (f32[64,264]{1,0:T(8,128)S(1)}, f32[64,264]{1,0:T(8,128)S(1)}, u32[]{:S(2)}, u32[]{:S(2)}) collective-permute-start(f32[64,264]{1,0:T(8,128)S(1)} %get-tuple-element.79.own_ref), channel_id=1, source_target_pairs={{0,1},{1,0},{2,3},{3,2},{4,5},{5,4},{6,7},{7,6},{8,9},{9,8},{10,11... | collective-permute-start | bytes 202760 | tf_op jit(solution)/shard_map/ppermute | solution.py:339
  41.1 16.4 %collective-permute-start.13 = (bf16[24,2688]{1,0:T(8,128)(2,1)S(1)}, bf16[24,2688]{1,0:T(8,128)(2,1)S(1)}, u32[]{:S(2)}, u32[]{:S(2)}) collective-permute-start(bf16[24,2688]{1,0:T(8,128)(2,1)S(1)} %copy-done.17), channel_id=1, source_target_pairs={{0,12},{4,14},{8,10},{12,6},{14,2},{10,0},{6,4},{2,8},{1,13},{5,15... | collective-permute-start | bytes 387080 | tf_op jit(solution)/shard_map/ppermute | solution.py:372
  43.2 14.3 %collective-permute-start.14 = (bf16[24,2688]{1,0:T(8,128)(2,1)S(1)}, bf16[24,2688]{1,0:T(8,128)(2,1)S(1)}, u32[]{:S(2)}, u32[]{:S(2)}) collective-permute-start(bf16[24,2688]{1,0:T(8,128)(2,1)S(1)} %copy-done.16), channel_id=1, source_target_pairs={{0,10},{4,6},{8,2},{12,0},{14,4},{10,8},{6,12},{2,14},{1,11},{5,7}... | collective-permute-start | bytes 387080 | tf_op jit(solution)/shard_map/ppermute | solution.py:372
  45.0 12.5 %collective-permute-start.9 = (bf16[24,2688]{1,0:T(8,128)(2,1)S(1)}, bf16[24,2688]{1,0:T(8,128)(2,1)S(1)}, u32[]{:S(2)}, u32[]{:S(2)}) collective-permute-start(bf16[24,2688]{1,0:T(8,128)(2,1)S(1)} %copy-done.15), channel_id=1, source_target_pairs={{0,14},{4,10},{8,6},{12,2},{14,0},{10,4},{6,8},{2,12},{1,15},{5,11... | collective-permute-start | bytes 387080 | tf_op jit(solution)/shard_map/ppermute | solution.py:372
  57.6 9.1 %collective-permute-start.16 = (bf16[40,2560]{1,0:T(8,128)(2,1)S(1)}, bf16[40,2560]{1,0:T(8,128)(2,1)S(1)}, u32[]{:S(2)}, u32[]{:S(2)}) collective-permute-start(bf16[40,2560]{1,0:T(8,128)(2,1)S(1)} %slice.15), channel_id=1, source_target_pairs={{0,2},{4,0},{8,4},{12,8},{14,12},{10,14},{6,10},{2,6},{1,3},{5,1},... | collective-permute-start | bytes 614408 | tf_op jit(solution)/shard_map/ppermute | solution.py:372
  58.6 7.4 %collective-permute-start.15 = (bf16[32,2560]{1,0:T(8,128)(2,1)S(1)}, bf16[32,2560]{1,0:T(8,128)(2,1)S(1)}, u32[]{:S(2)}, u32[]{:S(2)}) collective-permute-start(bf16[32,2560]{1,0:T(8,128)(2,1)S(1)} %slice.14), channel_id=1, source_target_pairs={{0,4},{4,8},{8,12},{12,14},{14,10},{10,6},{6,2},{2,0},{1,5},{5,9},... | collective-permute-start | bytes 491528 | tf_op jit(solution)/shard_map/ppermute | solution.py:372
  62.1 1.3 %collective-permute-start.17 = (f32[64,216]{1,0:T(8,128)S(1)}, f32[64,216]{1,0:T(8,128)S(1)}, u32[]{:S(2)}, u32[]{:S(2)}) collective-permute-start(f32[64,216]{1,0:T(8,128)S(1)} %get-tuple-element.90.own_ref), channel_id=1, source_target_pairs={{0,1},{1,0},{2,3},{3,2},{4,5},{5,4},{6,7},{7,6},{8,9},{9,8},{10,11... | collective-permute-start | bytes 165896 | tf_op jit(solution)/shard_map/ppermute | solution.py:339
  66.6 26.4 %all-to-all-start = ((bf16[8,24,2048]{2,1,0:T(8,128)(2,1)}), bf16[8,24,2048]{2,1,0:T(8,128)(2,1)S(1)}, u32[]{:S(2)}, u32[]{:S(2)}) async-start(bf16[8,24,2048]{2,1,0:T(8,128)(2,1)} %shard_map.98), calls=%async_computation | async-start | bytes 1572864 | tf_op jit(solution)/shard_map/all_to_all | solution.py:429
  75.7 17.4 %copy-start.13 = (f32[128]{0:T(128)S(1)}, f32[128]{0:T(128)}, u32[]{:S(2)}) copy-start(f32[128]{0:T(128)} %param.13) | copy-start | bytes 1540
  75.7 1.3 %collective-permute-start.18 = (f32[64,72]{1,0:T(8,128)S(1)}, f32[64,72]{1,0:T(8,128)S(1)}, u32[]{:S(2)}, u32[]{:S(2)}) collective-permute-start(f32[64,72]{1,0:T(8,128)S(1)} %get-tuple-element.95.own_ref), channel_id=1, source_target_pairs={{0,1},{1,0},{2,3},{3,2},{4,5},{5,4},{6,7},{7,6},{8,9},{9,8},{10,11... | collective-permute-start | bytes 55304 | tf_op jit(solution)/shard_map/ppermute | solution.py:339
  82.3 9.1 %collective-permute-start.19 = (f32[256,512]{1,0:T(8,128)S(1)}, f32[256,512]{1,0:T(8,128)S(1)}, u32[]{:S(2)}, u32[]{:S(2)}) collective-permute-start(f32[256,512]{1,0:T(8,128)S(1)} %get-tuple-element.100), channel_id=1, source_target_pairs={{0,1},{1,0},{2,3},{3,2},{4,5},{5,4},{6,7},{7,6},{8,9},{9,8},{10,11... | collective-permute-start | bytes 1572872 | tf_op jit(solution)/shard_map/ppermute | solution.py:339
  83.7 7.6 %collective-permute-start.20 = (bf16[1,24,1536]{2,1,0:T(8,128)(2,1)S(1)}, bf16[1,24,1536]{2,1,0:T(8,128)(2,1)S(1)}, u32[]{:S(2)}, u32[]{:S(2)}) collective-permute-start(bf16[1,24,1536]{2,1,0:T(8,128)(2,1)S(1)} %shard_map.100), channel_id=1, source_target_pairs={{0,14},{4,10},{8,6},{12,2},{14,0},{10,4},{6,8},{2,12},{1,15},{5,11... | collective-permute-start | bytes 221192 | tf_op jit(solution)/shard_map/ppermute | solution.py:372
  (16 other events, 130.5 us)

commit v8 on v7

--- a/solution.py
+++ b/solution.py
@@ -126,10 +126,11 @@
     return copies, size
 
 
-def base_kernel(side_ref, tokens_ref, place_ref, weight_hbm, own_ref, other_ref, column_ref, weight, sems):
+def base_kernel(side_ref, tokens_ref, place_ref, weight_hbm, own_ref, other_ref, chosen_ref, weight, sems):
     half = own_ref.shape[1]
     copies, size = fetch_rows(weight_hbm, weight, sems)
-    column_ref[...] = to_column(place_ref[...])
+    chosen = to_column(place_ref[...]) == lax.broadcasted_iota(jnp.int32, chosen_ref.shape, 1)
+    chosen_ref[...] = chosen.astype(jnp.float32).astype(jnp.bfloat16)
     total = None
     for k, copy in enumerate(copies):
         copy.wait()
@@ -151,14 +152,14 @@
         other_ref[...] = total[:, :half]
 
 
-def base_product(side, tokens, place, weight):
-    column = jax.ShapeDtypeStruct((tokens.shape[0], 1), jnp.int32)
+def base_product(side, tokens, place, places, weight):
+    chosen = jax.ShapeDtypeStruct((tokens.shape[0], places), jnp.bfloat16)
     half = jax.ShapeDtypeStruct((tokens.shape[0], weight.shape[1] // 2), jnp.float32)
     return pl.pallas_call(
         base_kernel,
         in_specs=[scalars(), whole(), whole(), pl.BlockSpec(memory_space=pltpu.HBM)],
         out_specs=(whole(),) * 3,
-        out_shape=(half, half, column),
+        out_shape=(half, half, chosen),
         scratch_shapes=[pltpu.VMEM(weight.shape, weight.dtype), pltpu.SemaphoreType.DMA((5,))],
         compiler_params=params(),
         cost_estimate=LITTLE,
@@ -284,9 +285,9 @@
 
 
 def finish_kernel(
-    head, busy_ref, far_ref, own_ref, other_ref, back_ref, last_ref, place_ref, scale_ref, cos_ref, sin_ref, out_ref
+    head, busy_ref, far_ref, base_ref, back_ref, last_ref, chosen_ref, scale_ref, cos_ref, sin_ref, out_ref
 ):
-    count, width = own_ref.shape
+    width = base_ref.shape[1]
     owners, share, _ = back_ref.shape
     pieces = [back_ref[o, :, HOT_PARTS * width :].astype(jnp.float32) for o in range(owners)]
     from_far = busy_ref[0] == far_ref[0]
@@ -295,10 +296,7 @@
         near = back_ref[busy_ref[0], :, columns].astype(jnp.float32)
         pieces.append(jnp.where(from_far, last_ref[0, :, columns].astype(jnp.float32), near))
     back = jnp.concatenate(pieces, axis=0).astype(jnp.bfloat16)
-    chosen = place_ref[...] == lax.broadcasted_iota(jnp.int32, (count, back.shape[0]), 1)
-    keys = (own_ref[...] + other_ref[...]) + jnp.dot(
-        chosen.astype(jnp.float32).astype(jnp.bfloat16), back, preferred_element_type=jnp.float32
-    )
+    keys = base_ref[...] + jnp.dot(chosen_ref[...], back, preferred_element_type=jnp.float32)
     cosine = cos_ref[...]
     sine = sin_ref[...]
     for h in range(width // head):
@@ -312,14 +310,14 @@
         out_ref[:, h * head : (h + 1) * head] = (normed * cosine + turned * sine).astype(jnp.bfloat16)
 
 
-def finish(busy, far, own, other, back, last, place, scale, cosine, sine):
+def finish(busy, far, base, back, last, chosen, scale, cosine, sine):
     return pl.pallas_call(
         functools.partial(finish_kernel, scale.shape[0]),
-        in_specs=[scalars()] * 2 + [whole()] * 8,
+        in_specs=[scalars()] * 2 + [whole()] * 7,
         out_specs=whole(),
-        out_shape=jax.ShapeDtypeStruct(own.shape, jnp.bfloat16),
+        out_shape=jax.ShapeDtypeStruct(base.shape, jnp.bfloat16),
         compiler_params=params(),
-    )(busy, far, own, other, back, last, place, scale.reshape(1, -1), cosine, sine)
+    )(busy, far, base, back, last, chosen, scale.reshape(1, -1), cosine, sine)
 
 
 def after(value, *earlier):
@@ -392,6 +390,7 @@
     got = {0: cold[0]}
     for d in waves[1]:
         got[d] = along(cold[d], d)
+    first_hot = owners * share
     cut = hot_count // 2 // 16 * 16 if hot_count >= 32 else hot_count // 2
 
     def hot_units(first, blocks):
@@ -425,7 +424,7 @@
         delta = up(order, units + cold_units(chosen), *product(blocks, rows), up_table, delta)
         todo = [delta] + [got[d] for d in waves.get(step + 1, [])]
         group = following
-    *group, delta = lax.optimization_barrier((*group, delta))
+    delta = after(delta, *group)
     back = lax.all_to_all(delta, "dp", split_axis=0, concat_axis=0, tiled=True)
     last = product([(HOT, half_way), (REST, half_way)], list(group))
     far_delta = jax.ShapeDtypeStruct((1, share, HOT_PARTS * features), jnp.bfloat16)
@@ -434,18 +433,17 @@
     )
     tokens = after(tokens, far_delta)
     far_delta = along(far_delta, half_way)
-    base_own, base_give, place = base_product(
-        side.reshape(1).astype(jnp.int32), tokens, place, base_key_matrix
+    base_own, base_give, chosen = base_product(
+        side.reshape(1).astype(jnp.int32), tokens, place, first_hot + hot_count, base_key_matrix
     )
     cosine, sine = rope_tables(key_norm_scale.shape[0], cached_token_length)
     return finish(
         busy.reshape(1),
         order[owners - 1 : owners],
-        base_own,
-        swap(base_give),
+        base_own + swap(base_give),
         back,
         far_delta,
-        place,
+        chosen,
         key_norm_scale,
         cosine,
         sine,

time: 96 us -> 95.9 us (level)
  no operation moved by 1% of the time
where the time goes in v8:
time: 95.9 us; the launch traced here: 95.5 us
  starting transfers between devices  30.7 us (32%)
  waiting for transfers between devices  26.6 us (28%)
  Pallas kernels  21.9 us (23%)
  local copies, waits for them, and re-layouts  15.3 us (16%)
    ppermute x16, starting transfers between devices, along(): lax.ppermute(rows, 'dp', [(ring[i], ring[(i + distance) % owners]) for i...  26.1 us
    ppermute x16, waiting for transfers between devices, along(): lax.ppermute(rows, 'dp', [(ring[i], ring[(i + distance) % owners]) for i...  21.9 us
    unnamed x36, local copies, waits for them, and re-layouts  13.9 us
    pallas_call x4, Pallas kernels, down(): pl.pallas_call(functools.partial(down_kernel, rank, blocks, len(guides)),...  7.48 us
    pallas_call x4, Pallas kernels, up(): pl.pallas_call(functools.partial(up_kernel, units, len(given)), in_specs=...  5.7 us
    all_to_all x1, starting transfers between devices, on_device(): back = lax.all_to_all(delta, 'dp', split_axis=0, concat_axis=0, tiled=True)  4.15 us
    pallas_call x1, Pallas kernels, route(): pl.pallas_call(functools.partial(route_kernel, stored, owners, share), ou...  3.57 us
    ppermute x5, waiting for transfers between devices, swap(): return lax.ppermute(x, 'tensor', [(0, 1), (1, 0)])  2.98 us
  transfers between devices with their start and end apart: 22, of which 11 were waited for; matrix products, arithmetic and copies ran while one was open for 2% of the time, Pallas kernels for 17%

profile of v8, /device:TPU:0, one launch (start us, length us, event | category | flops | bytes accessed | tf_op | source)
XLA Modules:
  0.0 95.5 jit_solution(5974181000444813274)
XLA Ops:
  0.0 3.6 %shard_map.91 = (bf16[72,2560]{1,0:T(8,128)(2,1)}, bf16[24,2688]{1,0:T(8,128)(2,1)}, bf16[24,2688]{1,0:T(8,128)(2,1)}, bf16[24,2688]{1,0:T(8,128)(2,1)}, bf16[24...) custom-call(s32[1]{0:T(128)} %bitcast.me_ref, ...), custom_call_target="tpu_custom_call" | custom-call | tf_op jit(solution)/shard_map/pallas_call | solution.py:103
  3.6 3.1 %collective-permute-start = (bf16[72,2560]{1,0:T(8,128)(2,1)}, bf16[72,2560]{1,0:T(8,128)(2,1)S(1)}, u32[]{:S(2)}, u32[]{:S(2)}) collective-permute-start(bf16[72,2560]{1,0:T(8,128)(2,1)} %get-tuple-element.54.refs_3_), channel_id=1, source_target_pairs={{0,4},{4,8},{8,12},{12,14},{14,10},{10,6},{6,2},{2,0},{1,5},{5,9},... | collective-permute-start | bytes 1105928 | tf_op jit(solution)/shard_map/ppermute | solution.py:370
  6.7 2.0 %collective-permute-start.2 = (bf16[24,2688]{1,0:T(8,128)(2,1)}, bf16[24,2688]{1,0:T(8,128)(2,1)S(1)}, u32[]{:S(2)}, u32[]{:S(2)}) collective-permute-start(bf16[24,2688]{1,0:T(8,128)(2,1)} %get-tuple-element.55), channel_id=1, source_target_pairs={{0,4},{4,8},{8,12},{12,14},{14,10},{10,6},{6,2},{2,0},{1,5},{5,9},... | collective-permute-start | bytes 387080 | tf_op jit(solution)/shard_map/ppermute | solution.py:370
  8.7 2.5 %copy-done.5 = bf16[16,64,2560]{2,1,0:T(8,128)(2,1)S(1)} copy-done((bf16[16,64,2560]{2,1,0:T(8,128)(2,1)S(1)}, bf16[16,64,2560]{2,1,0:T(8,128)(2,1)}, u32[]{:S(2)}) %copy-start.5) | copy-done | bytes 5242904
  11.6 2.3 %copy-done = bf16[1024,2560]{1,0:T(8,128)(2,1)} copy-done((bf16[1024,2560]{1,0:T(8,128)(2,1)}, bf16[1024,2560]{1,0:T(8,128)(2,1)S(1)}, u32[]{:S(2)}) %copy-start) | copy-done | bytes 5242904
  13.9 4.2 %collective-permute-done.2.refs_1_ = bf16[24,2688]{1,0:T(8,128)(2,1)S(1)} collective-permute-done((bf16[24,2688]{1,0:T(8,128)(2,1)}, bf16[24,2688]{1,0:T(8,128)(2,1)S(1)}, u32[]{:S(2)}, u32[]{:S(2)}) %collective-permute-start.2) | collective-permute-done | bytes 129056 | tf_op jit(solution)/shard_map/ppermute | solution.py:370
  21.7 2.6 %collective-permute-start.7 = (bf16[24,2688]{1,0:T(8,128)(2,1)}, bf16[24,2688]{1,0:T(8,128)(2,1)S(1)}, u32[]{:S(2)}, u32[]{:S(2)}) collective-permute-start(bf16[24,2688]{1,0:T(8,128)(2,1)} %get-tuple-element.66), channel_id=1, source_target_pairs={{0,8},{4,12},{8,14},{12,10},{14,6},{10,2},{6,0},{2,4},{1,9},{5,13}... | collective-permute-start | bytes 387080 | tf_op jit(solution)/shard_map/ppermute | solution.py:370
  24.7 2.5 %copy-done.1 = bf16[1024,2560]{1,0:T(8,128)(2,1)S(1)} copy-done((bf16[1024,2560]{1,0:T(8,128)(2,1)S(1)}, bf16[1024,2560]{1,0:T(8,128)(2,1)}, u32[]{:S(2)}) %copy-start.1) | copy-done | bytes 5242904
  30.1 1.7 %shard_map.94.refs_0_ = bf16[8,24,2048]{2,1,0:T(8,128)(2,1)} custom-call(s32[16]{0:T(128)S(1)} %get-tuple-element.99.to_ref, f32[64,216]{1,0:T(8,128)S(1)} %get-tuple-element.63.own_ref, f32[64,216]{1,0:T(8,128)S(1)} %collective-permute-done.6.other_ref, f32[1,216]{1,0:T(1,128)S(1)} %get-tuple-element.64.local_ref, bf16[1024,512]{1,0:T(8,128)(2,1)S(1)} %bitcast.11), custom_call_target="tpu_custom_call" | custom-call | flops 1 | bytes 1 | tf_op jit(solution)/shard_map/pallas_call | solution.py:272
  31.8 2.1 %collective-permute-done.7.refs_2_ = bf16[24,2688]{1,0:T(8,128)(2,1)S(1)} collective-permute-done((bf16[24,2688]{1,0:T(8,128)(2,1)}, bf16[24,2688]{1,0:T(8,128)(2,1)S(1)}, u32[]{:S(2)}, u32[]{:S(2)}) %collective-permute-start.7) | collective-permute-done | bytes 129056 | tf_op jit(solution)/shard_map/ppermute | solution.py:370
  35.4 2.8 %collective-permute-start.10 = (bf16[72,2560]{1,0:T(8,128)(2,1)S(1)}, bf16[72,2560]{1,0:T(8,128)(2,1)S(1)}, u32[]{:S(2)}, u32[]{:S(2)}) collective-permute-start(bf16[72,2560]{1,0:T(8,128)(2,1)S(1)} %collective-permute-done.4.refs_5_), channel_id=1, source_target_pairs={{0,4},{4,8},{8,12},{12,14},{14,10},{10,6},{6,2},{2,0},{1,5},{5,9},... | collective-permute-start | bytes 1105928 | tf_op jit(solution)/shard_map/ppermute | solution.py:370
  38.2 2.9 %shard_map.95 = (f32[64,264]{1,0:T(8,128)S(1)}, f32[1,264]{1,0:T(1,128)S(1)}) custom-call(s32[1]{0:T(128)} %bitcast.me_ref, bf16[24,2688]{1,0:T(8,128)(2,1)S(1)} %copy-done.8, bf16[24,2688]{1,0:T(8,128)(2,1)S(1)} %collective-permute-done.2.refs_1_, bf16[24,2688]{1,0:T(8,128)(2,1)S(1)} %collective-permute-done.7.refs_2_, ...), custom_call_target="tpu_custom_call" | custom-call | flops 1 | bytes 1 | tf_op jit(solution)/shard_map/pallas_call | solution.py:224
  41.1 2.0 %collective-permute-start.13 = (bf16[24,2688]{1,0:T(8,128)(2,1)S(1)}, bf16[24,2688]{1,0:T(8,128)(2,1)S(1)}, u32[]{:S(2)}, u32[]{:S(2)}) collective-permute-start(bf16[24,2688]{1,0:T(8,128)(2,1)S(1)} %copy-done.17), channel_id=1, source_target_pairs={{0,12},{4,14},{8,10},{12,6},{14,2},{10,0},{6,4},{2,8},{1,13},{5,15... | collective-permute-start | bytes 387080 | tf_op jit(solution)/shard_map/ppermute | solution.py:370
  43.2 1.8 %collective-permute-start.14 = (bf16[24,2688]{1,0:T(8,128)(2,1)S(1)}, bf16[24,2688]{1,0:T(8,128)(2,1)S(1)}, u32[]{:S(2)}, u32[]{:S(2)}) collective-permute-start(bf16[24,2688]{1,0:T(8,128)(2,1)S(1)} %copy-done.16), channel_id=1, source_target_pairs={{0,10},{4,6},{8,2},{12,0},{14,4},{10,8},{6,12},{2,14},{1,11},{5,7}... | collective-permute-start | bytes 387080 | tf_op jit(solution)/shard_map/ppermute | solution.py:370
  46.6 1.8 %shard_map.96.refs_0_ = bf16[8,24,2048]{2,1,0:T(8,128)(2,1)} custom-call(s32[16]{0:T(128)S(1)} %get-tuple-element.99.to_ref, f32[64,264]{1,0:T(8,128)S(1)} %get-tuple-element.77.own_ref, f32[64,264]{1,0:T(8,128)S(1)} %collective-permute-done.12.other_ref, f32[1,264]{1,0:T(1,128)S(1)} %get-tuple-element.78.local_ref, ...), custom_call_target="tpu_custom_call", output_to_operand_aliasing={{}: (5, {})} | custom-call | flops 1 | bytes 1 | tf_op jit(solution)/shard_map/pallas_call | solution.py:272
  48.4 9.1 %collective-permute-done.13.refs_0_ = bf16[24,2688]{1,0:T(8,128)(2,1)S(1)} collective-permute-done((bf16[24,2688]{1,0:T(8,128)(2,1)S(1)}, bf16[24,2688]{1,0:T(8,128)(2,1)S(1)}, u32[]{:S(2)}, u32[]{:S(2)}) %collective-permute-start.13) | collective-permute-done | bytes 129056 | tf_op jit(solution)/shard_map/ppermute | solution.py:370
  58.6 2.0 %collective-permute-start.15 = (bf16[32,2560]{1,0:T(8,128)(2,1)S(1)}, bf16[32,2560]{1,0:T(8,128)(2,1)S(1)}, u32[]{:S(2)}, u32[]{:S(2)}) collective-permute-start(bf16[32,2560]{1,0:T(8,128)(2,1)S(1)} %slice.14), channel_id=1, source_target_pairs={{0,4},{4,8},{8,12},{12,14},{14,10},{10,6},{6,2},{2,0},{1,5},{5,9},... | collective-permute-start | bytes 491528 | tf_op jit(solution)/shard_map/ppermute | solution.py:370
  66.6 4.1 %all-to-all-start = ((bf16[8,24,2048]{2,1,0:T(8,128)(2,1)}), bf16[8,24,2048]{2,1,0:T(8,128)(2,1)S(1)}, u32[]{:S(2)}, u32[]{:S(2)}) async-start(bf16[8,24,2048]{2,1,0:T(8,128)(2,1)} %shard_map.101), calls=%async_computation | async-start | bytes 1572864 | tf_op jit(solution)/shard_map/all_to_all | solution.py:428
  70.8 2.5 %copy-done.3 = bf16[1024,2560]{1,0:T(8,128)(2,1)S(1)} copy-done((bf16[1024,2560]{1,0:T(8,128)(2,1)S(1)}, bf16[1024,2560]{1,0:T(8,128)(2,1)}, u32[]{:S(2)}) %copy-start.3) | copy-done | bytes 5242904
  77.5 2.5 %copy-done.6 = bf16[2560,1024]{1,0:T(8,128)(2,1)S(1)} copy-done((bf16[2560,1024]{1,0:T(8,128)(2,1)S(1)}, bf16[2560,1024]{1,0:T(8,128)(2,1)}, u32[]{:S(2)}) %copy-start.6) | copy-done | bytes 5242904
  79.9 2.3 %shard_map.99 = (f32[256,512]{1,0:T(8,128)S(1)}, f32[256,512]{1,0:T(8,128)S(1)}, bf16[256,264]{1,0:T(8,128)(2,1)S(1)}) custom-call(s32[1]{0:T(128)} %bitcast.5.side_ref, bf16[256,2560]{1,0:T(8,128)(2,1)S(1)} %copy-done.7, s32[1,256]{1,0:T(1,128)S(1)} %copy-done.12, bf16[2560,1024]{1,0:T(8,128)(2,1)S(1)} %copy-done.6), custom_call_target="tpu_custom_call" | custom-call | flops 1 | bytes 1 | tf_op jit(solution)/shard_map/pallas_call | solution.py:158
  83.7 4.8 %collective-permute-start.20 = (bf16[1,24,1536]{2,1,0:T(8,128)(2,1)S(1)}, bf16[1,24,1536]{2,1,0:T(8,128)(2,1)S(1)}, u32[]{:S(2)}, u32[]{:S(2)}) collective-permute-start(bf16[1,24,1536]{2,1,0:T(8,128)(2,1)S(1)} %shard_map.98), channel_id=1, source_target_pairs={{0,14},{4,10},{8,6},{12,2},{14,0},{10,4},{6,8},{2,12},{1,15},{5,11... | collective-permute-start | bytes 221192 | tf_op jit(solution)/shard_map/ppermute | solution.py:370
  88.8 2.6 %collective-permute-done.20.last_ref = bf16[1,24,1536]{2,1,0:T(8,128)(2,1)S(1)} collective-permute-done((bf16[1,24,1536]{2,1,0:T(8,128)(2,1)S(1)}, bf16[1,24,1536]{2,1,0:T(8,128)(2,1)S(1)}, u32[]{:S(2)}, u32[]{:S(2)}) %collective-permute-start.20) | collective-permute-done | bytes 73760 | tf_op jit(solution)/shard_map/ppermute | solution.py:370
  93.1 2.5 %shard_map.102 = bf16[256,512]{1,0:T(8,128)(2,1)} custom-call(s32[1]{0:T(128)} %bitcast.3.busy_ref, s32[1]{0:T(128)} %bitcast.4.far_ref, f32[256,512]{1,0:T(8,128)S(1)} %add.8.base_ref, bf16[8,24,2048]{2,1,0:T(8,128)(2,1)S(1)} %all-to-all-done.back_ref, bf16[1,24,1536]{2,1,0:T(8,128)(2,1)S(1)} %collective-permute-done.20.last_ref, ...), custom_call_target="tpu_custom_call" | custom-call | tf_op jit(solution)/shard_map/pallas_call | solution.py:314
  (77 shorter events, 24.8 us)
Async XLA Ops:
  3.6 16.1 %collective-permute-start = (bf16[72,2560]{1,0:T(8,128)(2,1)}, bf16[72,2560]{1,0:T(8,128)(2,1)S(1)}, u32[]{:S(2)}, u32[]{:S(2)}) collective-permute-start(bf16[72,2560]{1,0:T(8,128)(2,1)} %get-tuple-element.54.refs_3_), channel_id=1, source_target_pairs={{0,4},{4,8},{8,12},{12,14},{14,10},{10,6},{6,2},{2,0},{1,5},{5,9},... | collective-permute-start | bytes 1105928 | tf_op jit(solution)/shard_map/ppermute | solution.py:370
  6.7 13.0 %collective-permute-start.1 = (bf16[72,2560]{1,0:T(8,128)(2,1)}, bf16[72,2560]{1,0:T(8,128)(2,1)S(1)}, u32[]{:S(2)}, u32[]{:S(2)}) collective-permute-start(bf16[72,2560]{1,0:T(8,128)(2,1)} %get-tuple-element.54.refs_3_), channel_id=1, source_target_pairs={{0,2},{4,0},{8,4},{12,8},{14,12},{10,14},{6,10},{2,6},{1,3},{5,1},... | collective-permute-start | bytes 1105928 | tf_op jit(solution)/shard_map/ppermute | solution.py:370
  6.7 11.5 %collective-permute-start.2 = (bf16[24,2688]{1,0:T(8,128)(2,1)}, bf16[24,2688]{1,0:T(8,128)(2,1)S(1)}, u32[]{:S(2)}, u32[]{:S(2)}) collective-permute-start(bf16[24,2688]{1,0:T(8,128)(2,1)} %get-tuple-element.55), channel_id=1, source_target_pairs={{0,4},{4,8},{8,12},{12,14},{14,10},{10,6},{6,2},{2,0},{1,5},{5,9},... | collective-permute-start | bytes 387080 | tf_op jit(solution)/shard_map/ppermute | solution.py:370
  8.7 11.0 %collective-permute-start.3 = (bf16[24,2688]{1,0:T(8,128)(2,1)}, bf16[24,2688]{1,0:T(8,128)(2,1)S(1)}, u32[]{:S(2)}, u32[]{:S(2)}) collective-permute-start(bf16[24,2688]{1,0:T(8,128)(2,1)} %get-tuple-element.56), channel_id=1, source_target_pairs={{0,2},{4,0},{8,4},{12,8},{14,12},{10,14},{6,10},{2,6},{1,3},{5,1},... | collective-permute-start | bytes 387080 | tf_op jit(solution)/shard_map/ppermute | solution.py:370
  11.2 18.9 %copy-start.4 = (bf16[16,64,512]{2,1,0:T(8,128)(2,1)S(1)}, bf16[16,64,512]{2,1,0:T(8,128)(2,1)}, u32[]{:S(2)}) copy-start(bf16[16,64,512]{2,1,0:T(8,128)(2,1)} %param.12) | copy-start | bytes 3145732
  19.7 15.7 %collective-permute-start.4 = (bf16[72,2560]{1,0:T(8,128)(2,1)S(1)}, bf16[72,2560]{1,0:T(8,128)(2,1)S(1)}, u32[]{:S(2)}, u32[]{:S(2)}) collective-permute-start(bf16[72,2560]{1,0:T(8,128)(2,1)S(1)} %collective-permute-done.refs_4_), channel_id=1, source_target_pairs={{0,4},{4,8},{8,12},{12,14},{14,10},{10,6},{6,2},{2,0},{1,5},{5,9},... | collective-permute-start | bytes 1105928 | tf_op jit(solution)/shard_map/ppermute | solution.py:370
  21.3 14.1 %collective-permute-start.5 = (bf16[72,2560]{1,0:T(8,128)(2,1)S(1)}, bf16[72,2560]{1,0:T(8,128)(2,1)S(1)}, u32[]{:S(2)}, u32[]{:S(2)}) collective-permute-start(bf16[72,2560]{1,0:T(8,128)(2,1)S(1)} %collective-permute-done.1.refs_5_), channel_id=1, source_target_pairs={{0,2},{4,0},{8,4},{12,8},{14,12},{10,14},{6,10},{2,6},{1,3},{5,1},... | collective-permute-start | bytes 1105928 | tf_op jit(solution)/shard_map/ppermute | solution.py:370
  21.7 12.2 %collective-permute-start.7 = (bf16[24,2688]{1,0:T(8,128)(2,1)}, bf16[24,2688]{1,0:T(8,128)(2,1)S(1)}, u32[]{:S(2)}, u32[]{:S(2)}) collective-permute-start(bf16[24,2688]{1,0:T(8,128)(2,1)} %get-tuple-element.66), channel_id=1, source_target_pairs={{0,8},{4,12},{8,14},{12,10},{14,6},{10,2},{6,0},{2,4},{1,9},{5,13}... | collective-permute-start | bytes 387080 | tf_op jit(solution)/shard_map/ppermute | solution.py:370
  24.3 11.1 %collective-permute-start.8 = (bf16[24,2688]{1,0:T(8,128)(2,1)}, bf16[24,2688]{1,0:T(8,128)(2,1)S(1)}, u32[]{:S(2)}, u32[]{:S(2)}) collective-permute-start(bf16[24,2688]{1,0:T(8,128)(2,1)} %get-tuple-element.68), channel_id=1, source_target_pairs={{0,6},{4,2},{8,0},{12,4},{14,8},{10,12},{6,14},{2,10},{1,7},{5,3},... | collective-permute-start | bytes 387080 | tf_op jit(solution)/shard_map/ppermute | solution.py:370
  28.7 1.3 %collective-permute-start.6 = (f32[64,216]{1,0:T(8,128)S(1)}, f32[64,216]{1,0:T(8,128)S(1)}, u32[]{:S(2)}, u32[]{:S(2)}) collective-permute-start(f32[64,216]{1,0:T(8,128)S(1)} %get-tuple-element.63.own_ref), channel_id=1, source_target_pairs={{0,1},{1,0},{2,3},{3,2},{4,5},{5,4},{6,7},{7,6},{8,9},{9,8},{10,11... | collective-permute-start | bytes 165896 | tf_op jit(solution)/shard_map/ppermute | solution.py:337
  35.4 22.1 %collective-permute-start.10 = (bf16[72,2560]{1,0:T(8,128)(2,1)S(1)}, bf16[72,2560]{1,0:T(8,128)(2,1)S(1)}, u32[]{:S(2)}, u32[]{:S(2)}) collective-permute-start(bf16[72,2560]{1,0:T(8,128)(2,1)S(1)} %collective-permute-done.4.refs_5_), channel_id=1, source_target_pairs={{0,4},{4,8},{8,12},{12,14},{14,10},{10,6},{6,2},{2,0},{1,5},{5,9},... | collective-permute-start | bytes 1105928 | tf_op jit(solution)/shard_map/ppermute | solution.py:370
  38.2 19.4 %collective-permute-start.11 = (bf16[72,2560]{1,0:T(8,128)(2,1)S(1)}, bf16[72,2560]{1,0:T(8,128)(2,1)S(1)}, u32[]{:S(2)}, u32[]{:S(2)}) collective-permute-start(bf16[72,2560]{1,0:T(8,128)(2,1)S(1)} %collective-permute-done.5.refs_6_), channel_id=1, source_target_pairs={{0,2},{4,0},{8,4},{12,8},{14,12},{10,14},{6,10},{2,6},{1,3},{5,1},... | collective-permute-start | bytes 1105928 | tf_op jit(solution)/shard_map/ppermute | solution.py:370
  41.1 4.0 %collective-permute-start.12 = (f32[64,264]{1,0:T(8,128)S(1)}, f32[64,264]{1,0:T(8,128)S(1)}, u32[]{:S(2)}, u32[]{:S(2)}) collective-permute-start(f32[64,264]{1,0:T(8,128)S(1)} %get-tuple-element.77.own_ref), channel_id=1, source_target_pairs={{0,1},{1,0},{2,3},{3,2},{4,5},{5,4},{6,7},{7,6},{8,9},{9,8},{10,11... | collective-permute-start | bytes 202760 | tf_op jit(solution)/shard_map/ppermute | solution.py:337
  41.1 16.4 %collective-permute-start.13 = (bf16[24,2688]{1,0:T(8,128)(2,1)S(1)}, bf16[24,2688]{1,0:T(8,128)(2,1)S(1)}, u32[]{:S(2)}, u32[]{:S(2)}) collective-permute-start(bf16[24,2688]{1,0:T(8,128)(2,1)S(1)} %copy-done.17), channel_id=1, source_target_pairs={{0,12},{4,14},{8,10},{12,6},{14,2},{10,0},{6,4},{2,8},{1,13},{5,15... | collective-permute-start | bytes 387080 | tf_op jit(solution)/shard_map/ppermute | solution.py:370
  43.2 14.3 %collective-permute-start.14 = (bf16[24,2688]{1,0:T(8,128)(2,1)S(1)}, bf16[24,2688]{1,0:T(8,128)(2,1)S(1)}, u32[]{:S(2)}, u32[]{:S(2)}) collective-permute-start(bf16[24,2688]{1,0:T(8,128)(2,1)S(1)} %copy-done.16), channel_id=1, source_target_pairs={{0,10},{4,6},{8,2},{12,0},{14,4},{10,8},{6,12},{2,14},{1,11},{5,7}... | collective-permute-start | bytes 387080 | tf_op jit(solution)/shard_map/ppermute | solution.py:370
  45.0 12.5 %collective-permute-start.9 = (bf16[24,2688]{1,0:T(8,128)(2,1)S(1)}, bf16[24,2688]{1,0:T(8,128)(2,1)S(1)}, u32[]{:S(2)}, u32[]{:S(2)}) collective-permute-start(bf16[24,2688]{1,0:T(8,128)(2,1)S(1)} %copy-done.15), channel_id=1, source_target_pairs={{0,14},{4,10},{8,6},{12,2},{14,0},{10,4},{6,8},{2,12},{1,15},{5,11... | collective-permute-start | bytes 387080 | tf_op jit(solution)/shard_map/ppermute | solution.py:370
  57.6 9.1 %collective-permute-start.16 = (bf16[40,2560]{1,0:T(8,128)(2,1)S(1)}, bf16[40,2560]{1,0:T(8,128)(2,1)S(1)}, u32[]{:S(2)}, u32[]{:S(2)}) collective-permute-start(bf16[40,2560]{1,0:T(8,128)(2,1)S(1)} %slice.15), channel_id=1, source_target_pairs={{0,2},{4,0},{8,4},{12,8},{14,12},{10,14},{6,10},{2,6},{1,3},{5,1},... | collective-permute-start | bytes 614408 | tf_op jit(solution)/shard_map/ppermute | solution.py:370
  58.6 7.4 %collective-permute-start.15 = (bf16[32,2560]{1,0:T(8,128)(2,1)S(1)}, bf16[32,2560]{1,0:T(8,128)(2,1)S(1)}, u32[]{:S(2)}, u32[]{:S(2)}) collective-permute-start(bf16[32,2560]{1,0:T(8,128)(2,1)S(1)} %slice.14), channel_id=1, source_target_pairs={{0,4},{4,8},{8,12},{12,14},{14,10},{10,6},{6,2},{2,0},{1,5},{5,9},... | collective-permute-start | bytes 491528 | tf_op jit(solution)/shard_map/ppermute | solution.py:370
  62.1 1.3 %collective-permute-start.19 = (f32[64,216]{1,0:T(8,128)S(1)}, f32[64,216]{1,0:T(8,128)S(1)}, u32[]{:S(2)}, u32[]{:S(2)}) collective-permute-start(f32[64,216]{1,0:T(8,128)S(1)} %get-tuple-element.95.own_ref), channel_id=1, source_target_pairs={{0,1},{1,0},{2,3},{3,2},{4,5},{5,4},{6,7},{7,6},{8,9},{9,8},{10,11... | collective-permute-start | bytes 165896 | tf_op jit(solution)/shard_map/ppermute | solution.py:337
  66.6 26.4 %all-to-all-start = ((bf16[8,24,2048]{2,1,0:T(8,128)(2,1)}), bf16[8,24,2048]{2,1,0:T(8,128)(2,1)S(1)}, u32[]{:S(2)}, u32[]{:S(2)}) async-start(bf16[8,24,2048]{2,1,0:T(8,128)(2,1)} %shard_map.101), calls=%async_computation | async-start | bytes 1572864 | tf_op jit(solution)/shard_map/all_to_all | solution.py:428
  75.7 17.4 %copy-start.13 = (f32[128]{0:T(128)S(1)}, f32[128]{0:T(128)}, u32[]{:S(2)}) copy-start(f32[128]{0:T(128)} %param.13) | copy-start | bytes 1540
  75.7 1.3 %collective-permute-start.17 = (f32[64,72]{1,0:T(8,128)S(1)}, f32[64,72]{1,0:T(8,128)S(1)}, u32[]{:S(2)}, u32[]{:S(2)}) collective-permute-start(f32[64,72]{1,0:T(8,128)S(1)} %get-tuple-element.86.own_ref), channel_id=1, source_target_pairs={{0,1},{1,0},{2,3},{3,2},{4,5},{5,4},{6,7},{7,6},{8,9},{9,8},{10,11... | collective-permute-start | bytes 55304 | tf_op jit(solution)/shard_map/ppermute | solution.py:337
  82.3 6.4 %collective-permute-start.18 = (f32[256,512]{1,0:T(8,128)S(1)}, f32[256,512]{1,0:T(8,128)S(1)}, u32[]{:S(2)}, u32[]{:S(2)}) collective-permute-start(f32[256,512]{1,0:T(8,128)S(1)} %get-tuple-element.91), channel_id=1, source_target_pairs={{0,1},{1,0},{2,3},{3,2},{4,5},{5,4},{6,7},{7,6},{8,9},{9,8},{10,11... | collective-permute-start | bytes 1572872 | tf_op jit(solution)/shard_map/ppermute | solution.py:337
  83.7 7.6 %collective-permute-start.20 = (bf16[1,24,1536]{2,1,0:T(8,128)(2,1)S(1)}, bf16[1,24,1536]{2,1,0:T(8,128)(2,1)S(1)}, u32[]{:S(2)}, u32[]{:S(2)}) collective-permute-start(bf16[1,24,1536]{2,1,0:T(8,128)(2,1)S(1)} %shard_map.98), channel_id=1, source_target_pairs={{0,14},{4,10},{8,6},{12,2},{14,0},{10,4},{6,8},{2,12},{1,15},{5,11... | collective-permute-start | bytes 221192 | tf_op jit(solution)/shard_map/ppermute | solution.py:370
  (16 other events, 130.5 us)
